TPU v7x, 128 devices: a whole 4x4x4 slice. The times are simulated.
128 devices in a mesh: row: 8 (over y, core), col: 16 (over z, x).
Axes of the slice: x: 4, y: 4, z: 4, core: 2. Of those that a mesh axis runs over, the one named last changes fastest.
Arguments:
- amplitudes: bfloat16 [16384, 32768], P('col', 'row'), may hold values from -6 to 6
- amp_mask: int32 [128, 256], P('col', 'row'), may hold values from 0 to 1, as said below
- integrals: bfloat16 [2, 4096, 10240], P(None, 'col', 'row'), may hold values from -0.09375 to 0.09375
- int_mask: int32 [2, 32, 80], P(None, 'col', 'row'), may hold values 0 or 1
- steps: int32 [2], replicated, may hold values from 0 to 7, as said below
Outputs:
- ladder: float32 [16384, 10240], P('col', 'row')
Inputs may be any that keep to these rules, and one draw needn't show every extreme that they name: `steps`: distinct grid rows. `amp_mask`: split the 32 cd tile columns of one row device's panel into 16 aligned groups of 2; for every column device's 8 pair tile rows, exactly 1 tile columns of every group hold a nonzero tile; on some column devices every pair tile row of those columns is nonzero.
All inputs are finite; a program needn't handle non-finite values. No bound on the sum of `int_mask` on one device may be relied on, other than what follows from the above.
Results may differ from a plain program's by a relative error of at most 0.0003.
Values may be sent and summed in bfloat16 or wider, within the bound.
No kernel may reach another device: no remote copies, remote signals or barrier semaphores. Data moves between devices by JAX's collectives and lax.ppermute only.
A program may use at most 192 MiB of HBM per device.

v0:
```python
import jax
import jax.numpy as jnp
from jax import lax
from jax.sharding import PartitionSpec as P

TW = 128
PTD = 2
STEPS = 2


def spread(block, axis, owner):
    block = jnp.where(lax.axis_index(axis) == owner, block, jnp.zeros_like(block))
    return lax.psum(block, axis)


def local(amplitudes, amp_mask, integrals, int_mask, steps):
    own_rows = amplitudes.shape[0]
    panel_width = amplitudes.shape[1]
    pair_tiles = amp_mask.shape[0]
    panel_tiles = amp_mask.shape[1]
    ab_width = integrals.shape[2]
    ab_tiles = ab_width // TW
    ladder = jnp.zeros((own_rows, ab_width), jnp.float32)
    for step_index in range(STEPS):
        amp_panel, panel_mask = (
            spread(amplitudes, "row", steps[step_index]),
            spread(amp_mask, "row", steps[step_index]),
        )
        tile_gate = panel_mask.astype(jnp.bfloat16)[:, None, :, None]
        masked = (amp_panel.reshape(pair_tiles, TW, panel_tiles, TW) * tile_gate).reshape(
            own_rows, panel_width
        )
        block_gate = int_mask[step_index].astype(jnp.bfloat16)[:, None, :, None]
        int_block = (integrals[step_index].reshape(PTD, TW, ab_tiles, TW) * block_gate).reshape(
            PTD * TW, ab_width
        )
        ladder = ladder + jnp.dot(
            masked,
            lax.all_gather(int_block, "col", axis=0, tiled=True),
            preferred_element_type=jnp.float32,
        )
    return ladder


def solution(mesh):
    return jax.shard_map(
        local,
        mesh=mesh,
        in_specs=(
            P("col", "row"),
            P("col", "row"),
            P(None, "col", "row"),
            P(None, "col", "row"),
            P(),
        ),
        out_specs=P("col", "row"),
        check_vma=False,
    )
```

profile of v0, /device:TPU:1, one launch (start us, length us, event | category | flops | bytes accessed | tf_op | source)
XLA Modules:
  0.0 267.9 jit_solution(9889551580946124755)
XLA Ops:
  7.4 0.0 all-reduce.4.cloned.1.call-start
  7.4 1.3 fusion.6
  10.0 9.5 %broadcast_select_fusion.1 = (bf16[1024,4096]{1,0:T(8,128)(2,1)}, bf16[1024,4096]{1,0:T(8,128)(2,1)}) fusion(bf16[1024,4096]{1,0:T(8,128)(2,1)} %param.5, pred[]{:T(512)S(6)} %eq.8, pred[]{:T(512)S(6)} %eq.9), kind=kLoop, calls=%fused_computation.7 | loop fusion | flops 8388608 | bytes 25165826 | tf_op jit(solution)/shard_map/jit(_where)/select_n | solution.py:12
  19.5 0.0 copy-start
  19.5 0.0 copy-start.2
  19.5 0.0 all-reduce.4.cloned.1.call-update
  19.6 0.0 copy-start.1
  19.6 0.0 all-gather.5.cloned.1.call-start
  19.6 1.2 copy-done
  20.9 0.1 fusion.5
  20.9 0.2 copy.11
  21.2 0.0 copy-done.2
  21.2 0.1 copy.9
  21.3 0.4 mul.53
  21.7 0.9 bitcast_multiply_fusion.6
  22.7 0.0 all-gather.5.cloned.1.call-update
  22.7 0.0 all-gather.3.cloned.1.call-start
  22.8 0.2 copy.10
  23.0 0.1 copy.7
  23.1 0.4 mul.47
  23.5 0.9 bitcast_multiply_fusion.7
  24.5 0.0 all-gather.3.cloned.1.call-update
  24.5 0.0 copy-done.1
  24.5 8.9 %all-reduce = (s32[8,32]{1,0:T(8,128)S(1)}, s32[8,32]{1,0:T(8,128)S(1)}) all-reduce(s32[8,32]{1,0:T(8,128)S(1)} %get-tuple-element.14, s32[8,32]{1,0:T(8,128)S(1)} %get-tuple-element.13), channel_id=1, replica_groups=mesh['row'=8,'col'=16] {'row'}, use_global_device_ids=true, to_apply=%region_3.4 | all-reduce | flops 512 | bytes 4096 | tf_op jit(solution)/shard_map/psum | solution.py:13
  33.5 172.4 %all-reduce.4.cloned.1.call-done = (bf16[1024,4096]{1,0:T(8,128)(2,1)}, bf16[1024,4096]{1,0:T(8,128)(2,1)}) async-done(((bf16[1024,4096]{1,0:T(8,128)(2,1)}, bf16[1024,4096]{1,0:T(8,128)(2,1)}), (bf16[1024,4096]{1,0:T(8,128)(2,1)}, bf16[1024,4096]{1,0:T(8,128)(2,1)})) %all-reduce.4.cloned.1.call-update) | async-done | bytes 16777232 | tf_op jit(solution)/shard_map/psum | solution.py:13
  205.9 0.0 all-gather.5.cloned.1.call-done
  205.9 4.4 %mul.50 = bf16[8,128,32,128]{3,2,1,0:T(8,128)(2,1)} broadcast(bf16[8,32]{1,0:T(8,128)(2,1)S(1)} %convert_element_type.24), dimensions={0,2} | broadcast | bytes 8389120 | tf_op jit(solution)/shard_map/mul | solution.py:30
  210.2 21.4 %fusion = f32[1024,1280]{1,0:T(8,128)} fusion(bf16[4096,1280]{0,1:T(8,128)(2,1)} %all-gather.5.cloned.1.call-done, bf16[1024,4096]{1,0:T(8,128)(2,1)} %get-tuple-element.7, bf16[128,8,32,128]{3,2,1,0:T(8,128)(2,1)} %bitcast.37), kind=kOutput, calls=%fused_computation.1 | convolution fusion | flops 10741612544 | bytes 32505856 | tf_op jit(solution)/shard_map/dot_general | solution.py:37
  231.6 0.0 all-gather.3.cloned.1.call-done
  231.6 4.5 %mul.44 = bf16[8,128,32,128]{3,2,1,0:T(8,128)(2,1)} broadcast(bf16[8,32]{1,0:T(8,128)(2,1)S(1)} %convert_element_type.22), dimensions={0,2} | broadcast | bytes 8389120 | tf_op jit(solution)/shard_map/mul | solution.py:30
  236.1 24.5 %fusion.4 = f32[1024,1280]{1,0:T(8,128)} fusion(f32[1024,1280]{1,0:T(8,128)} %fusion, bf16[4096,1280]{0,1:T(8,128)(2,1)} %all-gather.3.cloned.1.call-done, bf16[1024,4096]{1,0:T(8,128)(2,1)} %get-tuple-element.8, bf16[128,8,32,128]{3,2,1,0:T(8,128)(2,1)} %bitcast.36), kind=kOutput, calls=%fused_computation.8 | convolution fusion | flops 10742923264 | bytes 37748736 | tf_op jit(solution)/shard_map/dot_general | solution.py:37
  (5 shorter events, 0.0 us)
Async XLA Ops:
  7.4 198.5 %all-reduce.4.cloned.1.call-start = ((), (), s32[]{:S(2)}) async-start(), calls=%async_computation.2 | async-start | bytes 33554432 | tf_op jit(solution)/shard_map/psum | solution.py:13
  19.5 1.3 copy-start
  19.5 1.6 copy-start.2
  19.6 4.9 %copy-start.1 = (s32[8,32]{1,0:T(8,128)S(1)}, s32[8,32]{1,0:T(8,128)}, u32[]{:S(2)}) copy-start(s32[8,32]{1,0:T(8,128)} %param.6) | copy-start | bytes 3076
  19.6 186.3 %all-gather.5.cloned.1.call-start = ((), (), s32[]{:S(2)}) async-start(), calls=%async_computation.1 | async-start | bytes 11141120 | tf_op jit(solution)/shard_map/all_gather | solution.py:39
  22.7 208.9 %all-gather.3.cloned.1.call-start = ((), (), s32[]{:S(2)}) async-start(), calls=%async_computation | async-start | bytes 11141120 | tf_op jit(solution)/shard_map/all_gather | solution.py:39
Sparse Core Ops, SparseCore 0:
  19.7 186.1 all-reduce.3
Sparse Core Ops, SparseCore 1:
  22.8 90.4 all-gather.4
  115.2 87.6 all-gather.2
where the time goes:
time: 268 us
  waiting for transfers between devices  172 us (64%)
  matrix products  45.8 us (17%)
  between operations  16.2 us (6%)
  local copies, waits for them, and re-layouts  13 us (5%)
  other arithmetic  11.4 us (4%)
  blocking collectives  8.91 us (3%)
    psum x1, waiting for transfers between devices, spread(): return lax.psum(block, axis)  172 us
    dot_general x2, matrix products, local(): jnp.dot(masked, lax.all_gather(int_block, 'col', axis=0, tiled=True), pre...  45.8 us
    select_n x2, other arithmetic, spread(): jnp.where(lax.axis_index(axis) == owner, block, jnp.zeros_like(block))  9.55 us
    psum x1, blocking collectives, spread(): return lax.psum(block, axis)  8.91 us
    mul x2, local copies, waits for them, and re-layouts, local(): amp_panel.reshape(pair_tiles, TW, panel_tiles, TW) * tile_gate  8.81 us
  transfers between devices with their start and end apart: 3, of which 1 were waited for; matrix products, arithmetic and copies ran while one was open for 11% of the time, Pallas kernels for 0%

commit v1 on v0

v1 whole, which is shorter than its diff:
```python
import jax
import jax.numpy as jnp
from jax import lax
from jax.experimental import pallas as pl
from jax.experimental.pallas import tpu as pltpu
from jax.sharding import Mesh
from jax.sharding import PartitionSpec as P

TW = 128
STEPS = 2
RING = 4
ROW = ("y", "core")
COL = ("z", "x")
GRID = ("core", "z", "x")


def plane_perm(first, shift):
    pairs = []
    for core in range(2):
        for z in range(RING):
            for x in range(RING):
                along_z = (core == 0) == first
                to_z, to_x = ((z + shift) % RING, x) if along_z else (z, (x + shift) % RING)
                pairs.append((core * 16 + z * RING + x, core * 16 + to_z * RING + to_x))
    return pairs


def wrap(value):
    return lax.rem(value + 2 * RING, RING)


def origin(core, z, x, first_shift, second_shift):
    on_zero = wrap(z - first_shift) * RING + wrap(x - second_shift)
    on_one = wrap(z - second_shift) * RING + wrap(x - first_shift)
    return jnp.where(core == 0, on_zero, on_one)


def needed_tile(mask_ref, group):
    found = mask_ref[0, 2 * group + 1]
    for row in range(1, 8):
        found = found | mask_ref[row, 2 * group + 1]
    return jnp.where(found != 0, 1, 0)


def compress_kernel(mask_ref, info_ref, *refs):
    tiles, out_ref = refs[:-1], refs[-1]
    width = len(tiles)
    for place, tile_ref in enumerate(tiles):
        group = pl.program_id(0) * width + place
        column = 2 * group + needed_tile(mask_ref, group)
        for row in range(8):
            keep = mask_ref[row, column] != 0
            rows = slice(row * TW, (row + 1) * TW)
            tile = tile_ref[rows, :]
            for step in range(STEPS):
                shown = keep & (info_ref[step] == info_ref[2])
                out_ref[step, rows, place * TW:(place + 1) * TW] = jnp.where(shown, tile, jnp.zeros_like(tile))


def compress(amplitudes, amp_mask, info):
    rows = amplitudes.shape[0]
    groups = amp_mask.shape[1] // 2
    width = 2

    def column(place):
        def index(step, mask_ref, info_ref):
            group = step * width + place
            return 0, 2 * group + needed_tile(mask_ref, group)
        return index

    return pl.pallas_call(
        compress_kernel,
        grid_spec=pltpu.PrefetchScalarGridSpec(
            num_scalar_prefetch=2,
            grid=(groups // width,),
            in_specs=[pl.BlockSpec((rows, TW), column(place)) for place in range(width)],
            out_specs=pl.BlockSpec((STEPS, rows, width * TW), lambda step, *_: (0, 0, step)),
        ),
        out_shape=jax.ShapeDtypeStruct((STEPS, rows, groups * TW), amplitudes.dtype),
        compiler_params=pltpu.CompilerParams(vmem_limit_bytes=32 << 20),
        name="compress",
    )(amp_mask, info, *([amplitudes] * width))


def pick_kernel(step, needs_ref, info_ref, *refs):
    held, sent, sems = refs[:RING], refs[RING:2 * RING], refs[2 * RING]
    core, z, x = info_ref[3], info_ref[4], info_ref[5]
    copies = []
    for second in range(RING):
        reader = origin(core, z, x, 0, -second)
        for first in range(RING):
            group = origin(core, z, x, first, 0)
            tile = needs_ref[reader, step * 16 + group]
            copies.append(pltpu.make_async_copy(
                held[first].at[tile], sent[second].at[first], sems.at[second * RING + first]))
            copies[-1].start()
    for copy in copies:
        copy.wait()


def pick(step, needs, info, held):
    shape = jax.ShapeDtypeStruct((RING,) + held[0].shape[1:], held[0].dtype)
    return pl.pallas_call(
        lambda *refs: pick_kernel(step, *refs),
        in_specs=[pl.BlockSpec(memory_space=pltpu.SMEM)] * 2 + [pl.BlockSpec(memory_space=pl.ANY)] * RING,
        out_specs=[pl.BlockSpec(memory_space=pl.ANY)] * RING,
        out_shape=[shape] * RING,
        scratch_shapes=[pltpu.SemaphoreType.DMA((RING * RING,))],
        name="pick",
    )(needs, info, *held)


def ladder_kernel(info_ref, panel_ref, *refs):
    blocks, out_ref, gathered, sems = refs[:-3], refs[-3], refs[-2], refs[-1]
    depth = panel_ref.shape[2]

    @pl.when(pl.program_id(0) == 0)
    def _():
        core, z, x = info_ref[3], info_ref[4], info_ref[5]
        copies = []
        for step in range(STEPS):
            for second in range(RING):
                for first in range(RING):
                    place = origin(core, z, x, first, second)
                    start = pl.multiple_of(step * depth + place * TW, TW)
                    copies.append(pltpu.make_async_copy(
                        blocks[step * RING + second].at[first],
                        gathered.at[pl.ds(start, TW), :],
                        sems.at[len(copies)]))
                    copies[-1].start()
        for copy in copies:
            copy.wait()

    total = jnp.dot(panel_ref[0], gathered[:depth, :], preferred_element_type=jnp.float32)
    total += jnp.dot(panel_ref[1], gathered[depth:, :], preferred_element_type=jnp.float32)
    out_ref[...] = total


def multiply(info, panels, blocks):
    steps, rows, depth = panels.shape
    width = blocks[0].shape[-1]
    part = 256
    return pl.pallas_call(
        ladder_kernel,
        grid=(rows // part,),
        in_specs=[pl.BlockSpec(memory_space=pltpu.SMEM),
                  pl.BlockSpec((steps, part, depth), lambda m: (0, m, 0))]
        + [pl.BlockSpec(memory_space=pl.ANY)] * len(blocks),
        out_specs=pl.BlockSpec((part, width), lambda m: (m, 0)),
        out_shape=jax.ShapeDtypeStruct((rows, width), jnp.float32),
        scratch_shapes=[pltpu.VMEM((steps * depth, width), panels.dtype),
                        pltpu.SemaphoreType.DMA((steps * RING * RING,))],
        compiler_params=pltpu.CompilerParams(vmem_limit_bytes=40 << 20),
        cost_estimate=pl.CostEstimate(flops=2 * rows * steps * depth * width, bytes_accessed=24 << 20, transcendentals=0),
        name="ladder",
    )(info, panels, *blocks)


def local(amplitudes, amp_mask, integrals, int_mask, steps):
    tiles, ab_width = integrals.shape[1] // TW, integrals.shape[2]
    row = lax.axis_index(ROW)
    core, z, x = (lax.axis_index(axis) for axis in GRID)
    info = jnp.stack([steps[0], steps[1], row, core, z, x]).astype(jnp.int32)

    panels = lax.psum(compress(amplitudes, amp_mask, info), ROW)

    held = []
    for step in range(STEPS):
        gate = int_mask[step].astype(integrals.dtype)[:, None, :, None]
        block = integrals[step].reshape(tiles, TW, ab_width // TW, TW) * gate
        block = block.reshape(tiles, TW, ab_width)
        held.append([block] + [lax.ppermute(block, GRID, plane_perm(True, shift)) for shift in (1, 3, 2)])
        held[-1] = [held[-1][i] for i in (0, 1, 3, 2)]

    own = jnp.max(amp_mask, axis=0).reshape(-1, 2)[:, 1]
    groups = own.shape[0]
    by_row = lax.all_to_all(jnp.broadcast_to(own, (8, groups)), ROW, 0, 0, tiled=True)
    chosen = jnp.sum(jnp.where((steps[:, None] == jnp.arange(8))[:, :, None], by_row[None], 0), axis=1)
    needs = lax.all_to_all(
        jnp.broadcast_to(chosen.reshape(1, -1), (16, STEPS * groups)), COL, 0, 0, tiled=True)

    blocks = []
    for step in range(STEPS):
        sent = pick(step, needs, info, held[step])
        here = [sent[0]] + [lax.ppermute(sent[shift], GRID, plane_perm(False, shift)) for shift in (1, 2, 3)]
        blocks.extend(here)
    return multiply(info, panels, blocks)


def solution(mesh):
    grid = Mesh(mesh.devices.reshape(4, 2, 4, 4), ("y", "core", "z", "x"))
    return jax.shard_map(
        local,
        mesh=grid,
        in_specs=(P(COL, ROW), P(COL, ROW), P(None, COL, ROW), P(None, COL, ROW), P()),
        out_specs=P(COL, ROW),
        check_vma=False,
    )
```

time: 268 us -> 481 us (1.79); the launches traced: 268 us -> 473 us
  Pallas kernels: 0 us -> 345 us
  waiting for transfers between devices: 172 us -> 53.2 us
  matrix products: 45.8 us -> 0 us
  starting transfers between devices: 0.09 us -> 29.4 us
  other arithmetic: 11.4 us -> 0.28 us
  local copies, waits for them, and re-layouts: 13 us -> 21.1 us
    pallas_call x0 -> x4, Pallas kernels: none -> 345 us  [the longest x2 322 us: pick(): pl.pallas_call(lambda *refs: pick_kernel(step, *refs), in_specs=[pl.Block...]
    psum x1, waiting for transfers between devices: 172 us -> 0.01 us  [local(): panels = lax.psum(compress(amplitudes, amp_mask, info), ROW)]
    ppermute x0 -> x12, waiting for transfers between devices: none -> 48.4 us  [the longest x6 28.4 us: local(): lax.ppermute(sent[shift], GRID, plane_perm(False, shift))]
    dot_general x2 -> x0, matrix products: 45.8 us -> none  [local(): jnp.dot(masked, lax.all_gather(int_block, 'col', axis=0, tiled=True), pre...]
    ppermute x0 -> x12, starting transfers between devices: none -> 22.5 us  [the longest x6 13.6 us: local(): lax.ppermute(sent[shift], GRID, plane_perm(False, shift))]
    unnamed x8 -> x51, local copies, waits for them, and re-layouts: 1.71 us -> 19.3 us
    all_to_all x0 -> x1, blocking collectives: none -> 10.7 us  [local(): lax.all_to_all(jnp.broadcast_to(chosen.reshape(1, -1), (16, STEPS * group...]
    mul x4 -> x0, local copies, waits for them, and re-layouts: 9.65 us -> none  [the longest x2 8.81 us: local(): amp_panel.reshape(pair_tiles, TW, panel_tiles, TW) * tile_gate]
  transfers between devices with their start and end apart: 3 -> 14, of which waited for: 1 -> 5; matrix products, arithmetic and copies ran while one was open for 11% -> 0% of each run, Pallas kernels for 0% -> 68%
where the time goes in v1:
time: 481 us; the launch traced here: 473 us
  Pallas kernels  345 us (72%)
  waiting for transfers between devices  53.2 us (11%)
  starting transfers between devices  29.4 us (6%)
  local copies, waits for them, and re-layouts  21.1 us (4%)
  between operations  13.6 us (3%)
  blocking collectives  10.7 us (2%)
    pallas_call x2, Pallas kernels, pick(): pl.pallas_call(lambda *refs: pick_kernel(step, *refs), in_specs=[pl.Block...  322 us
    ppermute x6, waiting for transfers between devices, local(): lax.ppermute(sent[shift], GRID, plane_perm(False, shift))  28.4 us
    ppermute x6, waiting for transfers between devices, local(): lax.ppermute(block, GRID, plane_perm(True, shift))  20 us
    unnamed x51, local copies, waits for them, and re-layouts  19.3 us
    pallas_call x1, Pallas kernels, multiply(): pl.pallas_call(ladder_kernel, grid=(rows // part,), in_specs=[pl.BlockSpe...  17.5 us
    ppermute x6, starting transfers between devices, local(): lax.ppermute(sent[shift], GRID, plane_perm(False, shift))  13.6 us
    all_to_all x1, blocking collectives, local(): lax.all_to_all(jnp.broadcast_to(chosen.reshape(1, -1), (16, STEPS * group...  10.7 us
  transfers between devices with their start and end apart: 14, of which 5 were waited for; matrix products, arithmetic and copies ran while one was open for 0% of the time, Pallas kernels for 68%

profile of v1, /device:TPU:1, one launch (start us, length us, event | category | flops | bytes accessed | tf_op | source)
XLA Modules:
  0.0 472.8 jit_solution(409996397169274927)
XLA Ops:
  6.5 0.7 stack.19.info_ref.refs_1_
  7.3 3.4 copy-done
  10.7 0.7 copy-done.2
  11.3 5.4 %compress.1 = bf16[2,1024,2048]{2,1,0:T(8,128)(2,1)S(1)} custom-call(s32[8,32]{1,0:T(8,128)S(1)} %copy-done.2, s32[6]{0:T(128)S(1)} %stack.19.info_ref.refs_1_, bf16[1024,4096]{1,0:T(8,128)(2,1)S(1)} %copy-done, bf16[1024,4096]{1,0:T(8,128)(2,1)S(1)} %copy-done), custom_call_target="tpu_custom_call" | custom-call | tf_op jit(solution)/shard_map/compress/pallas_call | solution.py:71
  16.8 3.2 copy-done.1
  20.1 0.7 copy-done.22
  20.7 0.1 broadcast_bitcast_fusion
  20.8 0.5 copy-done.16
  21.4 0.1 fusion
  21.5 2.1 collective-permute-start
  23.7 2.5 collective-permute-start.1
  26.1 1.2 collective-permute-start.2
  27.3 0.1 reshape.60
  27.4 0.2 slice_reduce_fusion
  27.6 0.6 broadcast_in_dim.42
  28.2 6.8 %all-to-all-start = ((s32[8,1,16]{2,1,0:T(1,128)}), s32[8,1,16]{2,1,0:T(1,128)S(1)}, u32[]{:S(2)}, u32[]{:S(2)}) async-start(s32[8,1,16]{2,1,0:T(1,128)} %broadcast_in_dim.42), calls=%async_computation | async-start | bytes 8192 | tf_op jit(solution)/shard_map/all_to_all | solution.py:177
  35.0 0.1 iota_compare_fusion
  35.1 4.7 all-to-all-done
  39.8 0.1 select_reduce_fusion
  39.9 0.1 broadcast_in_dim.46
  40.0 10.7 %all_to_all.14 = s32[16,1,32]{2,1,0:T(1,128)} all-to-all(s32[16,1,32]{2,1,0:T(1,128)S(1)} %broadcast_in_dim.47), channel_id=1, replica_groups=mesh['y'=4,'core'=2,'z'=4,'x'=4] {'z','x'}, dimensions={0} | all-to-all | bytes 4096 | tf_op jit(solution)/shard_map/all_to_all | solution.py:179
  50.7 0.8 copy-done.17
  51.5 0.2 copy-done.18
  51.7 0.2 copy-done.19
  52.0 160.9 %pick.2 = (bf16[4,128,1280]{2,1,0:T(8,128)(2,1)}, bf16[4,128,1280]{2,1,0:T(8,128)(2,1)}, bf16[4,128,1280]{2,1,0:T(8,128)(2,1)}, bf16[4,128,1280]{2,1,0:T(8,128)(2,1)}) custom-call(s32[16,32]{1,0:T(8,128)} %bitcast.24, s32[6]{0:T(128)} %copy-done.4, bf16[2,128,1280]{2,1,0:T(8,128)(2,1)} %copy-done.14, bf16[2,128,1280]{2,1,0:T(8,128)(2,1)} %copy-done.17, ...), custom_call_target="tpu_custom_call" | custom-call | tf_op jit(solution)/shard_map/pick/pallas_call | solution.py:103
  212.8 0.2 collective-permute-start.3
  213.0 0.1 broadcast_multiply_fusion.refs_2_
  213.1 0.4 collective-permute-start.6
  213.5 1.8 collective-permute-start.7
  215.3 1.1 collective-permute-start.8
  216.3 1.6 collective-permute-start.4
  217.9 11.4 %collective-permute-done.6.refs_3_ = bf16[2,128,1280]{2,1,0:T(8,128)(2,1)S(1)} collective-permute-done((bf16[2,128,1280]{2,1,0:T(8,128)(2,1)S(1)}, bf16[2,128,1280]{2,1,0:T(8,128)(2,1)S(1)}, u32[]{:S(2)}, u32[]{:S(2)}) %collective-permute-start.6) | collective-permute-done | bytes 655392 | tf_op jit(solution)/shard_map/ppermute | solution.py:172
  229.4 4.3 collective-permute-start.5
  233.7 8.5 %collective-permute-done.7.refs_4_ = bf16[2,128,1280]{2,1,0:T(8,128)(2,1)S(1)} collective-permute-done((bf16[2,128,1280]{2,1,0:T(8,128)(2,1)S(1)}, bf16[2,128,1280]{2,1,0:T(8,128)(2,1)S(1)}, u32[]{:S(2)}, u32[]{:S(2)}) %collective-permute-start.7) | collective-permute-done | bytes 655392 | tf_op jit(solution)/shard_map/ppermute | solution.py:172
  242.2 0.8 copy-done.21
  243.1 160.9 %pick.3 = (bf16[4,128,1280]{2,1,0:T(8,128)(2,1)}, bf16[4,128,1280]{2,1,0:T(8,128)(2,1)}, bf16[4,128,1280]{2,1,0:T(8,128)(2,1)}, bf16[4,128,1280]{2,1,0:T(8,128)(2,1)}) custom-call(s32[16,32]{1,0:T(8,128)} %bitcast.25, s32[6]{0:T(128)} %copy-done.4, bf16[2,128,1280]{2,1,0:T(8,128)(2,1)} %copy-done.15, bf16[2,128,1280]{2,1,0:T(8,128)(2,1)} %copy-done.20, ...), custom_call_target="tpu_custom_call" | custom-call | tf_op jit(solution)/shard_map/pick/pallas_call | solution.py:103
  404.0 0.1 collective-permute-start.9
  404.1 7.4 %collective-permute-start.10 = (bf16[4,128,1280]{2,1,0:T(8,128)(2,1)}, bf16[4,128,1280]{2,1,0:T(8,128)(2,1)S(1)}, u32[]{:S(2)}, u32[]{:S(2)}) collective-permute-start(bf16[4,128,1280]{2,1,0:T(8,128)(2,1)} %get-tuple-element.19), channel_id=1, source_target_pairs={{0,2},{1,3},{2,0},{3,1},{4,6},{5,7},{6,4},{7,5},{8,10},{9,11},{10,... | collective-permute-start | bytes 3932168 | tf_op jit(solution)/shard_map/ppermute | solution.py:185
  411.5 14.3 %collective-permute-done.9.refs_5_ = bf16[4,128,1280]{2,1,0:T(8,128)(2,1)S(1)} collective-permute-done((bf16[4,128,1280]{2,1,0:T(8,128)(2,1)}, bf16[4,128,1280]{2,1,0:T(8,128)(2,1)S(1)}, u32[]{:S(2)}, u32[]{:S(2)}) %collective-permute-start.9) | collective-permute-done | bytes 1310752 | tf_op jit(solution)/shard_map/ppermute | solution.py:185
  425.8 1.1 copy-done.8
  426.9 14.1 %collective-permute-done.10.refs_6_ = bf16[4,128,1280]{2,1,0:T(8,128)(2,1)S(1)} collective-permute-done((bf16[4,128,1280]{2,1,0:T(8,128)(2,1)}, bf16[4,128,1280]{2,1,0:T(8,128)(2,1)S(1)}, u32[]{:S(2)}, u32[]{:S(2)}) %collective-permute-start.10) | collective-permute-done | bytes 1310752 | tf_op jit(solution)/shard_map/ppermute | solution.py:185
  441.0 1.1 copy-done.10
  442.1 1.1 copy-done.12
  443.2 1.3 copy-done.7
  444.5 1.3 copy-done.9
  445.8 1.3 copy-done.11
  447.2 1.3 copy-done.13
  448.5 17.5 %ladder.1 = f32[1024,1280]{1,0:T(8,128)} custom-call(s32[6]{0:T(128)S(1)} %copy-done.5, bf16[2,1024,2048]{2,1,0:T(8,128)(2,1)} %all-reduce.2.cloned.1.call-done.panel_ref, bf16[4,128,1280]{2,1,0:T(8,128)(2,1)S(1)} %copy-done.6, bf16[4,128,1280]{2,1,0:T(8,128)(2,1)S(1)} %collective-permute-done.3.refs_1_, ...), custom_call_target="tpu_custom_call" | custom-call | flops 10737418240 | bytes 25165824 | tf_op jit(solution)/shard_map/ladder/pallas_call | solution.py:143
  (51 shorter events, 0.2 us)
Async XLA Ops:
  6.5 436.7 %all-reduce.2.cloned.1.call-start = ((), (), s32[]{:S(2)}) async-start(), calls=%async_computation.2 | async-start | bytes 16777216 | tf_op jit(solution)/shard_map/psum | solution.py:165
  7.3 3.4 copy-start
  10.7 0.7 copy-start.2
  11.3 5.4 %copy-start.4 = (s32[6]{0:T(128)}, s32[6]{0:T(128)S(1)}, u32[]{:S(2)}) copy-start(s32[6]{0:T(128)S(1)} %stack.19.info_ref.refs_1_) | copy-start | bytes 76
  16.8 3.3 copy-start.1
  20.0 0.7 copy-start.22
  20.0 1.3 copy-start.16
  21.4 5.8 %copy-start.3 = (s32[8,32]{1,0:T(8,128)S(1)}, s32[8,32]{1,0:T(8,128)}, u32[]{:S(2)}) copy-start(s32[8,32]{1,0:T(8,128)} %mask_ref.1) | copy-start | bytes 3076
  21.5 13.5 %copy-start.23 = (s32[2]{0:T(128)S(1)}, s32[2]{0:T(128)}, u32[]{:S(2)}) copy-start(s32[2]{0:T(128)} %param.9) | copy-start | bytes 28
  21.5 29.2 %copy-start.14 = (bf16[2,128,1280]{2,1,0:T(8,128)(2,1)}, bf16[2,128,1280]{2,1,0:T(8,128)(2,1)S(1)}, u32[]{:S(2)}) copy-start(bf16[2,128,1280]{2,1,0:T(8,128)(2,1)S(1)} %broadcast_multiply_fusion.1.refs_2_) | copy-start | bytes 1966084
  21.5 29.1 %collective-permute-start = (bf16[2,128,1280]{2,1,0:T(8,128)(2,1)S(1)}, bf16[2,128,1280]{2,1,0:T(8,128)(2,1)S(1)}, u32[]{:S(2)}, u32[]{:S(2)}) collective-permute-start(bf16[2,128,1280]{2,1,0:T(8,128)(2,1)S(1)} %broadcast_multiply_fusion.1.refs_2_), channel_id=1, source_target_pairs={{0,4},{1,5},{2,6},{3,7},{4,8},{5,9},{6,10},{7,11},{8,12},{9,13},{1... | collective-permute-start | bytes 1966088 | tf_op jit(solution)/shard_map/ppermute | solution.py:172
  23.7 27.0 %collective-permute-start.1 = (bf16[2,128,1280]{2,1,0:T(8,128)(2,1)S(1)}, bf16[2,128,1280]{2,1,0:T(8,128)(2,1)S(1)}, u32[]{:S(2)}, u32[]{:S(2)}) collective-permute-start(bf16[2,128,1280]{2,1,0:T(8,128)(2,1)S(1)} %broadcast_multiply_fusion.1.refs_2_), channel_id=1, source_target_pairs={{0,8},{1,9},{2,10},{3,11},{4,12},{5,13},{6,14},{7,15},{8,0},{9,1},... | collective-permute-start | bytes 1966088 | tf_op jit(solution)/shard_map/ppermute | solution.py:172
  26.1 24.6 %collective-permute-start.2 = (bf16[2,128,1280]{2,1,0:T(8,128)(2,1)S(1)}, bf16[2,128,1280]{2,1,0:T(8,128)(2,1)S(1)}, u32[]{:S(2)}, u32[]{:S(2)}) collective-permute-start(bf16[2,128,1280]{2,1,0:T(8,128)(2,1)S(1)} %broadcast_multiply_fusion.1.refs_2_), channel_id=1, source_target_pairs={{0,12},{1,13},{2,14},{3,15},{4,0},{5,1},{6,2},{7,3},{8,4},{9,5},{1... | collective-permute-start | bytes 1966088 | tf_op jit(solution)/shard_map/ppermute | solution.py:172
  28.2 11.6 %all-to-all-start = ((s32[8,1,16]{2,1,0:T(1,128)}), s32[8,1,16]{2,1,0:T(1,128)S(1)}, u32[]{:S(2)}, u32[]{:S(2)}) async-start(s32[8,1,16]{2,1,0:T(1,128)} %broadcast_in_dim.42), calls=%async_computation | async-start | bytes 8192 | tf_op jit(solution)/shard_map/all_to_all | solution.py:177
  50.7 0.9 copy-start.17
  50.7 1.1 copy-start.18
  50.7 1.3 copy-start.19
  212.8 198.6 %collective-permute-start.3 = (bf16[4,128,1280]{2,1,0:T(8,128)(2,1)}, bf16[4,128,1280]{2,1,0:T(8,128)(2,1)S(1)}, u32[]{:S(2)}, u32[]{:S(2)}) collective-permute-start(bf16[4,128,1280]{2,1,0:T(8,128)(2,1)} %get-tuple-element.14), channel_id=1, source_target_pairs={{0,1},{1,2},{2,3},{3,0},{4,5},{5,6},{6,7},{7,4},{8,9},{9,10},{10,1... | collective-permute-start | bytes 3932168 | tf_op jit(solution)/shard_map/ppermute | solution.py:185
  213.1 30.0 %copy-start.15 = (bf16[2,128,1280]{2,1,0:T(8,128)(2,1)}, bf16[2,128,1280]{2,1,0:T(8,128)(2,1)S(1)}, u32[]{:S(2)}) copy-start(bf16[2,128,1280]{2,1,0:T(8,128)(2,1)S(1)} %broadcast_multiply_fusion.refs_2_) | copy-start | bytes 1966084
  213.1 16.3 %collective-permute-start.6 = (bf16[2,128,1280]{2,1,0:T(8,128)(2,1)S(1)}, bf16[2,128,1280]{2,1,0:T(8,128)(2,1)S(1)}, u32[]{:S(2)}, u32[]{:S(2)}) collective-permute-start(bf16[2,128,1280]{2,1,0:T(8,128)(2,1)S(1)} %broadcast_multiply_fusion.refs_2_), channel_id=1, source_target_pairs={{0,4},{1,5},{2,6},{3,7},{4,8},{5,9},{6,10},{7,11},{8,12},{9,13},{1... | collective-permute-start | bytes 1966088 | tf_op jit(solution)/shard_map/ppermute | solution.py:172
  213.5 28.8 %collective-permute-start.7 = (bf16[2,128,1280]{2,1,0:T(8,128)(2,1)S(1)}, bf16[2,128,1280]{2,1,0:T(8,128)(2,1)S(1)}, u32[]{:S(2)}, u32[]{:S(2)}) collective-permute-start(bf16[2,128,1280]{2,1,0:T(8,128)(2,1)S(1)} %broadcast_multiply_fusion.refs_2_), channel_id=1, source_target_pairs={{0,8},{1,9},{2,10},{3,11},{4,12},{5,13},{6,14},{7,15},{8,0},{9,1},... | collective-permute-start | bytes 1966088 | tf_op jit(solution)/shard_map/ppermute | solution.py:172
  215.3 27.8 %collective-permute-start.8 = (bf16[2,128,1280]{2,1,0:T(8,128)(2,1)S(1)}, bf16[2,128,1280]{2,1,0:T(8,128)(2,1)}, u32[]{:S(2)}, u32[]{:S(2)}) collective-permute-start(bf16[2,128,1280]{2,1,0:T(8,128)(2,1)S(1)} %broadcast_multiply_fusion.refs_2_), channel_id=1, source_target_pairs={{0,12},{1,13},{2,14},{3,15},{4,0},{5,1},{6,2},{7,3},{8,4},{9,5},{1... | collective-permute-start | bytes 1966088 | tf_op jit(solution)/shard_map/ppermute | solution.py:172
  216.3 195.1 %collective-permute-start.4 = (bf16[4,128,1280]{2,1,0:T(8,128)(2,1)}, bf16[4,128,1280]{2,1,0:T(8,128)(2,1)}, u32[]{:S(2)}, u32[]{:S(2)}) collective-permute-start(bf16[4,128,1280]{2,1,0:T(8,128)(2,1)} %get-tuple-element.15), channel_id=1, source_target_pairs={{0,2},{1,3},{2,0},{3,1},{4,6},{5,7},{6,4},{7,5},{8,10},{9,11},{10,... | collective-permute-start | bytes 3932168 | tf_op jit(solution)/shard_map/ppermute | solution.py:185
  229.4 12.9 %copy-start.20 = (bf16[2,128,1280]{2,1,0:T(8,128)(2,1)}, bf16[2,128,1280]{2,1,0:T(8,128)(2,1)S(1)}, u32[]{:S(2)}) copy-start(bf16[2,128,1280]{2,1,0:T(8,128)(2,1)S(1)} %collective-permute-done.6.refs_3_) | copy-start | bytes 1966084
  229.4 213.8 %copy-start.5 = (s32[6]{0:T(128)S(1)}, s32[6]{0:T(128)}, u32[]{:S(2)}) copy-start(s32[6]{0:T(128)} %copy-done.4) | copy-start | bytes 76
  229.4 213.8 %copy-start.6 = (bf16[4,128,1280]{2,1,0:T(8,128)(2,1)S(1)}, bf16[4,128,1280]{2,1,0:T(8,128)(2,1)}, u32[]{:S(2)}) copy-start(bf16[4,128,1280]{2,1,0:T(8,128)(2,1)} %get-tuple-element.13.refs_0_) | copy-start | bytes 3932164
  229.4 182.1 %collective-permute-start.5 = (bf16[4,128,1280]{2,1,0:T(8,128)(2,1)}, bf16[4,128,1280]{2,1,0:T(8,128)(2,1)}, u32[]{:S(2)}, u32[]{:S(2)}) collective-permute-start(bf16[4,128,1280]{2,1,0:T(8,128)(2,1)} %get-tuple-element.16), channel_id=1, source_target_pairs={{0,3},{1,0},{2,1},{3,2},{4,7},{5,4},{6,5},{7,6},{8,11},{9,8},{10,9... | collective-permute-start | bytes 3932168 | tf_op jit(solution)/shard_map/ppermute | solution.py:185
  242.2 0.8 copy-start.21
  404.0 21.8 %collective-permute-start.9 = (bf16[4,128,1280]{2,1,0:T(8,128)(2,1)}, bf16[4,128,1280]{2,1,0:T(8,128)(2,1)S(1)}, u32[]{:S(2)}, u32[]{:S(2)}) collective-permute-start(bf16[4,128,1280]{2,1,0:T(8,128)(2,1)} %get-tuple-element.18), channel_id=1, source_target_pairs={{0,1},{1,2},{2,3},{3,0},{4,5},{5,6},{6,7},{7,4},{8,9},{9,10},{10,1... | collective-permute-start | bytes 3932168 | tf_op jit(solution)/shard_map/ppermute | solution.py:185
  404.1 36.9 %collective-permute-start.10 = (bf16[4,128,1280]{2,1,0:T(8,128)(2,1)}, bf16[4,128,1280]{2,1,0:T(8,128)(2,1)S(1)}, u32[]{:S(2)}, u32[]{:S(2)}) collective-permute-start(bf16[4,128,1280]{2,1,0:T(8,128)(2,1)} %get-tuple-element.19), channel_id=1, source_target_pairs={{0,2},{1,3},{2,0},{3,1},{4,6},{5,7},{6,4},{7,5},{8,10},{9,11},{10,... | collective-permute-start | bytes 3932168 | tf_op jit(solution)/shard_map/ppermute | solution.py:185
  411.5 30.7 %collective-permute-start.11 = (bf16[4,128,1280]{2,1,0:T(8,128)(2,1)}, bf16[4,128,1280]{2,1,0:T(8,128)(2,1)S(1)}, u32[]{:S(2)}, u32[]{:S(2)}) collective-permute-start(bf16[4,128,1280]{2,1,0:T(8,128)(2,1)} %get-tuple-element.20), channel_id=1, source_target_pairs={{0,3},{1,0},{2,1},{3,2},{4,7},{5,4},{6,5},{7,6},{8,11},{9,8},{10,9... | collective-permute-start | bytes 3932168 | tf_op jit(solution)/shard_map/ppermute | solution.py:185
  425.8 1.1 copy-start.8
  441.0 1.1 copy-start.10
  442.1 1.1 copy-start.12
  443.2 1.3 copy-start.7
  444.5 1.3 copy-start.9
  445.8 1.3 copy-start.11
  447.2 1.3 copy-start.13
Sparse Core Ops, SparseCore 0:
  20.2 106.8 all-reduce.1

commit v2 on v1

--- a/solution.py
+++ b/solution.py
@@ -102,7 +102,7 @@
     shape = jax.ShapeDtypeStruct((RING,) + held[0].shape[1:], held[0].dtype)
     return pl.pallas_call(
         lambda *refs: pick_kernel(step, *refs),
-        in_specs=[pl.BlockSpec(memory_space=pltpu.SMEM)] * 2 + [pl.BlockSpec(memory_space=pl.ANY)] * RING,
+        in_specs=[pl.BlockSpec(memory_space=pltpu.SMEM)] * 2 + [pl.BlockSpec(memory_space=pltpu.VMEM)] * RING,
         out_specs=[pl.BlockSpec(memory_space=pl.ANY)] * RING,
         out_shape=[shape] * RING,
         scratch_shapes=[pltpu.SemaphoreType.DMA((RING * RING,))],
@@ -111,28 +111,19 @@
 
 
 def ladder_kernel(info_ref, panel_ref, *refs):
-    blocks, out_ref, gathered, sems = refs[:-3], refs[-3], refs[-2], refs[-1]
-    depth = panel_ref.shape[2]
-
-    @pl.when(pl.program_id(0) == 0)
-    def _():
-        core, z, x = info_ref[3], info_ref[4], info_ref[5]
-        copies = []
-        for step in range(STEPS):
-            for second in range(RING):
-                for first in range(RING):
-                    place = origin(core, z, x, first, second)
-                    start = pl.multiple_of(step * depth + place * TW, TW)
-                    copies.append(pltpu.make_async_copy(
-                        blocks[step * RING + second].at[first],
-                        gathered.at[pl.ds(start, TW), :],
-                        sems.at[len(copies)]))
-                    copies[-1].start()
-        for copy in copies:
-            copy.wait()
-
-    total = jnp.dot(panel_ref[0], gathered[:depth, :], preferred_element_type=jnp.float32)
-    total += jnp.dot(panel_ref[1], gathered[depth:, :], preferred_element_type=jnp.float32)
+    blocks, out_ref = refs[:-1], refs[-1]
+    core, z, x = info_ref[3], info_ref[4], info_ref[5]
+    total = None
+    for step in range(STEPS):
+        for second in range(RING):
+            columns = []
+            for first in range(RING):
+                start = pl.multiple_of(origin(core, z, x, first, second) * TW, TW)
+                columns.append(panel_ref[step, :, pl.ds(start, TW)])
+            block_ref = blocks[step * RING + second]
+            block = block_ref[...].reshape(RING * TW, block_ref.shape[2])
+            part = jnp.dot(jnp.concatenate(columns, axis=1), block, preferred_element_type=jnp.float32)
+            total = part if total is None else total + part
     out_ref[...] = total
 
 
@@ -145,11 +136,9 @@
         grid=(rows // part,),
         in_specs=[pl.BlockSpec(memory_space=pltpu.SMEM),
                   pl.BlockSpec((steps, part, depth), lambda m: (0, m, 0))]
-        + [pl.BlockSpec(memory_space=pl.ANY)] * len(blocks),
+        + [pl.BlockSpec(memory_space=pltpu.VMEM)] * len(blocks),
         out_specs=pl.BlockSpec((part, width), lambda m: (m, 0)),
         out_shape=jax.ShapeDtypeStruct((rows, width), jnp.float32),
-        scratch_shapes=[pltpu.VMEM((steps * depth, width), panels.dtype),
-                        pltpu.SemaphoreType.DMA((steps * RING * RING,))],
         compiler_params=pltpu.CompilerParams(vmem_limit_bytes=40 << 20),
         cost_estimate=pl.CostEstimate(flops=2 * rows * steps * depth * width, bytes_accessed=24 << 20, transcendentals=0),
         name="ladder",

time: 481 us -> 166 us (0.35); the launches traced: 473 us -> 163 us
  Pallas kernels: 345 us -> 29.3 us
  waiting for transfers between devices: 53.2 us -> 58.5 us
    pallas_call x2, Pallas kernels: 322 us -> 8.58 us  [pick(): pl.pallas_call(lambda *refs: pick_kernel(step, *refs), in_specs=[pl.Block...]
    ppermute x6, waiting for transfers between devices: 28.4 us -> 33.8 us  [local(): lax.ppermute(sent[shift], GRID, plane_perm(False, shift))]
  transfers between devices with their start and end apart: 14 -> 14, of which waited for: 5 -> 7; matrix products, arithmetic and copies ran while one was open for 0% -> 1% of each run, Pallas kernels for 68% -> 5%
where the time goes in v2:
time: 166 us; the launch traced here: 163 us
  waiting for transfers between devices  58.5 us (35%)
  starting transfers between devices  29.3 us (18%)
  Pallas kernels  29.3 us (18%)
  local copies, waits for them, and re-layouts  21.1 us (13%)
  between operations  13.6 us (8%)
  blocking collectives  10.7 us (6%)
    ppermute x6, waiting for transfers between devices, local(): lax.ppermute(sent[shift], GRID, plane_perm(False, shift))  33.8 us
    ppermute x6, waiting for transfers between devices, local(): lax.ppermute(block, GRID, plane_perm(True, shift))  20 us
    unnamed x51, local copies, waits for them, and re-layouts  19.3 us
    pallas_call x1, Pallas kernels, multiply(): pl.pallas_call(ladder_kernel, grid=(rows // part,), in_specs=[pl.BlockSpe...  15.3 us
    ppermute x6, starting transfers between devices, local(): lax.ppermute(sent[shift], GRID, plane_perm(False, shift))  13.6 us
    all_to_all x1, blocking collectives, local(): lax.all_to_all(jnp.broadcast_to(chosen.reshape(1, -1), (16, STEPS * group...  10.7 us
    ppermute x6, starting transfers between devices, local(): lax.ppermute(block, GRID, plane_perm(True, shift))  8.94 us
    pallas_call x2, Pallas kernels, pick(): pl.pallas_call(lambda *refs: pick_kernel(step, *refs), in_specs=[pl.Block...  8.58 us
  transfers between devices with their start and end apart: 14, of which 7 were waited for; matrix products, arithmetic and copies ran while one was open for 1% of the time, Pallas kernels for 5%

profile of v2, /device:TPU:1, one launch (start us, length us, event | category | flops | bytes accessed | tf_op | source)
XLA Modules:
  0.0 162.8 jit_solution(5576003673503818424)
XLA Ops:
  6.5 0.7 stack.19.info_ref.refs_1_
  7.3 3.4 %copy-done = bf16[1024,4096]{1,0:T(8,128)(2,1)S(1)} copy-done((bf16[1024,4096]{1,0:T(8,128)(2,1)S(1)}, bf16[1024,4096]{1,0:T(8,128)(2,1)}, u32[]{:S(2)}) %copy-start) | copy-done | bytes 8388632
  10.7 0.7 copy-done.2
  11.3 5.4 %compress.1 = bf16[2,1024,2048]{2,1,0:T(8,128)(2,1)S(1)} custom-call(s32[8,32]{1,0:T(8,128)S(1)} %copy-done.2, s32[6]{0:T(128)S(1)} %stack.19.info_ref.refs_1_, bf16[1024,4096]{1,0:T(8,128)(2,1)S(1)} %copy-done, bf16[1024,4096]{1,0:T(8,128)(2,1)S(1)} %copy-done), custom_call_target="tpu_custom_call" | custom-call | tf_op jit(solution)/shard_map/compress/pallas_call | solution.py:71
  16.8 3.2 %copy-done.1 = bf16[2,1024,2048]{2,1,0:T(8,128)(2,1)} copy-done((bf16[2,1024,2048]{2,1,0:T(8,128)(2,1)}, bf16[2,1024,2048]{2,1,0:T(8,128)(2,1)S(1)}, u32[]{:S(2)}) %copy-start.1) | copy-done | bytes 8388632
  20.1 0.7 copy-done.22
  20.7 0.1 broadcast_bitcast_fusion
  20.8 0.5 copy-done.16
  21.4 0.1 fusion
  21.5 2.1 %collective-permute-start = (bf16[2,128,1280]{2,1,0:T(8,128)(2,1)S(1)}, bf16[2,128,1280]{2,1,0:T(8,128)(2,1)S(1)}, u32[]{:S(2)}, u32[]{:S(2)}) collective-permute-start(bf16[2,128,1280]{2,1,0:T(8,128)(2,1)S(1)} %broadcast_multiply_fusion.1.refs_2_), channel_id=1, source_target_pairs={{0,4},{1,5},{2,6},{3,7},{4,8},{5,9},{6,10},{7,11},{8,12},{9,13},{1... | collective-permute-start | bytes 1966088 | tf_op jit(solution)/shard_map/ppermute | solution.py:161
  23.7 2.5 %collective-permute-start.1 = (bf16[2,128,1280]{2,1,0:T(8,128)(2,1)S(1)}, bf16[2,128,1280]{2,1,0:T(8,128)(2,1)S(1)}, u32[]{:S(2)}, u32[]{:S(2)}) collective-permute-start(bf16[2,128,1280]{2,1,0:T(8,128)(2,1)S(1)} %broadcast_multiply_fusion.1.refs_2_), channel_id=1, source_target_pairs={{0,8},{1,9},{2,10},{3,11},{4,12},{5,13},{6,14},{7,15},{8,0},{9,1},... | collective-permute-start | bytes 1966088 | tf_op jit(solution)/shard_map/ppermute | solution.py:161
  26.1 1.2 collective-permute-start.2
  27.3 0.1 reshape.60
  27.4 0.2 slice_reduce_fusion
  27.6 0.6 broadcast_in_dim.42
  28.2 6.8 %all-to-all-start = ((s32[8,1,16]{2,1,0:T(1,128)}), s32[8,1,16]{2,1,0:T(1,128)S(1)}, u32[]{:S(2)}, u32[]{:S(2)}) async-start(s32[8,1,16]{2,1,0:T(1,128)} %broadcast_in_dim.42), calls=%async_computation | async-start | bytes 8192 | tf_op jit(solution)/shard_map/all_to_all | solution.py:166
  35.1 4.7 %all-to-all-done = s32[8,1,16]{2,1,0:T(1,128)S(1)} async-done(((s32[8,1,16]{2,1,0:T(1,128)}), s32[8,1,16]{2,1,0:T(1,128)S(1)}, u32[]{:S(2)}, u32[]{:S(2)}) %all-to-all-start) | async-done | bytes 544 | tf_op jit(solution)/shard_map/all_to_all | solution.py:166
  39.8 0.1 select_reduce_fusion
  39.9 0.1 broadcast_in_dim.46
  40.0 10.7 %all_to_all.14 = s32[16,1,32]{2,1,0:T(1,128)} all-to-all(s32[16,1,32]{2,1,0:T(1,128)S(1)} %broadcast_in_dim.47), channel_id=1, replica_groups=mesh['y'=4,'core'=2,'z'=4,'x'=4] {'z','x'}, dimensions={0} | all-to-all | bytes 4096 | tf_op jit(solution)/shard_map/all_to_all | solution.py:168
  50.7 0.8 copy-done.17
  51.5 0.2 copy-done.18
  51.7 0.2 copy-done.19
  52.0 4.2 %pick.2 = (bf16[4,128,1280]{2,1,0:T(8,128)(2,1)}, bf16[4,128,1280]{2,1,0:T(8,128)(2,1)}, bf16[4,128,1280]{2,1,0:T(8,128)(2,1)}, bf16[4,128,1280]{2,1,0:T(8,128)(2,1)}) custom-call(s32[16,32]{1,0:T(8,128)} %bitcast.24, s32[6]{0:T(128)} %copy-done.4, bf16[2,128,1280]{2,1,0:T(8,128)(2,1)} %copy-done.14, bf16[2,128,1280]{2,1,0:T(8,128)(2,1)} %copy-done.17, ...), custom_call_target="tpu_custom_call" | custom-call | tf_op jit(solution)/shard_map/pick/pallas_call | solution.py:103
  56.2 0.2 collective-permute-start.3
  56.4 0.4 collective-permute-start.6
  56.8 1.8 %collective-permute-start.7 = (bf16[2,128,1280]{2,1,0:T(8,128)(2,1)S(1)}, bf16[2,128,1280]{2,1,0:T(8,128)(2,1)S(1)}, u32[]{:S(2)}, u32[]{:S(2)}) collective-permute-start(bf16[2,128,1280]{2,1,0:T(8,128)(2,1)S(1)} %broadcast_multiply_fusion.refs_2_), channel_id=1, source_target_pairs={{0,8},{1,9},{2,10},{3,11},{4,12},{5,13},{6,14},{7,15},{8,0},{9,1},... | collective-permute-start | bytes 1966088 | tf_op jit(solution)/shard_map/ppermute | solution.py:161
  58.6 1.1 collective-permute-start.8
  59.7 1.6 collective-permute-start.4
  61.3 11.5 %collective-permute-done.6.refs_3_ = bf16[2,128,1280]{2,1,0:T(8,128)(2,1)S(1)} collective-permute-done((bf16[2,128,1280]{2,1,0:T(8,128)(2,1)S(1)}, bf16[2,128,1280]{2,1,0:T(8,128)(2,1)S(1)}, u32[]{:S(2)}, u32[]{:S(2)}) %collective-permute-start.6) | collective-permute-done | bytes 655392 | tf_op jit(solution)/shard_map/ppermute | solution.py:161
  72.8 4.2 %collective-permute-start.5 = (bf16[4,128,1280]{2,1,0:T(8,128)(2,1)}, bf16[4,128,1280]{2,1,0:T(8,128)(2,1)}, u32[]{:S(2)}, u32[]{:S(2)}) collective-permute-start(bf16[4,128,1280]{2,1,0:T(8,128)(2,1)} %get-tuple-element.16), channel_id=1, source_target_pairs={{0,3},{1,0},{2,1},{3,2},{4,7},{5,4},{6,5},{7,6},{8,11},{9,8},{10,9... | collective-permute-start | bytes 3932168 | tf_op jit(solution)/shard_map/ppermute | solution.py:174
  77.0 8.5 %collective-permute-done.7.refs_4_ = bf16[2,128,1280]{2,1,0:T(8,128)(2,1)S(1)} collective-permute-done((bf16[2,128,1280]{2,1,0:T(8,128)(2,1)S(1)}, bf16[2,128,1280]{2,1,0:T(8,128)(2,1)S(1)}, u32[]{:S(2)}, u32[]{:S(2)}) %collective-permute-start.7) | collective-permute-done | bytes 655392 | tf_op jit(solution)/shard_map/ppermute | solution.py:161
  85.6 0.8 copy-done.21
  86.4 4.4 %pick.3 = (bf16[4,128,1280]{2,1,0:T(8,128)(2,1)}, bf16[4,128,1280]{2,1,0:T(8,128)(2,1)}, bf16[4,128,1280]{2,1,0:T(8,128)(2,1)}, bf16[4,128,1280]{2,1,0:T(8,128)(2,1)}) custom-call(s32[16,32]{1,0:T(8,128)} %bitcast.25, s32[6]{0:T(128)} %copy-done.4, bf16[2,128,1280]{2,1,0:T(8,128)(2,1)} %copy-done.15, bf16[2,128,1280]{2,1,0:T(8,128)(2,1)} %copy-done.20, ...), custom_call_target="tpu_custom_call" | custom-call | tf_op jit(solution)/shard_map/pick/pallas_call | solution.py:103
  90.8 0.1 collective-permute-start.9
  90.9 7.4 %collective-permute-start.10 = (bf16[4,128,1280]{2,1,0:T(8,128)(2,1)}, bf16[4,128,1280]{2,1,0:T(8,128)(2,1)S(1)}, u32[]{:S(2)}, u32[]{:S(2)}) collective-permute-start(bf16[4,128,1280]{2,1,0:T(8,128)(2,1)} %get-tuple-element.19), channel_id=1, source_target_pairs={{0,2},{1,3},{2,0},{3,1},{4,6},{5,7},{6,4},{7,5},{8,10},{9,11},{10,... | collective-permute-start | bytes 3932168 | tf_op jit(solution)/shard_map/ppermute | solution.py:174
  98.3 4.3 %collective-permute-done.3.refs_1_ = bf16[4,128,1280]{2,1,0:T(8,128)(2,1)S(1)} collective-permute-done((bf16[4,128,1280]{2,1,0:T(8,128)(2,1)}, bf16[4,128,1280]{2,1,0:T(8,128)(2,1)S(1)}, u32[]{:S(2)}, u32[]{:S(2)}) %collective-permute-start.3) | collective-permute-done | bytes 1310752 | tf_op jit(solution)/shard_map/ppermute | solution.py:174
  102.6 3.6 %collective-permute-done.5.refs_3_ = bf16[4,128,1280]{2,1,0:T(8,128)(2,1)} collective-permute-done((bf16[4,128,1280]{2,1,0:T(8,128)(2,1)}, bf16[4,128,1280]{2,1,0:T(8,128)(2,1)}, u32[]{:S(2)}, u32[]{:S(2)}) %collective-permute-start.5) | collective-permute-done | bytes 1310752 | tf_op jit(solution)/shard_map/ppermute | solution.py:174
  106.2 24.3 %collective-permute-done.9.refs_5_ = bf16[4,128,1280]{2,1,0:T(8,128)(2,1)S(1)} collective-permute-done((bf16[4,128,1280]{2,1,0:T(8,128)(2,1)}, bf16[4,128,1280]{2,1,0:T(8,128)(2,1)S(1)}, u32[]{:S(2)}, u32[]{:S(2)}) %collective-permute-start.9) | collective-permute-done | bytes 1310752 | tf_op jit(solution)/shard_map/ppermute | solution.py:174
  130.6 1.1 copy-done.8
  131.7 1.1 copy-done.10
  132.8 1.5 collective-permute-done.11.refs_7_
  134.3 1.1 copy-done.12
  135.4 1.3 copy-done.7
  136.7 1.3 copy-done.9
  138.0 1.3 copy-done.11
  139.3 1.3 copy-done.13
  140.6 15.3 %ladder.1 = f32[1024,1280]{1,0:T(8,128)} custom-call(s32[6]{0:T(128)S(1)} %copy-done.5, bf16[2,1024,2048]{2,1,0:T(8,128)(2,1)} %all-reduce.2.cloned.1.call-done.panel_ref, bf16[4,128,1280]{2,1,0:T(8,128)(2,1)S(1)} %copy-done.6, bf16[4,128,1280]{2,1,0:T(8,128)(2,1)S(1)} %collective-permute-done.3.refs_1_, ...), custom_call_target="tpu_custom_call" | custom-call | flops 10737418240 | bytes 25165824 | tf_op jit(solution)/shard_map/ladder/pallas_call | solution.py:134
  (51 shorter events, 0.3 us)
Async XLA Ops:
  6.5 128.8 %all-reduce.2.cloned.1.call-start = ((), (), s32[]{:S(2)}) async-start(), calls=%async_computation.2 | async-start | bytes 16777216 | tf_op jit(solution)/shard_map/psum | solution.py:154
  7.3 3.4 %copy-start = (bf16[1024,4096]{1,0:T(8,128)(2,1)S(1)}, bf16[1024,4096]{1,0:T(8,128)(2,1)}, u32[]{:S(2)}) copy-start(bf16[1024,4096]{1,0:T(8,128)(2,1)} %refs_1_.1) | copy-start | bytes 25165828
  10.7 0.7 copy-start.2
  11.3 5.4 %copy-start.4 = (s32[6]{0:T(128)}, s32[6]{0:T(128)S(1)}, u32[]{:S(2)}) copy-start(s32[6]{0:T(128)S(1)} %stack.19.info_ref.refs_1_) | copy-start | bytes 76
  16.8 3.3 %copy-start.1 = (bf16[2,1024,2048]{2,1,0:T(8,128)(2,1)}, bf16[2,1024,2048]{2,1,0:T(8,128)(2,1)S(1)}, u32[]{:S(2)}) copy-start(bf16[2,1024,2048]{2,1,0:T(8,128)(2,1)S(1)} %compress.1) | copy-start | bytes 25165828
  20.0 0.7 copy-start.22
  20.0 1.3 copy-start.16
  21.4 5.8 %copy-start.3 = (s32[8,32]{1,0:T(8,128)S(1)}, s32[8,32]{1,0:T(8,128)}, u32[]{:S(2)}) copy-start(s32[8,32]{1,0:T(8,128)} %mask_ref.1) | copy-start | bytes 3076
  21.5 13.5 %copy-start.23 = (s32[2]{0:T(128)S(1)}, s32[2]{0:T(128)}, u32[]{:S(2)}) copy-start(s32[2]{0:T(128)} %param.9) | copy-start | bytes 28
  21.5 29.2 %copy-start.14 = (bf16[2,128,1280]{2,1,0:T(8,128)(2,1)}, bf16[2,128,1280]{2,1,0:T(8,128)(2,1)S(1)}, u32[]{:S(2)}) copy-start(bf16[2,128,1280]{2,1,0:T(8,128)(2,1)S(1)} %broadcast_multiply_fusion.1.refs_2_) | copy-start | bytes 1966084
  21.5 29.1 %collective-permute-start = (bf16[2,128,1280]{2,1,0:T(8,128)(2,1)S(1)}, bf16[2,128,1280]{2,1,0:T(8,128)(2,1)S(1)}, u32[]{:S(2)}, u32[]{:S(2)}) collective-permute-start(bf16[2,128,1280]{2,1,0:T(8,128)(2,1)S(1)} %broadcast_multiply_fusion.1.refs_2_), channel_id=1, source_target_pairs={{0,4},{1,5},{2,6},{3,7},{4,8},{5,9},{6,10},{7,11},{8,12},{9,13},{1... | collective-permute-start | bytes 1966088 | tf_op jit(solution)/shard_map/ppermute | solution.py:161
  23.7 27.0 %collective-permute-start.1 = (bf16[2,128,1280]{2,1,0:T(8,128)(2,1)S(1)}, bf16[2,128,1280]{2,1,0:T(8,128)(2,1)S(1)}, u32[]{:S(2)}, u32[]{:S(2)}) collective-permute-start(bf16[2,128,1280]{2,1,0:T(8,128)(2,1)S(1)} %broadcast_multiply_fusion.1.refs_2_), channel_id=1, source_target_pairs={{0,8},{1,9},{2,10},{3,11},{4,12},{5,13},{6,14},{7,15},{8,0},{9,1},... | collective-permute-start | bytes 1966088 | tf_op jit(solution)/shard_map/ppermute | solution.py:161
  26.1 24.6 %collective-permute-start.2 = (bf16[2,128,1280]{2,1,0:T(8,128)(2,1)S(1)}, bf16[2,128,1280]{2,1,0:T(8,128)(2,1)S(1)}, u32[]{:S(2)}, u32[]{:S(2)}) collective-permute-start(bf16[2,128,1280]{2,1,0:T(8,128)(2,1)S(1)} %broadcast_multiply_fusion.1.refs_2_), channel_id=1, source_target_pairs={{0,12},{1,13},{2,14},{3,15},{4,0},{5,1},{6,2},{7,3},{8,4},{9,5},{1... | collective-permute-start | bytes 1966088 | tf_op jit(solution)/shard_map/ppermute | solution.py:161
  28.2 11.6 %all-to-all-start = ((s32[8,1,16]{2,1,0:T(1,128)}), s32[8,1,16]{2,1,0:T(1,128)S(1)}, u32[]{:S(2)}, u32[]{:S(2)}) async-start(s32[8,1,16]{2,1,0:T(1,128)} %broadcast_in_dim.42), calls=%async_computation | async-start | bytes 8192 | tf_op jit(solution)/shard_map/all_to_all | solution.py:166
  50.7 0.9 copy-start.17
  50.7 1.1 copy-start.18
  50.7 1.3 copy-start.19
  56.2 46.4 %collective-permute-start.3 = (bf16[4,128,1280]{2,1,0:T(8,128)(2,1)}, bf16[4,128,1280]{2,1,0:T(8,128)(2,1)S(1)}, u32[]{:S(2)}, u32[]{:S(2)}) collective-permute-start(bf16[4,128,1280]{2,1,0:T(8,128)(2,1)} %get-tuple-element.14), channel_id=1, source_target_pairs={{0,1},{1,2},{2,3},{3,0},{4,5},{5,6},{6,7},{7,4},{8,9},{9,10},{10,1... | collective-permute-start | bytes 3932168 | tf_op jit(solution)/shard_map/ppermute | solution.py:174
  56.4 30.0 %copy-start.15 = (bf16[2,128,1280]{2,1,0:T(8,128)(2,1)}, bf16[2,128,1280]{2,1,0:T(8,128)(2,1)S(1)}, u32[]{:S(2)}) copy-start(bf16[2,128,1280]{2,1,0:T(8,128)(2,1)S(1)} %broadcast_multiply_fusion.refs_2_) | copy-start | bytes 1966084
  56.4 16.4 %collective-permute-start.6 = (bf16[2,128,1280]{2,1,0:T(8,128)(2,1)S(1)}, bf16[2,128,1280]{2,1,0:T(8,128)(2,1)S(1)}, u32[]{:S(2)}, u32[]{:S(2)}) collective-permute-start(bf16[2,128,1280]{2,1,0:T(8,128)(2,1)S(1)} %broadcast_multiply_fusion.refs_2_), channel_id=1, source_target_pairs={{0,4},{1,5},{2,6},{3,7},{4,8},{5,9},{6,10},{7,11},{8,12},{9,13},{1... | collective-permute-start | bytes 1966088 | tf_op jit(solution)/shard_map/ppermute | solution.py:161
  56.8 28.7 %collective-permute-start.7 = (bf16[2,128,1280]{2,1,0:T(8,128)(2,1)S(1)}, bf16[2,128,1280]{2,1,0:T(8,128)(2,1)S(1)}, u32[]{:S(2)}, u32[]{:S(2)}) collective-permute-start(bf16[2,128,1280]{2,1,0:T(8,128)(2,1)S(1)} %broadcast_multiply_fusion.refs_2_), channel_id=1, source_target_pairs={{0,8},{1,9},{2,10},{3,11},{4,12},{5,13},{6,14},{7,15},{8,0},{9,1},... | collective-permute-start | bytes 1966088 | tf_op jit(solution)/shard_map/ppermute | solution.py:161
  58.6 27.8 %collective-permute-start.8 = (bf16[2,128,1280]{2,1,0:T(8,128)(2,1)S(1)}, bf16[2,128,1280]{2,1,0:T(8,128)(2,1)}, u32[]{:S(2)}, u32[]{:S(2)}) collective-permute-start(bf16[2,128,1280]{2,1,0:T(8,128)(2,1)S(1)} %broadcast_multiply_fusion.refs_2_), channel_id=1, source_target_pairs={{0,12},{1,13},{2,14},{3,15},{4,0},{5,1},{6,2},{7,3},{8,4},{9,5},{1... | collective-permute-start | bytes 1966088 | tf_op jit(solution)/shard_map/ppermute | solution.py:161
  59.7 42.9 %collective-permute-start.4 = (bf16[4,128,1280]{2,1,0:T(8,128)(2,1)}, bf16[4,128,1280]{2,1,0:T(8,128)(2,1)}, u32[]{:S(2)}, u32[]{:S(2)}) collective-permute-start(bf16[4,128,1280]{2,1,0:T(8,128)(2,1)} %get-tuple-element.15), channel_id=1, source_target_pairs={{0,2},{1,3},{2,0},{3,1},{4,6},{5,7},{6,4},{7,5},{8,10},{9,11},{10,... | collective-permute-start | bytes 3932168 | tf_op jit(solution)/shard_map/ppermute | solution.py:174
  72.8 12.8 %copy-start.20 = (bf16[2,128,1280]{2,1,0:T(8,128)(2,1)}, bf16[2,128,1280]{2,1,0:T(8,128)(2,1)S(1)}, u32[]{:S(2)}) copy-start(bf16[2,128,1280]{2,1,0:T(8,128)(2,1)S(1)} %collective-permute-done.6.refs_3_) | copy-start | bytes 1966084
  72.8 62.5 %copy-start.5 = (s32[6]{0:T(128)S(1)}, s32[6]{0:T(128)}, u32[]{:S(2)}) copy-start(s32[6]{0:T(128)} %copy-done.4) | copy-start | bytes 76
  72.8 62.5 %copy-start.6 = (bf16[4,128,1280]{2,1,0:T(8,128)(2,1)S(1)}, bf16[4,128,1280]{2,1,0:T(8,128)(2,1)}, u32[]{:S(2)}) copy-start(bf16[4,128,1280]{2,1,0:T(8,128)(2,1)} %get-tuple-element.13.refs_0_) | copy-start | bytes 3932164
  72.8 33.4 %collective-permute-start.5 = (bf16[4,128,1280]{2,1,0:T(8,128)(2,1)}, bf16[4,128,1280]{2,1,0:T(8,128)(2,1)}, u32[]{:S(2)}, u32[]{:S(2)}) collective-permute-start(bf16[4,128,1280]{2,1,0:T(8,128)(2,1)} %get-tuple-element.16), channel_id=1, source_target_pairs={{0,3},{1,0},{2,1},{3,2},{4,7},{5,4},{6,5},{7,6},{8,11},{9,8},{10,9... | collective-permute-start | bytes 3932168 | tf_op jit(solution)/shard_map/ppermute | solution.py:174
  85.6 0.8 copy-start.21
  90.8 39.8 %collective-permute-start.9 = (bf16[4,128,1280]{2,1,0:T(8,128)(2,1)}, bf16[4,128,1280]{2,1,0:T(8,128)(2,1)S(1)}, u32[]{:S(2)}, u32[]{:S(2)}) collective-permute-start(bf16[4,128,1280]{2,1,0:T(8,128)(2,1)} %get-tuple-element.18), channel_id=1, source_target_pairs={{0,1},{1,2},{2,3},{3,0},{4,5},{5,6},{6,7},{7,4},{8,9},{9,10},{10,1... | collective-permute-start | bytes 3932168 | tf_op jit(solution)/shard_map/ppermute | solution.py:174
  90.9 40.8 %collective-permute-start.10 = (bf16[4,128,1280]{2,1,0:T(8,128)(2,1)}, bf16[4,128,1280]{2,1,0:T(8,128)(2,1)S(1)}, u32[]{:S(2)}, u32[]{:S(2)}) collective-permute-start(bf16[4,128,1280]{2,1,0:T(8,128)(2,1)} %get-tuple-element.19), channel_id=1, source_target_pairs={{0,2},{1,3},{2,0},{3,1},{4,6},{5,7},{6,4},{7,5},{8,10},{9,11},{10,... | collective-permute-start | bytes 3932168 | tf_op jit(solution)/shard_map/ppermute | solution.py:174
  102.6 31.7 %collective-permute-start.11 = (bf16[4,128,1280]{2,1,0:T(8,128)(2,1)}, bf16[4,128,1280]{2,1,0:T(8,128)(2,1)S(1)}, u32[]{:S(2)}, u32[]{:S(2)}) collective-permute-start(bf16[4,128,1280]{2,1,0:T(8,128)(2,1)} %get-tuple-element.20), channel_id=1, source_target_pairs={{0,3},{1,0},{2,1},{3,2},{4,7},{5,4},{6,5},{7,6},{8,11},{9,8},{10,9... | collective-permute-start | bytes 3932168 | tf_op jit(solution)/shard_map/ppermute | solution.py:174
  130.6 1.1 copy-start.8
  131.7 1.1 copy-start.10
  134.3 1.1 copy-start.12
  135.3 1.3 copy-start.7
  136.7 1.3 copy-start.9
  138.0 1.3 copy-start.11
  139.3 1.3 copy-start.13
Sparse Core Ops, SparseCore 0:
  20.2 107.0 all-reduce.1

commit v3 on v2

v3 whole, which is shorter than its diff:
```python
import functools

import jax
import jax.numpy as jnp
from jax import lax
from jax.experimental import pallas as pl
from jax.experimental.pallas import tpu as pltpu
from jax.sharding import Mesh
from jax.sharding import PartitionSpec as P

TW = 128
PART = 256
STEPS = 2
RING = 4
ROWS = 8
ROW = ("y", "core")
COL = ("z", "x")
GRID = ("core", "z", "x")


def plane_perm(first, shift):
    pairs = []
    for core in range(2):
        for z in range(RING):
            for x in range(RING):
                along_z = (core == 0) == first
                to_z, to_x = ((z + shift) % RING, x) if along_z else (z, (x + shift) % RING)
                pairs.append((core * 16 + z * RING + x, core * 16 + to_z * RING + to_x))
    return pairs


def wrap(value):
    return lax.rem(value + 2 * RING, RING)


def origin(core, z, x, first_shift, second_shift):
    on_zero = wrap(z - first_shift) * RING + wrap(x - second_shift)
    on_one = wrap(z - second_shift) * RING + wrap(x - first_shift)
    return jnp.where(core == 0, on_zero, on_one)


def needed_tile(mask_ref, group):
    found = mask_ref[0, 2 * group + 1]
    for row in range(1, 8):
        found = found | mask_ref[row, 2 * group + 1]
    return jnp.where(found != 0, 1, 0)


def compress_kernel(mask_ref, info_ref, after_ref, amp_ref, panel_ref, *refs):
    panels = [panel_ref.at[step] for step in range(STEPS)]
    (held, blank, in_sems, out_sems, blank_sems) = refs
    groups, rows, _ = held.shape
    row = info_ref[2]
    mine = [info_ref[step] == row for step in range(STEPS)]
    some = functools.reduce(jnp.logical_or, mine)
    loads, columns = [], []
    for group in range(groups):
        column = 2 * group + needed_tile(mask_ref, group)
        columns.append(column)
        loads.append(pltpu.make_async_copy(
            amp_ref.at[:, pl.ds(pl.multiple_of(column * TW, TW), TW)], held.at[group], in_sems.at[group]))

    @pl.when(some)
    def _():
        for load in loads:
            load.start()

    blank[...] = jnp.zeros_like(blank)
    for step in range(STEPS):
        @pl.when(jnp.logical_not(mine[step]))
        def _():
            for group in range(groups):
                pltpu.make_async_copy(blank, panels[step].at[group], blank_sems.at[step, group]).start()

    @pl.when(some)
    def _():
        for group, load in enumerate(loads):
            load.wait()
            for tile in range(rows // TW):
                span = slice(tile * TW, (tile + 1) * TW)

                @pl.when(mask_ref[tile, columns[group]] == 0)
                def _():
                    held[group, span, :] = jnp.zeros((TW, TW), held.dtype)
            for step in range(STEPS):
                @pl.when(mine[step])
                def _():
                    pltpu.make_async_copy(held.at[group], panels[step].at[group], out_sems.at[group]).start()
        for group in range(groups):
            pltpu.make_async_copy(held.at[group], panels[0].at[group], out_sems.at[group]).wait()

    for step in range(STEPS):
        @pl.when(jnp.logical_not(mine[step]))
        def _():
            for group in range(groups):
                pltpu.make_async_copy(blank, panels[step].at[group], blank_sems.at[step, group]).wait()


def compress(amplitudes, amp_mask, info, after):
    rows, groups = amplitudes.shape[0], amp_mask.shape[1] // 2
    return pl.pallas_call(
        compress_kernel,
        in_specs=[pl.BlockSpec(memory_space=pltpu.SMEM)] * 2 + [pl.BlockSpec(memory_space=pl.ANY)] * 2,
        out_specs=pl.BlockSpec(memory_space=pl.ANY),
        out_shape=jax.ShapeDtypeStruct((STEPS, groups, rows, TW), amplitudes.dtype),
        scratch_shapes=[pltpu.VMEM((groups, rows, TW), amplitudes.dtype),
                        pltpu.VMEM((rows, TW), amplitudes.dtype),
                        pltpu.SemaphoreType.DMA((groups,)), pltpu.SemaphoreType.DMA((groups,)),
                        pltpu.SemaphoreType.DMA((STEPS, groups))],
        compiler_params=pltpu.CompilerParams(vmem_limit_bytes=60 << 20),
        name="compress",
    )(amp_mask, info, after, amplitudes)


def pick_kernel(needs_ref, info_ref, *refs):
    held, sent, sems = refs[:RING], refs[RING:2 * RING - 1], refs[2 * RING - 1]
    core, z, x = info_ref[3], info_ref[4], info_ref[5]
    copies = []
    for second in range(1, RING):
        reader = origin(core, z, x, 0, -second)
        for step in range(STEPS):
            for first in range(RING):
                group = origin(core, z, x, first, 0)
                tile = needs_ref[reader, step * 16 + group]
                copies.append(pltpu.make_async_copy(
                    held[first].at[step, tile], sent[second - 1].at[step, first], sems.at[len(copies)]))
                copies[-1].start()
    for copy in copies:
        copy.wait()


def pick(needs, info, held):
    steps, _, rows, width = held[0].shape
    shape = jax.ShapeDtypeStruct((steps, RING, rows, width), held[0].dtype)
    return pl.pallas_call(
        pick_kernel,
        in_specs=[pl.BlockSpec(memory_space=pltpu.SMEM)] * 2 + [pl.BlockSpec(memory_space=pltpu.VMEM)] * RING,
        out_specs=[pl.BlockSpec(memory_space=pl.ANY)] * (RING - 1),
        out_shape=[shape] * (RING - 1),
        scratch_shapes=[pltpu.SemaphoreType.DMA((steps * (RING - 1) * RING,))],
        compiler_params=pltpu.CompilerParams(vmem_limit_bytes=8 << 20),
        name="pick",
    )(needs, info, *held)


def ladder_kernel(needs_ref, info_ref, panel_ref, *refs):
    held, blocks, (out_ref, lefts, rights, total, left_sems, right_sems, out_sems) = (
        refs[:RING], refs[RING:2 * RING - 1], refs[2 * RING - 1:])
    core, z, x = info_ref[3], info_ref[4], info_ref[5]
    me = z * RING + x
    parts = total.shape[0]
    rows = total.shape[1]
    loads = []
    for step in range(STEPS):
        for second in range(RING):
            slot = len(loads)
            loads.append([])
            for first in range(RING):
                if second == 0:
                    tile = needs_ref[me, step * 16 + origin(core, z, x, first, 0)]
                    source = held[first].at[step, tile]
                else:
                    source = blocks[second - 1].at[step, first]
                group = origin(core, z, x, first, second)
                loads[slot].append(pltpu.make_async_copy(
                    panel_ref.at[step, group], lefts.at[step, :, pl.ds((second * RING + first) * TW, TW)], left_sems.at[slot, first]))
                loads[slot].append(pltpu.make_async_copy(
                    source, rights.at[step, pl.ds((second * RING + first) * TW, TW)], right_sems.at[slot, first]))
            for load in loads[slot]:
                load.start()
    for start, stop in ((0, 1), (1, RING), (RING, STEPS * RING)):
        for slot_loads in loads[start:stop]:
            for load in slot_loads:
                load.wait()

        @pl.loop(0, parts)
        def _(part):
            span = pl.ds(pl.multiple_of(part * PART, PART), PART)
            step, skip = start // RING, start % RING
            depth = slice(skip * RING * TW, (skip + stop - start) * RING * TW)
            product = jnp.dot(lefts[step, :, depth], rights[step, depth, span], preferred_element_type=jnp.float32)
            total[part] = product if start == 0 else total[part] + product
            if stop == len(loads):
                pltpu.make_async_copy(total.at[part], out_ref.at[:, span], out_sems.at[part]).start()

    for part in range(parts):
        pltpu.make_async_copy(total.at[part], out_ref.at[:, pl.ds(part * PART, PART)], out_sems.at[part]).wait()


def multiply(needs, info, panels, held, blocks):
    steps, groups, rows, _ = panels.shape
    depth, width = groups * TW, held[0].shape[-1]
    slots = steps * RING
    return pl.pallas_call(
        ladder_kernel,
        in_specs=[pl.BlockSpec(memory_space=pltpu.SMEM)] * 2 + [pl.BlockSpec(memory_space=pl.ANY)] * (2 * RING),
        out_specs=pl.BlockSpec(memory_space=pl.ANY),
        out_shape=jax.ShapeDtypeStruct((rows, width), jnp.float32),
        scratch_shapes=[pltpu.VMEM((steps, rows, groups * TW), panels.dtype),
                        pltpu.VMEM((steps, groups * TW, width), panels.dtype),
                        pltpu.VMEM((width // PART, rows, PART), jnp.float32),
                        pltpu.SemaphoreType.DMA((slots, RING)),
                        pltpu.SemaphoreType.DMA((slots, RING)),
                        pltpu.SemaphoreType.DMA((width // PART,))],
        compiler_params=pltpu.CompilerParams(vmem_limit_bytes=60 << 20),
        cost_estimate=pl.CostEstimate(flops=2 * rows * steps * depth * width, bytes_accessed=24 << 20, transcendentals=0),
        name="ladder",
    )(needs, info, panels, *held, *blocks)


def local(amplitudes, amp_mask, integrals, int_mask, steps):
    tiles, ab_width = integrals.shape[1] // TW, integrals.shape[2]
    row = lax.axis_index(ROW)
    core, z, x = (lax.axis_index(axis) for axis in GRID)
    info = jnp.stack([steps[0], steps[1], row, core, z, x]).astype(jnp.int32)

    gate = int_mask.astype(integrals.dtype)[:, :, None, :, None]
    block = integrals.reshape(STEPS, tiles, TW, ab_width // TW, TW) * gate
    block = block.reshape(STEPS, tiles, TW, ab_width)
    held = [block] + [lax.ppermute(block, GRID, plane_perm(True, shift)) for shift in (1, 2, 3)]

    panels = lax.psum(compress(amplitudes, amp_mask, info, block), ROW)

    own = jnp.max(amp_mask, axis=0).reshape(-1, 2)[:, 1]
    groups = own.shape[0]
    by_row = lax.all_to_all(jnp.broadcast_to(own, (8, groups)), ROW, 0, 0, tiled=True)
    chosen = jnp.sum(jnp.where((steps[:, None] == jnp.arange(8))[:, :, None], by_row[None], 0), axis=1)
    needs = lax.all_to_all(
        jnp.broadcast_to(chosen.reshape(1, -1), (16, STEPS * groups)), COL, 0, 0, tiled=True)

    sent = pick(needs, info, held)
    blocks = [lax.ppermute(sent[shift - 1], GRID, plane_perm(False, shift)) for shift in (1, 2, 3)]
    return multiply(needs, info, panels, held, blocks)


def solution(mesh):
    grid = Mesh(mesh.devices.reshape(4, 2, 4, 4), ("y", "core", "z", "x"))
    return jax.shard_map(
        local,
        mesh=grid,
        in_specs=(P(COL, ROW), P(COL, ROW), P(None, COL, ROW), P(None, COL, ROW), P()),
        out_specs=P(COL, ROW),
        check_vma=False,
    )
```

time: 166 us -> 149 us (0.90); the launches traced: 163 us -> 148 us
  local copies, waits for them, and re-layouts: 21.1 us -> 4.49 us
  starting transfers between devices: 29.3 us -> 16.6 us
  blocking collectives: 10.7 us -> 18.1 us
  waiting for transfers between devices: 58.5 us -> 64.4 us
  other arithmetic: 0.28 us -> 3.42 us
  Pallas kernels: 29.3 us -> 27.6 us
    ppermute x6 -> x3, waiting for transfers between devices: 33.8 us -> 56.9 us  [local(): lax.ppermute(sent[shift - 1], GRID, plane_perm(False, shift))]
    ppermute x6 -> x3, waiting for transfers between devices: 20 us -> 0.01 us  [local(): lax.ppermute(block, GRID, plane_perm(True, shift))]
    unnamed x51 -> x16, local copies, waits for them, and re-layouts: 19.3 us -> 2.82 us
    ppermute x6 -> x3, starting transfers between devices: 13.6 us -> 3.36 us  [local(): lax.ppermute(sent[shift - 1], GRID, plane_perm(False, shift))]
    all_to_all x1, blocking collectives: 10.7 us -> 18.1 us  [local(): lax.all_to_all(jnp.broadcast_to(chosen.reshape(1, -1), (16, STEPS * group...]
    ppermute x6 -> x3, starting transfers between devices: 8.94 us -> 5.64 us  [local(): lax.ppermute(block, GRID, plane_perm(True, shift))]
    psum x1, waiting for transfers between devices: 0.01 us -> 2.94 us  [local(): panels = lax.psum(compress(amplitudes, amp_mask, info, block), ROW)]
    mul x2 -> x1, other arithmetic: 0.1 us -> 2.54 us  [local(): block = integrals.reshape(STEPS, tiles, TW, ab_width // TW, TW) * gate]
  transfers between devices with their start and end apart: 14 -> 8, of which waited for: 7 -> 3; matrix products, arithmetic and copies ran while one was open for 1% -> 1% of each run, Pallas kernels for 5% -> 4%
where the time goes in v3:
time: 149 us; the launch traced here: 148 us
  waiting for transfers between devices  64.4 us (43%)
  Pallas kernels  27.6 us (19%)
  blocking collectives  18.1 us (12%)
  starting transfers between devices  16.6 us (11%)
  between operations  13.5 us (9%)
  local copies, waits for them, and re-layouts  4.49 us (3%)
  other arithmetic  3.42 us (2%)
    ppermute x3, waiting for transfers between devices, local(): lax.ppermute(sent[shift - 1], GRID, plane_perm(False, shift))  56.9 us
    all_to_all x1, blocking collectives, local(): lax.all_to_all(jnp.broadcast_to(chosen.reshape(1, -1), (16, STEPS * group...  18.1 us
    pallas_call x1, Pallas kernels, multiply(): pl.pallas_call(ladder_kernel, in_specs=[pl.BlockSpec(memory_space=pltpu.S...  17.6 us
    all_to_all x1, starting transfers between devices, local(): lax.all_to_all(jnp.broadcast_to(own, (8, groups)), ROW, 0, 0, tiled=True)  7.58 us
    ppermute x3, starting transfers between devices, local(): lax.ppermute(block, GRID, plane_perm(True, shift))  5.64 us
    pallas_call x1, Pallas kernels, pick(): pl.pallas_call(pick_kernel, in_specs=[pl.BlockSpec(memory_space=pltpu.SME...  5.4 us
    pallas_call x1, Pallas kernels, compress(): pl.pallas_call(compress_kernel, in_specs=[pl.BlockSpec(memory_space=pltpu...  4.57 us
    all_to_all x1, waiting for transfers between devices, local(): lax.all_to_all(jnp.broadcast_to(own, (8, groups)), ROW, 0, 0, tiled=True)  4.56 us
  transfers between devices with their start and end apart: 8, of which 3 were waited for; matrix products, arithmetic and copies ran while one was open for 1% of the time, Pallas kernels for 4%

profile of v3, /device:TPU:1, one launch (start us, length us, event | category | flops | bytes accessed | tf_op | source)
XLA Modules:
  0.0 148.2 jit_solution(10660667324574206020)
XLA Ops:
  6.5 0.0 copy-start.5
  6.5 0.0 all-reduce.2.cloned.1.call-start
  6.5 0.7 convert_element_type.3
  7.2 0.1 mul.17
  7.3 2.5 %broadcast_multiply_fusion.after_ref.refs_0_ = bf16[2,2,128,1280]{3,2,1,0:T(8,128)(2,1)} fusion(bf16[2,2,128,1280]{3,2,1,0:T(8,128)(2,1)} %bitcast.9, bf16[2,2,1280]{2,1,0:T(2,128)(2,1)S(1)} %mul.18), kind=kLoop, calls=%fused_computation | loop fusion | flops 655360 | bytes 2631680 | tf_op jit(solution)/shard_map/mul | solution.py:218
  9.9 0.0 copy-done.5
  9.9 0.6 stack.19.info_ref
  10.5 4.6 %compress.1 = bf16[2,16,1024,128]{3,2,1,0:T(8,128)(2,1)} custom-call(s32[8,32]{1,0:T(8,128)} %mask_ref.1, s32[6]{0:T(128)} %stack.19.info_ref, bf16[2,2,128,1280]{3,2,1,0:T(8,128)(2,1)} %broadcast_multiply_fusion.after_ref.refs_0_, bf16[1024,4096]{1,0:T(8,128)(2,1)} %amp_ref.1), custom_call_target="tpu_custom_call" | custom-call | tf_op jit(solution)/shard_map/compress/pallas_call | solution.py:101
  15.1 0.0 copy-start
  15.1 0.0 copy-start.4
  15.1 0.0 copy-start.3
  15.1 0.0 all-reduce.2.cloned.1.call-update
  15.1 1.3 copy-done
  16.4 2.0 %collective-permute-start = (bf16[2,2,128,1280]{3,2,1,0:T(8,128)(2,1)S(1)}, bf16[2,2,128,1280]{3,2,1,0:T(8,128)(2,1)S(1)}, u32[]{:S(2)}, u32[]{:S(2)}) collective-permute-start(bf16[2,2,128,1280]{3,2,1,0:T(8,128)(2,1)S(1)} %copy-done), channel_id=1, source_target_pairs={{0,4},{1,5},{2,6},{3,7},{4,8},{5,9},{6,10},{7,11},{8,12},{9,13},{1... | collective-permute-start | bytes 3932168 | tf_op jit(solution)/shard_map/ppermute | solution.py:220
  18.4 2.5 %collective-permute-start.1 = (bf16[2,2,128,1280]{3,2,1,0:T(8,128)(2,1)S(1)}, bf16[2,2,128,1280]{3,2,1,0:T(8,128)(2,1)}, u32[]{:S(2)}, u32[]{:S(2)}) collective-permute-start(bf16[2,2,128,1280]{3,2,1,0:T(8,128)(2,1)S(1)} %copy-done), channel_id=1, source_target_pairs={{0,8},{1,9},{2,10},{3,11},{4,12},{5,13},{6,14},{7,15},{8,0},{9,1},... | collective-permute-start | bytes 3932168 | tf_op jit(solution)/shard_map/ppermute | solution.py:220
  20.9 1.2 collective-permute-start.2
  22.0 0.0 copy-done.4
  22.1 0.1 reshape.49
  22.1 0.2 slice_reduce_fusion
  22.3 0.6 broadcast_in_dim.41
  22.9 7.6 %all-to-all-start = ((s32[8,1,16]{2,1,0:T(1,128)}), s32[8,1,16]{2,1,0:T(1,128)S(1)}, u32[]{:S(2)}, u32[]{:S(2)}) async-start(s32[8,1,16]{2,1,0:T(1,128)} %broadcast_in_dim.41), calls=%async_computation | async-start | bytes 8192 | tf_op jit(solution)/shard_map/all_to_all | solution.py:226
  30.5 0.1 iota_compare_fusion
  30.6 4.6 %all-to-all-done = s32[8,1,16]{2,1,0:T(1,128)S(1)} async-done(((s32[8,1,16]{2,1,0:T(1,128)}), s32[8,1,16]{2,1,0:T(1,128)S(1)}, u32[]{:S(2)}, u32[]{:S(2)}) %all-to-all-start) | async-done | bytes 544 | tf_op jit(solution)/shard_map/all_to_all | solution.py:226
  35.1 0.1 select_reduce_fusion
  35.2 0.1 broadcast_in_dim.45
  35.3 18.1 %all_to_all.14 = s32[16,1,32]{2,1,0:T(1,128)S(1)} all-to-all(s32[16,1,32]{2,1,0:T(1,128)S(1)} %broadcast_in_dim.46), channel_id=1, replica_groups=mesh['y'=4,'core'=2,'z'=4,'x'=4] {'z','x'}, dimensions={0} | all-to-all | bytes 4096 | tf_op jit(solution)/shard_map/all_to_all | solution.py:228
  53.5 0.0 copy-start.2
  53.5 0.0 collective-permute-done.refs_1_
  53.5 0.0 copy-start.1
  53.5 0.0 collective-permute-done.1.refs_2_
  53.5 0.0 collective-permute-done.2.refs_3_
  53.5 0.0 copy-done.3
  53.5 5.4 %pick.1 = (bf16[2,4,128,1280]{3,2,1,0:T(8,128)(2,1)S(1)}, bf16[2,4,128,1280]{3,2,1,0:T(8,128)(2,1)S(1)}, bf16[2,4,128,1280]{3,2,1,0:T(8,128)(2,1)S(1)}) custom-call(s32[16,32]{1,0:T(8,128)S(1)} %bitcast.7, s32[6]{0:T(128)S(1)} %copy-done.3, bf16[2,2,128,1280]{3,2,1,0:T(8,128)(2,1)S(1)} %copy-done, ...), custom_call_target="tpu_custom_call" | custom-call | tf_op jit(solution)/shard_map/pick/pallas_call | solution.py:135
  58.9 0.0 copy-done.2
  58.9 0.0 copy-done.1
  58.9 0.6 collective-permute-start.3
  59.6 1.0 collective-permute-start.4
  60.6 1.7 %collective-permute-start.5 = (bf16[2,4,128,1280]{3,2,1,0:T(8,128)(2,1)S(1)}, bf16[2,4,128,1280]{3,2,1,0:T(8,128)(2,1)}, u32[]{:S(2)}, u32[]{:S(2)}) collective-permute-start(bf16[2,4,128,1280]{3,2,1,0:T(8,128)(2,1)S(1)} %get-tuple-element.10), channel_id=1, source_target_pairs={{0,3},{1,0},{2,1},{3,2},{4,7},{5,4},{6,5},{7,6},{8,11},{9,8},{10,9... | collective-permute-start | bytes 7864328 | tf_op jit(solution)/shard_map/ppermute | solution.py:232
  62.3 56.9 %collective-permute-done.3.refs_4_ = bf16[2,4,128,1280]{3,2,1,0:T(8,128)(2,1)S(1)} collective-permute-done((bf16[2,4,128,1280]{3,2,1,0:T(8,128)(2,1)S(1)}, bf16[2,4,128,1280]{3,2,1,0:T(8,128)(2,1)S(1)}, u32[]{:S(2)}, u32[]{:S(2)}) %collective-permute-start.3) | collective-permute-done | bytes 2621472 | tf_op jit(solution)/shard_map/ppermute | solution.py:232
  119.2 0.0 copy-start.6
  119.2 0.0 collective-permute-done.4.refs_5_
  119.2 0.0 copy-start.7
  119.2 1.5 %copy-done.7 = bf16[2,4,128,1280]{3,2,1,0:T(8,128)(2,1)} copy-done((bf16[2,4,128,1280]{3,2,1,0:T(8,128)(2,1)}, bf16[2,4,128,1280]{3,2,1,0:T(8,128)(2,1)S(1)}, u32[]{:S(2)}) %copy-start.7) | copy-done | bytes 2621464
  120.7 0.0 collective-permute-done.5.refs_6_
  120.7 2.9 %all-reduce.2.cloned.1.call-done.panel_ref = bf16[2,16,1024,128]{3,2,1,0:T(8,128)(2,1)} async-done(((bf16[2,16,1024,128]{3,2,1,0:T(8,128)(2,1)}), bf16[2,16,1024,128]{3,2,1,0:T(8,128)(2,1)}) %all-reduce.2.cloned.1.call-update) | async-done | bytes 8388624 | tf_op jit(solution)/shard_map/psum | solution.py:222
  123.7 0.0 copy-done.6
  123.7 17.6 %ladder.1 = f32[1024,1280]{1,0:T(8,128)} custom-call(s32[16,32]{1,0:T(8,128)} %bitcast.8, s32[6]{0:T(128)} %stack.19.info_ref, bf16[2,16,1024,128]{3,2,1,0:T(8,128)(2,1)} %all-reduce.2.cloned.1.call-done.panel_ref, bf16[2,2,128,1280]{3,2,1,0:T(8,128)(2,1)} %broadcast_multiply_fusion.after_ref.refs_0_, bf16[2,2,128,1280]{3,2,1,0:T(8,128)(2,1)} %copy-done.1, ...), custom_call_target="tpu_custom_call" | custom-call | flops 10737418240 | bytes 25165824 | tf_op jit(solution)/shard_map/ladder/pallas_call | solution.py:194
  (3 shorter events, 0.0 us)
Async XLA Ops:
  6.5 3.3 %copy-start.5 = (s32[2]{0:T(128)S(1)}, s32[2]{0:T(128)}, u32[]{:S(2)}) copy-start(s32[2]{0:T(128)} %param.9) | copy-start | bytes 28
  6.5 117.1 %all-reduce.2.cloned.1.call-start = ((), (), s32[]{:S(2)}) async-start(), calls=%async_computation.2 | async-start | bytes 16777216 | tf_op jit(solution)/shard_map/psum | solution.py:222
  15.1 1.3 copy-start
  15.1 7.0 %copy-start.4 = (s32[8,32]{1,0:T(8,128)S(1)}, s32[8,32]{1,0:T(8,128)}, u32[]{:S(2)}) copy-start(s32[8,32]{1,0:T(8,128)} %mask_ref.1) | copy-start | bytes 3076
  15.1 38.4 %copy-start.3 = (s32[6]{0:T(128)S(1)}, s32[6]{0:T(128)}, u32[]{:S(2)}) copy-start(s32[6]{0:T(128)} %stack.19.info_ref) | copy-start | bytes 76
  16.4 37.1 %collective-permute-start = (bf16[2,2,128,1280]{3,2,1,0:T(8,128)(2,1)S(1)}, bf16[2,2,128,1280]{3,2,1,0:T(8,128)(2,1)S(1)}, u32[]{:S(2)}, u32[]{:S(2)}) collective-permute-start(bf16[2,2,128,1280]{3,2,1,0:T(8,128)(2,1)S(1)} %copy-done), channel_id=1, source_target_pairs={{0,4},{1,5},{2,6},{3,7},{4,8},{5,9},{6,10},{7,11},{8,12},{9,13},{1... | collective-permute-start | bytes 3932168 | tf_op jit(solution)/shard_map/ppermute | solution.py:220
  18.4 35.0 %collective-permute-start.1 = (bf16[2,2,128,1280]{3,2,1,0:T(8,128)(2,1)S(1)}, bf16[2,2,128,1280]{3,2,1,0:T(8,128)(2,1)}, u32[]{:S(2)}, u32[]{:S(2)}) collective-permute-start(bf16[2,2,128,1280]{3,2,1,0:T(8,128)(2,1)S(1)} %copy-done), channel_id=1, source_target_pairs={{0,8},{1,9},{2,10},{3,11},{4,12},{5,13},{6,14},{7,15},{8,0},{9,1},... | collective-permute-start | bytes 3932168 | tf_op jit(solution)/shard_map/ppermute | solution.py:220
  20.9 32.6 %collective-permute-start.2 = (bf16[2,2,128,1280]{3,2,1,0:T(8,128)(2,1)S(1)}, bf16[2,2,128,1280]{3,2,1,0:T(8,128)(2,1)}, u32[]{:S(2)}, u32[]{:S(2)}) collective-permute-start(bf16[2,2,128,1280]{3,2,1,0:T(8,128)(2,1)S(1)} %copy-done), channel_id=1, source_target_pairs={{0,12},{1,13},{2,14},{3,15},{4,0},{5,1},{6,2},{7,3},{8,4},{9,5},{1... | collective-permute-start | bytes 3932168 | tf_op jit(solution)/shard_map/ppermute | solution.py:220
  22.9 12.2 %all-to-all-start = ((s32[8,1,16]{2,1,0:T(1,128)}), s32[8,1,16]{2,1,0:T(1,128)S(1)}, u32[]{:S(2)}, u32[]{:S(2)}) async-start(s32[8,1,16]{2,1,0:T(1,128)} %broadcast_in_dim.41), calls=%async_computation | async-start | bytes 8192 | tf_op jit(solution)/shard_map/all_to_all | solution.py:226
  53.5 5.4 %copy-start.2 = (s32[16,1,32]{2,1,0:T(1,128)}, s32[16,1,32]{2,1,0:T(1,128)S(1)}, u32[]{:S(2)}) copy-start(s32[16,1,32]{2,1,0:T(1,128)S(1)} %all_to_all.14) | copy-start | bytes 6148
  53.5 5.4 %copy-start.1 = (bf16[2,2,128,1280]{3,2,1,0:T(8,128)(2,1)}, bf16[2,2,128,1280]{3,2,1,0:T(8,128)(2,1)S(1)}, u32[]{:S(2)}) copy-start(bf16[2,2,128,1280]{3,2,1,0:T(8,128)(2,1)S(1)} %collective-permute-done.refs_1_) | copy-start | bytes 3932164
  58.9 60.3 %collective-permute-start.3 = (bf16[2,4,128,1280]{3,2,1,0:T(8,128)(2,1)S(1)}, bf16[2,4,128,1280]{3,2,1,0:T(8,128)(2,1)S(1)}, u32[]{:S(2)}, u32[]{:S(2)}) collective-permute-start(bf16[2,4,128,1280]{3,2,1,0:T(8,128)(2,1)S(1)} %get-tuple-element.8), channel_id=1, source_target_pairs={{0,1},{1,2},{2,3},{3,0},{4,5},{5,6},{6,7},{7,4},{8,9},{9,10},{10,1... | collective-permute-start | bytes 7864328 | tf_op jit(solution)/shard_map/ppermute | solution.py:232
  59.6 59.6 %collective-permute-start.4 = (bf16[2,4,128,1280]{3,2,1,0:T(8,128)(2,1)S(1)}, bf16[2,4,128,1280]{3,2,1,0:T(8,128)(2,1)S(1)}, u32[]{:S(2)}, u32[]{:S(2)}) collective-permute-start(bf16[2,4,128,1280]{3,2,1,0:T(8,128)(2,1)S(1)} %get-tuple-element.9), channel_id=1, source_target_pairs={{0,2},{1,3},{2,0},{3,1},{4,6},{5,7},{6,4},{7,5},{8,10},{9,11},{10,... | collective-permute-start | bytes 7864328 | tf_op jit(solution)/shard_map/ppermute | solution.py:232
  60.6 60.2 %collective-permute-start.5 = (bf16[2,4,128,1280]{3,2,1,0:T(8,128)(2,1)S(1)}, bf16[2,4,128,1280]{3,2,1,0:T(8,128)(2,1)}, u32[]{:S(2)}, u32[]{:S(2)}) collective-permute-start(bf16[2,4,128,1280]{3,2,1,0:T(8,128)(2,1)S(1)} %get-tuple-element.10), channel_id=1, source_target_pairs={{0,3},{1,0},{2,1},{3,2},{4,7},{5,4},{6,5},{7,6},{8,11},{9,8},{10,9... | collective-permute-start | bytes 7864328 | tf_op jit(solution)/shard_map/ppermute | solution.py:232
  119.2 4.5 %copy-start.6 = (bf16[2,4,128,1280]{3,2,1,0:T(8,128)(2,1)}, bf16[2,4,128,1280]{3,2,1,0:T(8,128)(2,1)S(1)}, u32[]{:S(2)}) copy-start(bf16[2,4,128,1280]{3,2,1,0:T(8,128)(2,1)S(1)} %collective-permute-done.3.refs_4_) | copy-start | bytes 7864324
  119.2 1.5 %copy-start.7 = (bf16[2,4,128,1280]{3,2,1,0:T(8,128)(2,1)}, bf16[2,4,128,1280]{3,2,1,0:T(8,128)(2,1)S(1)}, u32[]{:S(2)}) copy-start(bf16[2,4,128,1280]{3,2,1,0:T(8,128)(2,1)S(1)} %collective-permute-done.4.refs_5_) | copy-start | bytes 7864324
Sparse Core Ops, SparseCore 0:
  15.2 108.3 all-reduce.1

commit v4 on v3

v4 whole, which is shorter than its diff:
```python
import functools

import jax
import jax.numpy as jnp
from jax import lax
from jax.experimental import pallas as pl
from jax.experimental.pallas import tpu as pltpu
from jax.sharding import Mesh
from jax.sharding import PartitionSpec as P

TW = 128
PART = 256
STEPS = 2
RING = 4
ROWS = 8
ROW = ("y", "core")
COL = ("z", "x")
GRID = ("core", "z", "x")


def plane_perm(first, shift):
    pairs = []
    for core in range(2):
        for z in range(RING):
            for x in range(RING):
                along_z = (core == 0) == first
                to_z, to_x = ((z + shift) % RING, x) if along_z else (z, (x + shift) % RING)
                pairs.append((core * 16 + z * RING + x, core * 16 + to_z * RING + to_x))
    return pairs


def round_y(shift):
    return [(chip, (chip + shift) % RING) for chip in range(RING)]


def wrap(value):
    return value & (RING - 1)


def origin(core, z, x, first_shift, second_shift):
    on_zero = wrap(z - first_shift) * RING + wrap(x - second_shift)
    on_one = wrap(z - second_shift) * RING + wrap(x - first_shift)
    return jnp.where(core == 0, on_zero, on_one)


def needed_tile(mask_ref, group):
    found = mask_ref[0, 2 * group + 1]
    for row in range(1, 8):
        found = found | mask_ref[row, 2 * group + 1]
    return jnp.where(found != 0, 1, 0)


def column_loads(mask_ref, amp_ref, held, sems, groups):
    loads, columns = [], []
    for place, group in enumerate(groups):
        column = 2 * group + needed_tile(mask_ref, group)
        columns.append(column)
        loads.append(pltpu.make_async_copy(
            amp_ref.at[:, pl.ds(pl.multiple_of(column * TW, TW), TW)], held.at[place], sems.at[place]))
        loads[place].start()
    return loads, columns


def apply_mask(mask_ref, held, place, column):
    for tile in range(held.shape[1] // TW):
        span = slice(tile * TW, (tile + 1) * TW)

        @pl.when(mask_ref[tile, column] == 0)
        def _():
            held[place, span, :] = jnp.zeros((TW, TW), held.dtype)


def compress_kernel(mask_ref, amp_ref, out_ref, held, in_sems, out_sems):
    groups = held.shape[0]
    loads, columns = column_loads(mask_ref, amp_ref, held, in_sems, range(groups))
    stores = []
    for group, load in enumerate(loads):
        load.wait()
        apply_mask(mask_ref, held, group, columns[group])
        stores.append(pltpu.make_async_copy(held.at[group], out_ref.at[group], out_sems.at[group]))
        stores[-1].start()
    for store in stores:
        store.wait()


def compress(amplitudes, amp_mask):
    rows, groups = amplitudes.shape[0], amp_mask.shape[1] // 2
    kind = amplitudes.dtype
    return pl.pallas_call(
        compress_kernel,
        in_specs=[pl.BlockSpec(memory_space=pltpu.SMEM), pl.BlockSpec(memory_space=pl.ANY)],
        out_specs=pl.BlockSpec(memory_space=pl.ANY),
        out_shape=jax.ShapeDtypeStruct((groups, rows, TW), kind),
        scratch_shapes=[pltpu.VMEM((groups, rows, TW), kind),
                        pltpu.SemaphoreType.DMA((groups,)), pltpu.SemaphoreType.DMA((groups,))],
        compiler_params=pltpu.CompilerParams(vmem_limit_bytes=60 << 20),
        name="compress",
    )(amp_mask, amplitudes)


def choose_kernel(info_ref, after_ref, pieces_ref, out_ref, held, in_sems, out_sems):
    each = held.shape[1]
    loads = [pltpu.make_async_copy(pieces_ref.at[pl.ds(info_ref[step] * each, each)], held.at[step], in_sems.at[step])
             for step in range(STEPS)]
    stores = [pltpu.make_async_copy(held.at[step], out_ref.at[step], out_sems.at[step]) for step in range(STEPS)]
    for load in loads:
        load.start()
    for load, store in zip(loads, stores):
        load.wait()
        store.start()
    for store in stores:
        store.wait()


def choose(info, after, pieces):
    groups, rows, _ = pieces.shape
    shape = (STEPS, groups // ROWS, rows, TW)
    return pl.pallas_call(
        choose_kernel,
        in_specs=[pl.BlockSpec(memory_space=pltpu.SMEM)] + [pl.BlockSpec(memory_space=pl.ANY)] * 2,
        out_specs=pl.BlockSpec(memory_space=pl.ANY),
        out_shape=jax.ShapeDtypeStruct(shape, pieces.dtype),
        scratch_shapes=[pltpu.VMEM(shape, pieces.dtype),
                        pltpu.SemaphoreType.DMA((STEPS,)), pltpu.SemaphoreType.DMA((STEPS,))],
        compiler_params=pltpu.CompilerParams(vmem_limit_bytes=4 << 20),
        name="choose",
    )(info, after, pieces)


def pick_kernel(needs_ref, info_ref, *refs):
    held, sent, sems = refs[:RING], refs[RING:2 * RING - 1], refs[2 * RING - 1]
    core, z, x = info_ref[3], info_ref[4], info_ref[5]
    copies = []
    for second in range(1, RING):
        for step in range(STEPS):
            for first in range(RING):
                group = origin(core, z, x, first, 0)
                tile = needs_ref[info_ref[step], second * 16 + group]
                copies.append(pltpu.make_async_copy(
                    held[first].at[step, tile], sent[second - 1].at[step, first], sems.at[len(copies)]))
                copies[-1].start()
    for copy in copies:
        copy.wait()


def pick(needs, info, held):
    steps, _, rows, width = held[0].shape
    shape = jax.ShapeDtypeStruct((steps, RING, rows, width), held[0].dtype)
    return pl.pallas_call(
        pick_kernel,
        in_specs=[pl.BlockSpec(memory_space=pltpu.SMEM)] * 2 + [pl.BlockSpec(memory_space=pltpu.VMEM)] * RING,
        out_specs=[pl.BlockSpec(memory_space=pl.ANY)] * (RING - 1),
        out_shape=[shape] * (RING - 1),
        scratch_shapes=[pltpu.SemaphoreType.DMA((steps * (RING - 1) * RING,))],
        compiler_params=pltpu.CompilerParams(vmem_limit_bytes=8 << 20),
        cost_estimate=pl.CostEstimate(flops=18400000000, bytes_accessed=8 << 20, transcendentals=0),
        name="pick",
    )(needs, info, *held)


def ladder_kernel(needs_ref, info_ref, *refs):
    halves, refs = refs[:10], refs[10:]
    held, blocks, (out_ref, lefts, rights, total, left_sems, right_sems, out_sems) = (
        refs[:RING], refs[RING:2 * RING - 1], refs[2 * RING - 1:])
    chip, core, z, x = (info_ref[2] >> 1), info_ref[3], info_ref[4], info_ref[5]
    each = halves[0].shape[1]
    parts = total.shape[0]

    def left(source, step, group):
        start = pl.multiple_of(group * TW, TW)
        return pltpu.make_async_copy(source, lefts.at[step, :, pl.ds(start, TW)], left_sems.at[step, group])

    def slot_of(group):
        back_z, back_x = wrap(z - (group >> 2)), wrap(x - group)
        return jnp.where(core == 0, back_x * RING + back_z, back_z * RING + back_x)

    def right(source, step, second, first=0, count=RING):
        return pltpu.make_async_copy(
            source, rights.at[step, pl.ds((second * RING + first) * TW, count * TW)], right_sems.at[step, second])

    def block(step, second):
        return blocks[second - 1].at[step]

    for step in range(STEPS):
        for place, half in enumerate((core, 1 - core)):
            for shift in range(RING):
                for inner in range(each):
                    group = (wrap(chip - shift) * 2 + half) * each + inner
                    part = halves[place * 5 + (0, 1, 3 + step, 2)[shift]]
                    left(part.at[inner] if shift == 2 else part.at[step, inner], step, slot_of(group)).start()
        for first in range(RING):
            tile = needs_ref[info_ref[step], origin(core, z, x, first, 0)]
            right(held[first].at[step, tile], step, 0, first, 1).start()
        for second in range(1, RING):
            right(block(step, second), step, second).start()

    for step, start, stop in ((0, 0, 1), (0, 1, RING), (1, 0, RING)):
        for second in range(start, stop):
            for first in range(RING):
                left(halves[0].at[step, 0], step, second * RING + first).wait()
            right(block(step, 1), step, second).wait()

        @pl.loop(0, parts)
        def _(part):
            span = pl.ds(pl.multiple_of(part * PART, PART), PART)
            depth = slice(start * RING * TW, stop * RING * TW)
            product = jnp.dot(lefts[step, :, depth], rights[step, depth, span], preferred_element_type=jnp.float32)
            total[part] = product if step == 0 and start == 0 else total[part] + product
            if step == STEPS - 1:
                pltpu.make_async_copy(total.at[part], out_ref.at[:, span], out_sems.at[part]).start()

    for part in range(parts):
        pltpu.make_async_copy(total.at[part], out_ref.at[:, pl.ds(part * PART, PART)], out_sems.at[part]).wait()


def multiply(needs, info, halves, held, blocks):
    steps, each, rows, _ = halves[0].shape
    groups = 2 * RING * each
    depth, width = groups * TW, held[0].shape[-1]
    kind = held[0].dtype
    return pl.pallas_call(
        ladder_kernel,
        in_specs=[pl.BlockSpec(memory_space=pltpu.SMEM)] * 2
        + [pl.BlockSpec(memory_space=pl.ANY)] * (len(halves) + len(held) + len(blocks)),
        out_specs=pl.BlockSpec(memory_space=pl.ANY),
        out_shape=jax.ShapeDtypeStruct((rows, width), jnp.float32),
        scratch_shapes=[pltpu.VMEM((steps, rows, depth), kind),
                        pltpu.VMEM((steps, depth, width), kind),
                        pltpu.VMEM((width // PART, rows, PART), jnp.float32),
                        pltpu.SemaphoreType.DMA((steps, groups)),
                        pltpu.SemaphoreType.DMA((steps, RING)),
                        pltpu.SemaphoreType.DMA((width // PART,))],
        compiler_params=pltpu.CompilerParams(vmem_limit_bytes=60 << 20),
        cost_estimate=pl.CostEstimate(flops=2 * rows * steps * depth * width, bytes_accessed=24 << 20, transcendentals=0),
        name="ladder",
    )(needs, info, *halves, *held, *[block.reshape(steps, RING * TW, width) for block in blocks])


def local(amplitudes, amp_mask, integrals, int_mask, steps):
    tiles, ab_width = integrals.shape[1] // TW, integrals.shape[2]
    row = lax.axis_index(ROW)
    core, z, x = (lax.axis_index(axis) for axis in GRID)
    info = jnp.stack([steps[0], steps[1], row, core, z, x]).astype(jnp.int32)

    own = jnp.max(amp_mask, axis=0).reshape(1, -1, 2)[:, :, 1]
    by_row = lax.all_to_all(jnp.broadcast_to(own, (ROWS, own.shape[1])), ROW, 0, 0, tiled=True)
    readers = [by_row] + [lax.ppermute(by_row, GRID, plane_perm(False, RING - ahead)) for ahead in (1, 2, 3)]
    needs = jnp.concatenate(readers, axis=1)

    gate = int_mask.astype(integrals.dtype)[:, :, None, :, None]
    block = integrals.reshape(STEPS, tiles, TW, ab_width // TW, TW) * gate
    block = block.reshape(STEPS, tiles, TW, ab_width)
    held = [block] + [lax.ppermute(block, GRID, plane_perm(True, shift)) for shift in (1, 2, 3)]

    sent = pick(needs, info, held)
    pieces = lax.all_to_all(compress(amplitudes, amp_mask), ROW, 0, 0, tiled=True)
    halves = [choose(info, sent[0], pieces)]
    halves += [lax.ppermute(halves[0], "y", round_y(shift)) for shift in (1, 3)]
    halves += [lax.ppermute(halves[1][0], "y", round_y(1)), lax.ppermute(halves[2][1], "y", round_y(3))]
    halves += [lax.ppermute(half, "core", [(0, 1), (1, 0)]) for half in halves]

    blocks = [lax.ppermute(sent[shift - 1], GRID, plane_perm(False, shift)) for shift in (1, 2, 3)]
    return multiply(needs, info, halves, held, blocks)


def solution(mesh):
    grid = Mesh(mesh.devices.reshape(4, 2, 4, 4), ("y", "core", "z", "x"))
    return jax.shard_map(
        local,
        mesh=grid,
        in_specs=(P(COL, ROW), P(COL, ROW), P(None, COL, ROW), P(None, COL, ROW), P()),
        out_specs=P(COL, ROW),
        check_vma=False,
    )
```

time: 149 us -> 141 us (0.946)
  blocking collectives: 18.1 us -> 0 us
  starting transfers between devices: 16.6 us -> 34.5 us
  between operations: 13.5 us -> 0.18 us
  Pallas kernels: 27.6 us -> 30.6 us
  waiting for transfers between devices: 64.4 us -> 66.5 us
  local copies, waits for them, and re-layouts: 4.49 us -> 6.35 us
    ppermute x3, waiting for transfers between devices: 56.9 us -> 4.64 us  [local(): lax.ppermute(sent[shift - 1], GRID, plane_perm(False, shift))]
    ppermute x0 -> x12, waiting for transfers between devices: none -> 33.9 us  [the longest x2 22.5 us: local(): halves += [lax.ppermute(halves[0], 'y', round_y(shift)) for shift in (1, 3)]]
    all_to_all x1 -> x0, blocking collectives: 18.1 us -> none  [local(): lax.all_to_all(jnp.broadcast_to(chosen.reshape(1, -1), (16, STEPS * group...]
    all_to_all x1 -> x2, waiting for transfers between devices: 4.56 us -> 22.6 us  [the longest x1 22.6 us: local(): lax.all_to_all(compress(amplitudes, amp_mask), ROW, 0, 0, tiled=True)]
    ppermute x0 -> x12, starting transfers between devices: none -> 13.5 us  [the longest x5 6.41 us: local(): halves += [lax.ppermute(half, 'core', [(0, 1), (1, 0)]) for half in halves]]
    ppermute x3, waiting for transfers between devices: 0.01 us -> 5.44 us  [local(): lax.ppermute(block, GRID, plane_perm(True, shift))]
    all_to_all x1 -> x2, starting transfers between devices: 7.58 us -> 11.7 us  [the longest x1 6.83 us: local(): lax.all_to_all(jnp.broadcast_to(own, (ROWS, own.shape[1])), ROW, 0, 0, ti...]
    psum x1 -> x0, waiting for transfers between devices: 2.94 us -> none  [local(): panels = lax.psum(compress(amplitudes, amp_mask, info, block), ROW)]
  transfers between devices with their start and end apart: 8 -> 20, of which waited for: 3 -> 12; matrix products, arithmetic and copies ran while one was open for 1% -> 1% of each run, Pallas kernels for 4% -> 9%
where the time goes in v4:
time: 141 us; the launch traced here: 140 us
  waiting for transfers between devices  66.5 us (47%)
  starting transfers between devices  34.5 us (24%)
  Pallas kernels  30.6 us (22%)
  local copies, waits for them, and re-layouts  6.35 us (5%)
  other arithmetic  2.2 us (2%)
    all_to_all x1, waiting for transfers between devices, local(): lax.all_to_all(compress(amplitudes, amp_mask), ROW, 0, 0, tiled=True)  22.6 us
    ppermute x2, waiting for transfers between devices, local(): halves += [lax.ppermute(halves[0], 'y', round_y(shift)) for shift in (1, 3)]  22.5 us
    pallas_call x1, Pallas kernels, multiply(): pl.pallas_call(ladder_kernel, in_specs=[pl.BlockSpec(memory_space=pltpu.S...  18.6 us
    all_to_all x1, starting transfers between devices, local(): lax.all_to_all(jnp.broadcast_to(own, (ROWS, own.shape[1])), ROW, 0, 0, ti...  6.83 us
    ppermute x5, starting transfers between devices, local(): halves += [lax.ppermute(half, 'core', [(0, 1), (1, 0)]) for half in halves]  6.41 us
    ppermute x3, waiting for transfers between devices, local(): lax.ppermute(block, GRID, plane_perm(True, shift))  5.44 us
    unnamed x36, local copies, waits for them, and re-layouts  5.23 us
    pallas_call x1, Pallas kernels, pick(): pl.pallas_call(pick_kernel, in_specs=[pl.BlockSpec(memory_space=pltpu.SME...  5.1 us
  transfers between devices with their start and end apart: 20, of which 12 were waited for; matrix products, arithmetic and copies ran while one was open for 1% of the time, Pallas kernels for 9%

profile of v4, /device:TPU:1, one launch (start us, length us, event | category | flops | bytes accessed | tf_op | source)
XLA Modules:
  0.0 140.3 jit_solution(6925808503570071624)
XLA Ops:
  0.0 0.7 convert_element_type.3
  0.8 1.4 %broadcast_multiply_fusion.refs_0_.refs_10_ = bf16[2,2,128,1280]{3,2,1,0:T(8,128)(2,1)S(1)} fusion(bf16[2,2,128,1280]{3,2,1,0:T(8,128)(2,1)} %bitcast.13, bf16[2,2,1280]{2,1,0:T(2,128)(2,1)S(1)} %mul.18), kind=kLoop, calls=%fused_computation | loop fusion | flops 655360 | bytes 2631680 | tf_op jit(solution)/shard_map/mul | solution.py:251
  2.2 3.4 %collective-permute-start.5 = (bf16[2,2,128,1280]{3,2,1,0:T(8,128)(2,1)S(1)}, bf16[2,2,128,1280]{3,2,1,0:T(8,128)(2,1)S(1)}, u32[]{:S(2)}, u32[]{:S(2)}) collective-permute-start(bf16[2,2,128,1280]{3,2,1,0:T(8,128)(2,1)S(1)} %broadcast_multiply_fusion.refs_0_.refs_10_), channel_id=1, source_target_pairs={{0,12},{1,13},{2,14},{3,15},{4,0},{5,1},{6,2},{7,3},{8,4},{9,5},{1... | collective-permute-start | bytes 3932168 | tf_op jit(solution)/shard_map/ppermute | solution.py:253
  5.6 0.5 collective-permute-start.4
  6.1 0.6 collective-permute-start.3
  6.7 0.1 reshape.27
  6.8 0.2 slice_reduce_fusion
  7.0 0.6 broadcast_in_dim.9
  7.6 6.8 %all-to-all-start = ((s32[8,1,16]{2,1,0:T(1,128)}), s32[8,1,16]{2,1,0:T(1,128)S(1)}, u32[]{:S(2)}, u32[]{:S(2)}) async-start(s32[8,1,16]{2,1,0:T(1,128)} %broadcast_in_dim.9), calls=%async_computation | async-start | bytes 8192 | tf_op jit(solution)/shard_map/all_to_all | solution.py:246
  14.5 5.0 %compress.1 = bf16[16,1024,128]{2,1,0:T(8,128)(2,1)} custom-call(s32[8,32]{1,0:T(8,128)} %mask_ref.1, bf16[1024,4096]{1,0:T(8,128)(2,1)} %amp_ref.1), custom_call_target="tpu_custom_call" | custom-call | tf_op jit(solution)/shard_map/compress/pallas_call | solution.py:89
  19.5 4.8 %all-to-all-start.1 = ((bf16[16,1024,128]{2,1,0:T(8,128)(2,1)}), bf16[16,1024,128]{2,1,0:T(8,128)(2,1)}, u32[]{:S(2)}, u32[]{:S(2)}) async-start(bf16[16,1024,128]{2,1,0:T(8,128)(2,1)} %compress.1), calls=%async_computation.1 | async-start | bytes 8388608 | tf_op jit(solution)/shard_map/all_to_all | solution.py:256
  24.4 2.0 %collective-permute-start.2 = (s32[8,16]{1,0:T(8,128)S(1)}, s32[8,16]{1,0:T(8,128)S(1)}, u32[]{:S(2)}, u32[]{:S(2)}) collective-permute-start(s32[8,16]{1,0:T(8,128)S(1)} %bitcast.14), channel_id=1, source_target_pairs={{0,1},{1,2},{2,3},{3,0},{4,5},{5,6},{6,7},{7,4},{8,9},{9,10},{10,1... | collective-permute-start | bytes 1544 | tf_op jit(solution)/shard_map/ppermute | solution.py:247
  26.3 0.9 collective-permute-start.1
  27.2 1.3 collective-permute-done.2
  28.5 0.5 collective-permute-start
  29.0 0.1 stack.19.info_ref
  29.1 1.7 %collective-permute-done.1 = s32[8,16]{1,0:T(8,128)S(1)} collective-permute-done((s32[8,16]{1,0:T(8,128)S(1)}, s32[8,16]{1,0:T(8,128)S(1)}, u32[]{:S(2)}, u32[]{:S(2)}) %collective-permute-start.1) | collective-permute-done | bytes 544 | tf_op jit(solution)/shard_map/ppermute | solution.py:247
  30.8 0.7 collective-permute-done
  31.5 0.1 pad_add_fusion.needs_ref
  31.6 2.7 %collective-permute-done.5.refs_3_.refs_13_ = bf16[2,2,128,1280]{3,2,1,0:T(8,128)(2,1)S(1)} collective-permute-done((bf16[2,2,128,1280]{3,2,1,0:T(8,128)(2,1)S(1)}, bf16[2,2,128,1280]{3,2,1,0:T(8,128)(2,1)S(1)}, u32[]{:S(2)}, u32[]{:S(2)}) %collective-permute-start.5) | collective-permute-done | bytes 1310752 | tf_op jit(solution)/shard_map/ppermute | solution.py:253
  34.3 1.1 copy-done.5
  35.4 2.7 %collective-permute-done.3.refs_1_.refs_11_ = bf16[2,2,128,1280]{3,2,1,0:T(8,128)(2,1)} collective-permute-done((bf16[2,2,128,1280]{3,2,1,0:T(8,128)(2,1)S(1)}, bf16[2,2,128,1280]{3,2,1,0:T(8,128)(2,1)}, u32[]{:S(2)}, u32[]{:S(2)}) %collective-permute-start.3) | collective-permute-done | bytes 1310752 | tf_op jit(solution)/shard_map/ppermute | solution.py:253
  38.1 1.3 copy-done.1
  39.4 1.3 copy-done.6
  40.7 5.1 %pick.1 = (bf16[2,4,128,1280]{3,2,1,0:T(8,128)(2,1)S(1)}, bf16[2,4,128,1280]{3,2,1,0:T(8,128)(2,1)}, bf16[2,4,128,1280]{3,2,1,0:T(8,128)(2,1)}) custom-call(s32[8,64]{1,0:T(8,128)S(1)} %pad_add_fusion.needs_ref, s32[6]{0:T(128)S(1)} %stack.19.info_ref, bf16[2,2,128,1280]{3,2,1,0:T(8,128)(2,1)S(1)} %copy-done.1, ...), custom_call_target="tpu_custom_call" | custom-call | flops 18400000000 | bytes 8388608 | tf_op jit(solution)/shard_map/pick/pallas_call | solution.py:149
  45.8 3.4 %collective-permute-start.16 = (bf16[2,4,128,1280]{3,2,1,0:T(8,128)(2,1)}, bf16[2,4,128,1280]{3,2,1,0:T(8,128)(2,1)}, u32[]{:S(2)}, u32[]{:S(2)}) collective-permute-start(bf16[2,4,128,1280]{3,2,1,0:T(8,128)(2,1)} %get-tuple-element.9), channel_id=1, source_target_pairs={{0,2},{1,3},{2,0},{3,1},{4,6},{5,7},{6,4},{7,5},{8,10},{9,11},{10,... | collective-permute-start | bytes 7864328 | tf_op jit(solution)/shard_map/ppermute | solution.py:262
  49.2 0.7 collective-permute-start.17
  50.0 0.8 collective-permute-start.15
  50.7 22.6 %all-to-all-done.1.pieces_ref = bf16[16,1024,128]{2,1,0:T(8,128)(2,1)} async-done(((bf16[16,1024,128]{2,1,0:T(8,128)(2,1)}), bf16[16,1024,128]{2,1,0:T(8,128)(2,1)}, u32[]{:S(2)}, u32[]{:S(2)}) %all-to-all-start.1) | async-done | bytes 4194336 | tf_op jit(solution)/shard_map/all_to_all | solution.py:256
  73.3 1.8 %choose.1.refs_0_ = bf16[2,2,1024,128]{3,2,1,0:T(8,128)(2,1)S(1)} custom-call(s32[6]{0:T(128)S(1)} %stack.19.info_ref, bf16[2,4,128,1280]{3,2,1,0:T(8,128)(2,1)S(1)} %get-tuple-element.8.after_ref, bf16[16,1024,128]{2,1,0:T(8,128)(2,1)} %all-to-all-done.1.pieces_ref), custom_call_target="tpu_custom_call" | custom-call | tf_op jit(solution)/shard_map/choose/pallas_call | solution.py:118
  75.1 1.0 collective-permute-start.7
  76.1 0.6 collective-permute-start.6
  76.6 22.4 %collective-permute-done.7.refs_2_ = bf16[2,2,1024,128]{3,2,1,0:T(8,128)(2,1)S(1)} collective-permute-done((bf16[2,2,1024,128]{3,2,1,0:T(8,128)(2,1)S(1)}, bf16[2,2,1024,128]{3,2,1,0:T(8,128)(2,1)S(1)}, u32[]{:S(2)}, u32[]{:S(2)}) %collective-permute-start.7) | collective-permute-done | bytes 1048608 | tf_op jit(solution)/shard_map/ppermute | solution.py:258
  99.1 1.7 %collective-permute-start.10 = (bf16[2,2,1024,128]{3,2,1,0:T(8,128)(2,1)S(1)}, bf16[2,2,1024,128]{3,2,1,0:T(8,128)(2,1)S(1)}, u32[]{:S(2)}, u32[]{:S(2)}) collective-permute-start(bf16[2,2,1024,128]{3,2,1,0:T(8,128)(2,1)S(1)} %choose.1.refs_0_), channel_id=1, source_target_pairs={{0,16},{16,0},{1,17},{17,1},{2,18},{18,2},{3,19},{19,3},{4,20},{20... | collective-permute-start | bytes 3145736 | tf_op jit(solution)/shard_map/ppermute | solution.py:260
  100.8 0.1 collective-permute-done.6.refs_1_
  100.9 2.1 %collective-permute-start.9 = (bf16[2,1024,128]{2,1,0:T(8,128)(2,1)S(1)}, bf16[2,1024,128]{2,1,0:T(8,128)(2,1)S(1)}, u32[]{:S(2)}, u32[]{:S(2)}) collective-permute-start(bf16[2,1024,128]{2,1,0:T(8,128)(2,1)S(1)} %slice_bitcast_fusion), channel_id=1, source_target_pairs={{0,96},{32,0},{64,32},{96,64},{1,97},{33,1},{65,33},{97,65},{2,98}... | collective-permute-start | bytes 1572872 | tf_op jit(solution)/shard_map/ppermute | solution.py:259
  103.1 4.6 %collective-permute-done.17 = bf16[2,4,128,1280]{3,2,1,0:T(8,128)(2,1)} collective-permute-done((bf16[2,4,128,1280]{3,2,1,0:T(8,128)(2,1)}, bf16[2,4,128,1280]{3,2,1,0:T(8,128)(2,1)}, u32[]{:S(2)}, u32[]{:S(2)}) %collective-permute-start.17) | collective-permute-done | bytes 2621472 | tf_op jit(solution)/shard_map/ppermute | solution.py:262
  107.7 2.7 %collective-permute-start.12 = (bf16[2,2,1024,128]{3,2,1,0:T(8,128)(2,1)S(1)}, bf16[2,2,1024,128]{3,2,1,0:T(8,128)(2,1)S(1)}, u32[]{:S(2)}, u32[]{:S(2)}) collective-permute-start(bf16[2,2,1024,128]{3,2,1,0:T(8,128)(2,1)S(1)} %collective-permute-done.7.refs_2_), channel_id=1, source_target_pairs={{0,16},{16,0},{1,17},{17,1},{2,18},{18,2},{3,19},{19,3},{4,20},{20... | collective-permute-start | bytes 3145736 | tf_op jit(solution)/shard_map/ppermute | solution.py:260
  110.4 0.1 collective-permute-start.11
  110.5 3.8 %collective-permute-done.9.refs_4_ = bf16[2,1024,128]{2,1,0:T(8,128)(2,1)S(1)} collective-permute-done((bf16[2,1024,128]{2,1,0:T(8,128)(2,1)S(1)}, bf16[2,1024,128]{2,1,0:T(8,128)(2,1)S(1)}, u32[]{:S(2)}, u32[]{:S(2)}) %collective-permute-start.9) | collective-permute-done | bytes 524320 | tf_op jit(solution)/shard_map/ppermute | solution.py:259
  114.3 0.9 collective-permute-start.14
  115.2 2.3 %collective-permute-done.8.refs_3_ = bf16[2,1024,128]{2,1,0:T(8,128)(2,1)S(1)} collective-permute-done((bf16[2,1024,128]{2,1,0:T(8,128)(2,1)S(1)}, bf16[2,1024,128]{2,1,0:T(8,128)(2,1)S(1)}, u32[]{:S(2)}, u32[]{:S(2)}) %collective-permute-start.8) | collective-permute-done | bytes 524320 | tf_op jit(solution)/shard_map/ppermute | solution.py:259
  117.5 1.1 collective-permute-start.13
  118.7 1.5 %collective-permute-done.13.refs_8_ = bf16[2,1024,128]{2,1,0:T(8,128)(2,1)S(1)} collective-permute-done((bf16[2,1024,128]{2,1,0:T(8,128)(2,1)S(1)}, bf16[2,1024,128]{2,1,0:T(8,128)(2,1)S(1)}, u32[]{:S(2)}, u32[]{:S(2)}) %collective-permute-start.13) | collective-permute-done | bytes 524320 | tf_op jit(solution)/shard_map/ppermute | solution.py:260
  120.2 1.0 copy-done.12
  121.2 0.1 copy-done.17
  121.4 0.4 copy-done.13
  121.7 18.6 %ladder.1 = f32[1024,1280]{1,0:T(8,128)} custom-call(s32[8,64]{1,0:T(8,128)} %copy-done.3, s32[6]{0:T(128)} %copy-done.4, bf16[2,2,1024,128]{3,2,1,0:T(8,128)(2,1)} %copy-done.2, bf16[2,2,1024,128]{3,2,1,0:T(8,128)(2,1)} %copy-done.8, bf16[2,2,1024,128]{3,2,1,0:T(8,128)(2,1)} %copy-done.7, bf16[2,1024,128]{2,1,0:T(8,128)(2,1)} %copy-done.15, ...), custom_call_target="tpu_custom_call" | custom-call | flops 10737418240 | bytes 25165824 | tf_op jit(solution)/shard_map/ladder/pallas_call | solution.py:221
  (44 shorter events, 0.3 us)
Async XLA Ops:
  0.0 6.7 %copy-start.9 = (s32[8,32]{1,0:T(8,128)S(1)}, s32[8,32]{1,0:T(8,128)}, u32[]{:S(2)}) copy-start(s32[8,32]{1,0:T(8,128)} %mask_ref.1) | copy-start | bytes 3076
  2.2 17.3 %copy-start = (bf16[2,2,128,1280]{3,2,1,0:T(8,128)(2,1)}, bf16[2,2,128,1280]{3,2,1,0:T(8,128)(2,1)S(1)}, u32[]{:S(2)}) copy-start(bf16[2,2,128,1280]{3,2,1,0:T(8,128)(2,1)S(1)} %broadcast_multiply_fusion.refs_0_.refs_10_) | copy-start | bytes 3932164
  2.2 32.1 %collective-permute-start.5 = (bf16[2,2,128,1280]{3,2,1,0:T(8,128)(2,1)S(1)}, bf16[2,2,128,1280]{3,2,1,0:T(8,128)(2,1)S(1)}, u32[]{:S(2)}, u32[]{:S(2)}) collective-permute-start(bf16[2,2,128,1280]{3,2,1,0:T(8,128)(2,1)S(1)} %broadcast_multiply_fusion.refs_0_.refs_10_), channel_id=1, source_target_pairs={{0,12},{1,13},{2,14},{3,15},{4,0},{5,1},{6,2},{7,3},{8,4},{9,5},{1... | collective-permute-start | bytes 3932168 | tf_op jit(solution)/shard_map/ppermute | solution.py:253
  5.6 29.8 %collective-permute-start.4 = (bf16[2,2,128,1280]{3,2,1,0:T(8,128)(2,1)S(1)}, bf16[2,2,128,1280]{3,2,1,0:T(8,128)(2,1)}, u32[]{:S(2)}, u32[]{:S(2)}) collective-permute-start(bf16[2,2,128,1280]{3,2,1,0:T(8,128)(2,1)S(1)} %broadcast_multiply_fusion.refs_0_.refs_10_), channel_id=1, source_target_pairs={{0,8},{1,9},{2,10},{3,11},{4,12},{5,13},{6,14},{7,15},{8,0},{9,1},... | collective-permute-start | bytes 3932168 | tf_op jit(solution)/shard_map/ppermute | solution.py:253
  6.1 32.0 %collective-permute-start.3 = (bf16[2,2,128,1280]{3,2,1,0:T(8,128)(2,1)S(1)}, bf16[2,2,128,1280]{3,2,1,0:T(8,128)(2,1)}, u32[]{:S(2)}, u32[]{:S(2)}) collective-permute-start(bf16[2,2,128,1280]{3,2,1,0:T(8,128)(2,1)S(1)} %broadcast_multiply_fusion.refs_0_.refs_10_), channel_id=1, source_target_pairs={{0,4},{1,5},{2,6},{3,7},{4,8},{5,9},{6,10},{7,11},{8,12},{9,13},{1... | collective-permute-start | bytes 3932168 | tf_op jit(solution)/shard_map/ppermute | solution.py:253
  7.6 11.9 %all-to-all-start = ((s32[8,1,16]{2,1,0:T(1,128)}), s32[8,1,16]{2,1,0:T(1,128)S(1)}, u32[]{:S(2)}, u32[]{:S(2)}) async-start(s32[8,1,16]{2,1,0:T(1,128)} %broadcast_in_dim.9), calls=%async_computation | async-start | bytes 8192 | tf_op jit(solution)/shard_map/all_to_all | solution.py:246
  19.5 9.5 %copy-start.10 = (s32[2]{0:T(128)S(1)}, s32[2]{0:T(128)}, u32[]{:S(2)}) copy-start(s32[2]{0:T(128)} %param.9) | copy-start | bytes 28
  19.5 53.7 %all-to-all-start.1 = ((bf16[16,1024,128]{2,1,0:T(8,128)(2,1)}), bf16[16,1024,128]{2,1,0:T(8,128)(2,1)}, u32[]{:S(2)}, u32[]{:S(2)}) async-start(bf16[16,1024,128]{2,1,0:T(8,128)(2,1)} %compress.1), calls=%async_computation.1 | async-start | bytes 8388608 | tf_op jit(solution)/shard_map/all_to_all | solution.py:256
  24.4 4.2 %collective-permute-start.2 = (s32[8,16]{1,0:T(8,128)S(1)}, s32[8,16]{1,0:T(8,128)S(1)}, u32[]{:S(2)}, u32[]{:S(2)}) collective-permute-start(s32[8,16]{1,0:T(8,128)S(1)} %bitcast.14), channel_id=1, source_target_pairs={{0,1},{1,2},{2,3},{3,0},{4,5},{5,6},{6,7},{7,4},{8,9},{9,10},{10,1... | collective-permute-start | bytes 1544 | tf_op jit(solution)/shard_map/ppermute | solution.py:247
  26.3 4.5 %collective-permute-start.1 = (s32[8,16]{1,0:T(8,128)S(1)}, s32[8,16]{1,0:T(8,128)S(1)}, u32[]{:S(2)}, u32[]{:S(2)}) collective-permute-start(s32[8,16]{1,0:T(8,128)S(1)} %bitcast.15), channel_id=1, source_target_pairs={{0,2},{1,3},{2,0},{3,1},{4,6},{5,7},{6,4},{7,5},{8,10},{9,11},{10,... | collective-permute-start | bytes 1544 | tf_op jit(solution)/shard_map/ppermute | solution.py:247
  28.5 3.0 %collective-permute-start = (s32[8,16]{1,0:T(8,128)S(1)}, s32[8,16]{1,0:T(8,128)S(1)}, u32[]{:S(2)}, u32[]{:S(2)}) collective-permute-start(s32[8,16]{1,0:T(8,128)S(1)} %bitcast.16), channel_id=1, source_target_pairs={{0,3},{1,0},{2,1},{3,2},{4,7},{5,4},{6,5},{7,6},{8,11},{9,8},{10,9... | collective-permute-start | bytes 1544 | tf_op jit(solution)/shard_map/ppermute | solution.py:247
  29.1 44.2 %copy-start.4 = (s32[6]{0:T(128)}, s32[6]{0:T(128)S(1)}, u32[]{:S(2)}) copy-start(s32[6]{0:T(128)S(1)} %stack.19.info_ref) | copy-start | bytes 76
  31.6 14.3 %copy-start.3 = (s32[8,64]{1,0:T(8,128)}, s32[8,64]{1,0:T(8,128)S(1)}, u32[]{:S(2)}) copy-start(s32[8,64]{1,0:T(8,128)S(1)} %pad_add_fusion.needs_ref) | copy-start | bytes 6148
  34.3 1.1 copy-start.5
  38.1 1.3 copy-start.1
  39.4 1.3 copy-start.6
  45.8 57.2 %collective-permute-start.16 = (bf16[2,4,128,1280]{3,2,1,0:T(8,128)(2,1)}, bf16[2,4,128,1280]{3,2,1,0:T(8,128)(2,1)}, u32[]{:S(2)}, u32[]{:S(2)}) collective-permute-start(bf16[2,4,128,1280]{3,2,1,0:T(8,128)(2,1)} %get-tuple-element.9), channel_id=1, source_target_pairs={{0,2},{1,3},{2,0},{3,1},{4,6},{5,7},{6,4},{7,5},{8,10},{9,11},{10,... | collective-permute-start | bytes 7864328 | tf_op jit(solution)/shard_map/ppermute | solution.py:262
  49.2 58.5 %collective-permute-start.17 = (bf16[2,4,128,1280]{3,2,1,0:T(8,128)(2,1)}, bf16[2,4,128,1280]{3,2,1,0:T(8,128)(2,1)}, u32[]{:S(2)}, u32[]{:S(2)}) collective-permute-start(bf16[2,4,128,1280]{3,2,1,0:T(8,128)(2,1)} %get-tuple-element.10), channel_id=1, source_target_pairs={{0,3},{1,0},{2,1},{3,2},{4,7},{5,4},{6,5},{7,6},{8,11},{9,8},{10,9... | collective-permute-start | bytes 7864328 | tf_op jit(solution)/shard_map/ppermute | solution.py:262
  50.0 60.5 %collective-permute-start.15 = (bf16[2,4,128,1280]{3,2,1,0:T(8,128)(2,1)S(1)}, bf16[2,4,128,1280]{3,2,1,0:T(8,128)(2,1)}, u32[]{:S(2)}, u32[]{:S(2)}) collective-permute-start(bf16[2,4,128,1280]{3,2,1,0:T(8,128)(2,1)S(1)} %get-tuple-element.8.after_ref), channel_id=1, source_target_pairs={{0,1},{1,2},{2,3},{3,0},{4,5},{5,6},{6,7},{7,4},{8,9},{9,10},{10,1... | collective-permute-start | bytes 7864328 | tf_op jit(solution)/shard_map/ppermute | solution.py:262
  75.1 35.3 %copy-start.2 = (bf16[2,2,1024,128]{3,2,1,0:T(8,128)(2,1)}, bf16[2,2,1024,128]{3,2,1,0:T(8,128)(2,1)S(1)}, u32[]{:S(2)}) copy-start(bf16[2,2,1024,128]{3,2,1,0:T(8,128)(2,1)S(1)} %choose.1.refs_0_) | copy-start | bytes 3145732
  75.1 24.0 %collective-permute-start.7 = (bf16[2,2,1024,128]{3,2,1,0:T(8,128)(2,1)S(1)}, bf16[2,2,1024,128]{3,2,1,0:T(8,128)(2,1)S(1)}, u32[]{:S(2)}, u32[]{:S(2)}) collective-permute-start(bf16[2,2,1024,128]{3,2,1,0:T(8,128)(2,1)S(1)} %choose.1.refs_0_), channel_id=1, source_target_pairs={{0,96},{32,0},{64,32},{96,64},{1,97},{33,1},{65,33},{97,65},{2,98}... | collective-permute-start | bytes 3145736 | tf_op jit(solution)/shard_map/ppermute | solution.py:258
  76.1 24.8 %collective-permute-start.6 = (bf16[2,2,1024,128]{3,2,1,0:T(8,128)(2,1)S(1)}, bf16[2,2,1024,128]{3,2,1,0:T(8,128)(2,1)S(1)}, u32[]{:S(2)}, u32[]{:S(2)}) collective-permute-start(bf16[2,2,1024,128]{3,2,1,0:T(8,128)(2,1)S(1)} %choose.1.refs_0_), channel_id=1, source_target_pairs={{0,32},{32,64},{64,96},{96,0},{1,33},{33,65},{65,97},{97,1},{2,34}... | collective-permute-start | bytes 3145736 | tf_op jit(solution)/shard_map/ppermute | solution.py:258
  99.1 19.6 %copy-start.7 = (bf16[2,2,1024,128]{3,2,1,0:T(8,128)(2,1)}, bf16[2,2,1024,128]{3,2,1,0:T(8,128)(2,1)S(1)}, u32[]{:S(2)}) copy-start(bf16[2,2,1024,128]{3,2,1,0:T(8,128)(2,1)S(1)} %collective-permute-done.7.refs_2_) | copy-start | bytes 3145732
  99.1 19.6 %collective-permute-start.10 = (bf16[2,2,1024,128]{3,2,1,0:T(8,128)(2,1)S(1)}, bf16[2,2,1024,128]{3,2,1,0:T(8,128)(2,1)S(1)}, u32[]{:S(2)}, u32[]{:S(2)}) collective-permute-start(bf16[2,2,1024,128]{3,2,1,0:T(8,128)(2,1)S(1)} %choose.1.refs_0_), channel_id=1, source_target_pairs={{0,16},{16,0},{1,17},{17,1},{2,18},{18,2},{3,19},{19,3},{4,20},{20... | collective-permute-start | bytes 3145736 | tf_op jit(solution)/shard_map/ppermute | solution.py:260
  100.9 19.3 %copy-start.8 = (bf16[2,2,1024,128]{3,2,1,0:T(8,128)(2,1)}, bf16[2,2,1024,128]{3,2,1,0:T(8,128)(2,1)S(1)}, u32[]{:S(2)}) copy-start(bf16[2,2,1024,128]{3,2,1,0:T(8,128)(2,1)S(1)} %collective-permute-done.6.refs_1_) | copy-start | bytes 3145732
  100.9 13.5 %collective-permute-start.9 = (bf16[2,1024,128]{2,1,0:T(8,128)(2,1)S(1)}, bf16[2,1024,128]{2,1,0:T(8,128)(2,1)S(1)}, u32[]{:S(2)}, u32[]{:S(2)}) collective-permute-start(bf16[2,1024,128]{2,1,0:T(8,128)(2,1)S(1)} %slice_bitcast_fusion), channel_id=1, source_target_pairs={{0,96},{32,0},{64,32},{96,64},{1,97},{33,1},{65,33},{97,65},{2,98}... | collective-permute-start | bytes 1572872 | tf_op jit(solution)/shard_map/ppermute | solution.py:259
  103.0 14.5 %collective-permute-start.8 = (bf16[2,1024,128]{2,1,0:T(8,128)(2,1)S(1)}, bf16[2,1024,128]{2,1,0:T(8,128)(2,1)S(1)}, u32[]{:S(2)}, u32[]{:S(2)}) collective-permute-start(bf16[2,1024,128]{2,1,0:T(8,128)(2,1)S(1)} %slice_bitcast_fusion.1), channel_id=1, source_target_pairs={{0,32},{32,64},{64,96},{96,0},{1,33},{33,65},{65,97},{97,1},{2,34}... | collective-permute-start | bytes 1572872 | tf_op jit(solution)/shard_map/ppermute | solution.py:259
  107.7 12.4 %collective-permute-start.12 = (bf16[2,2,1024,128]{3,2,1,0:T(8,128)(2,1)S(1)}, bf16[2,2,1024,128]{3,2,1,0:T(8,128)(2,1)S(1)}, u32[]{:S(2)}, u32[]{:S(2)}) collective-permute-start(bf16[2,2,1024,128]{3,2,1,0:T(8,128)(2,1)S(1)} %collective-permute-done.7.refs_2_), channel_id=1, source_target_pairs={{0,16},{16,0},{1,17},{17,1},{2,18},{18,2},{3,19},{19,3},{4,20},{20... | collective-permute-start | bytes 3145736 | tf_op jit(solution)/shard_map/ppermute | solution.py:260
  110.4 9.8 %collective-permute-start.11 = (bf16[2,2,1024,128]{3,2,1,0:T(8,128)(2,1)S(1)}, bf16[2,2,1024,128]{3,2,1,0:T(8,128)(2,1)S(1)}, u32[]{:S(2)}, u32[]{:S(2)}) collective-permute-start(bf16[2,2,1024,128]{3,2,1,0:T(8,128)(2,1)S(1)} %collective-permute-done.6.refs_1_), channel_id=1, source_target_pairs={{0,16},{16,0},{1,17},{17,1},{2,18},{18,2},{3,19},{19,3},{4,20},{20... | collective-permute-start | bytes 3145736 | tf_op jit(solution)/shard_map/ppermute | solution.py:260
  114.3 6.9 %copy-start.14 = (bf16[2,1024,128]{2,1,0:T(8,128)(2,1)}, bf16[2,1024,128]{2,1,0:T(8,128)(2,1)S(1)}, u32[]{:S(2)}) copy-start(bf16[2,1024,128]{2,1,0:T(8,128)(2,1)S(1)} %collective-permute-done.9.refs_4_) | copy-start | bytes 1572868
  114.3 4.3 %collective-permute-start.14 = (bf16[2,1024,128]{2,1,0:T(8,128)(2,1)S(1)}, bf16[2,1024,128]{2,1,0:T(8,128)(2,1)S(1)}, u32[]{:S(2)}, u32[]{:S(2)}) collective-permute-start(bf16[2,1024,128]{2,1,0:T(8,128)(2,1)S(1)} %collective-permute-done.9.refs_4_), channel_id=1, source_target_pairs={{0,16},{16,0},{1,17},{17,1},{2,18},{18,2},{3,19},{19,3},{4,20},{20... | collective-permute-start | bytes 1572872 | tf_op jit(solution)/shard_map/ppermute | solution.py:260
  117.5 3.7 %copy-start.15 = (bf16[2,1024,128]{2,1,0:T(8,128)(2,1)}, bf16[2,1024,128]{2,1,0:T(8,128)(2,1)S(1)}, u32[]{:S(2)}) copy-start(bf16[2,1024,128]{2,1,0:T(8,128)(2,1)S(1)} %collective-permute-done.8.refs_3_) | copy-start | bytes 1572868
  117.5 2.6 %collective-permute-start.13 = (bf16[2,1024,128]{2,1,0:T(8,128)(2,1)S(1)}, bf16[2,1024,128]{2,1,0:T(8,128)(2,1)S(1)}, u32[]{:S(2)}, u32[]{:S(2)}) collective-permute-start(bf16[2,1024,128]{2,1,0:T(8,128)(2,1)S(1)} %collective-permute-done.8.refs_3_), channel_id=1, source_target_pairs={{0,16},{16,0},{1,17},{17,1},{2,18},{18,2},{3,19},{19,3},{4,20},{20... | collective-permute-start | bytes 1572872 | tf_op jit(solution)/shard_map/ppermute | solution.py:260
  118.7 1.6 %copy-start.11 = (bf16[2,2,1024,128]{3,2,1,0:T(8,128)(2,1)}, bf16[2,2,1024,128]{3,2,1,0:T(8,128)(2,1)S(1)}, u32[]{:S(2)}) copy-start(bf16[2,2,1024,128]{3,2,1,0:T(8,128)(2,1)S(1)} %collective-permute-done.10.refs_5_) | copy-start | bytes 3145732
  118.7 2.6 %copy-start.16 = (bf16[2,1024,128]{2,1,0:T(8,128)(2,1)}, bf16[2,1024,128]{2,1,0:T(8,128)(2,1)S(1)}, u32[]{:S(2)}) copy-start(bf16[2,1024,128]{2,1,0:T(8,128)(2,1)S(1)} %collective-permute-done.14.refs_9_) | copy-start | bytes 1572868
  120.2 1.2 copy-start.17
  120.2 1.0 copy-start.12
  120.2 1.5 %copy-start.13 = (bf16[2,2,1024,128]{3,2,1,0:T(8,128)(2,1)}, bf16[2,2,1024,128]{3,2,1,0:T(8,128)(2,1)S(1)}, u32[]{:S(2)}) copy-start(bf16[2,2,1024,128]{3,2,1,0:T(8,128)(2,1)S(1)} %collective-permute-done.11.refs_6_) | copy-start | bytes 3145732

commit v5 on v4

--- a/solution.py
+++ b/solution.py
@@ -93,7 +93,7 @@
         out_shape=jax.ShapeDtypeStruct((groups, rows, TW), kind),
         scratch_shapes=[pltpu.VMEM((groups, rows, TW), kind),
                         pltpu.SemaphoreType.DMA((groups,)), pltpu.SemaphoreType.DMA((groups,))],
-        compiler_params=pltpu.CompilerParams(vmem_limit_bytes=60 << 20),
+        compiler_params=pltpu.CompilerParams(vmem_limit_bytes=54 << 20),
         name="compress",
     )(amp_mask, amplitudes)
 
@@ -123,6 +123,7 @@
         scratch_shapes=[pltpu.VMEM(shape, pieces.dtype),
                         pltpu.SemaphoreType.DMA((STEPS,)), pltpu.SemaphoreType.DMA((STEPS,))],
         compiler_params=pltpu.CompilerParams(vmem_limit_bytes=4 << 20),
+        cost_estimate=pl.CostEstimate(flops=13800000000, bytes_accessed=2 << 20, transcendentals=0),
         name="choose",
     )(info, after, pieces)
 
@@ -153,7 +154,7 @@
         out_shape=[shape] * (RING - 1),
         scratch_shapes=[pltpu.SemaphoreType.DMA((steps * (RING - 1) * RING,))],
         compiler_params=pltpu.CompilerParams(vmem_limit_bytes=8 << 20),
-        cost_estimate=pl.CostEstimate(flops=18400000000, bytes_accessed=8 << 20, transcendentals=0),
+        cost_estimate=pl.CostEstimate(flops=27600000000, bytes_accessed=8 << 20, transcendentals=0),
         name="pick",
     )(needs, info, *held)
 
@@ -194,7 +195,7 @@
         for second in range(1, RING):
             right(block(step, second), step, second).start()
 
-    for step, start, stop in ((0, 0, 1), (0, 1, RING), (1, 0, RING)):
+    for step, start, stop in ((0, 0, RING), (1, 0, RING)):
         for second in range(start, stop):
             for first in range(RING):
                 left(halves[0].at[step, 0], step, second * RING + first).wait()
@@ -230,7 +231,7 @@
                         pltpu.SemaphoreType.DMA((steps, groups)),
                         pltpu.SemaphoreType.DMA((steps, RING)),
                         pltpu.SemaphoreType.DMA((width // PART,))],
-        compiler_params=pltpu.CompilerParams(vmem_limit_bytes=60 << 20),
+        compiler_params=pltpu.CompilerParams(vmem_limit_bytes=28 << 20),
         cost_estimate=pl.CostEstimate(flops=2 * rows * steps * depth * width, bytes_accessed=24 << 20, transcendentals=0),
         name="ladder",
     )(needs, info, *halves, *held, *[block.reshape(steps, RING * TW, width) for block in blocks])

time: 141 us -> 139 us (0.986)
  local copies, waits for them, and re-layouts: 6.35 us -> 1.13 us
  waiting for transfers between devices: 66.5 us -> 70.2 us
    unnamed x36 -> x4, local copies, waits for them, and re-layouts: 5.23 us -> 0.01 us
    ppermute x1, waiting for transfers between devices: 3.82 us -> 6.65 us  [local(): lax.ppermute(halves[2][1], 'y', round_y(3))]
    ppermute x3, waiting for transfers between devices: 4.64 us -> 1.9 us  [local(): lax.ppermute(sent[shift - 1], GRID, plane_perm(False, shift))]
    all_to_all x1, waiting for transfers between devices: 22.6 us -> 25.2 us  [local(): lax.all_to_all(compress(amplitudes, amp_mask), ROW, 0, 0, tiled=True)]
where the time goes in v5:
time: 139 us; the launch traced here: 138 us
  waiting for transfers between devices  70.2 us (51%)
  starting transfers between devices  34.6 us (25%)
  Pallas kernels  30.2 us (22%)
  other arithmetic  2.2 us (2%)
    all_to_all x1, waiting for transfers between devices, local(): lax.all_to_all(compress(amplitudes, amp_mask), ROW, 0, 0, tiled=True)  25.2 us
    ppermute x2, waiting for transfers between devices, local(): halves += [lax.ppermute(halves[0], 'y', round_y(shift)) for shift in (1, 3)]  22.5 us
    pallas_call x1, Pallas kernels, multiply(): pl.pallas_call(ladder_kernel, in_specs=[pl.BlockSpec(memory_space=pltpu.S...  18.3 us
    all_to_all x1, starting transfers between devices, local(): lax.all_to_all(jnp.broadcast_to(own, (ROWS, own.shape[1])), ROW, 0, 0, ti...  6.83 us
    ppermute x1, waiting for transfers between devices, local(): lax.ppermute(halves[2][1], 'y', round_y(3))  6.65 us
    ppermute x3, waiting for transfers between devices, local(): lax.ppermute(block, GRID, plane_perm(True, shift))  6.49 us
    ppermute x5, starting transfers between devices, local(): halves += [lax.ppermute(half, 'core', [(0, 1), (1, 0)]) for half in halves]  6.34 us
    pallas_call x1, Pallas kernels, compress(): pl.pallas_call(compress_kernel, in_specs=[pl.BlockSpec(memory_space=pltpu...  5.06 us
  transfers between devices with their start and end apart: 20, of which 12 were waited for; matrix products, arithmetic and copies ran while one was open for 1% of the time, Pallas kernels for 9%

profile of v5, /device:TPU:1, one launch (start us, length us, event | category | flops | bytes accessed | tf_op | source)
XLA Modules:
  0.0 138.5 jit_solution(2312867856384064618)
XLA Ops:
  0.0 0.7 convert_element_type.3
  0.7 0.1 mul.17
  0.8 1.4 %broadcast_multiply_fusion.refs_0_.refs_10_ = bf16[2,2,128,1280]{3,2,1,0:T(8,128)(2,1)S(1)} fusion(bf16[2,2,128,1280]{3,2,1,0:T(8,128)(2,1)} %bitcast.13, bf16[2,2,1280]{2,1,0:T(2,128)(2,1)S(1)} %mul.18), kind=kLoop, calls=%fused_computation | loop fusion | flops 655360 | bytes 2631680 | tf_op jit(solution)/shard_map/mul | solution.py:252
  2.2 3.4 %collective-permute-start.5 = (bf16[2,2,128,1280]{3,2,1,0:T(8,128)(2,1)S(1)}, bf16[2,2,128,1280]{3,2,1,0:T(8,128)(2,1)S(1)}, u32[]{:S(2)}, u32[]{:S(2)}) collective-permute-start(bf16[2,2,128,1280]{3,2,1,0:T(8,128)(2,1)S(1)} %broadcast_multiply_fusion.refs_0_.refs_10_), channel_id=1, source_target_pairs={{0,12},{1,13},{2,14},{3,15},{4,0},{5,1},{6,2},{7,3},{8,4},{9,5},{1... | collective-permute-start | bytes 3932168 | tf_op jit(solution)/shard_map/ppermute | solution.py:254
  5.6 0.5 collective-permute-start.4
  6.1 0.6 collective-permute-start.3
  6.7 0.1 reshape.27
  6.8 0.2 slice_reduce_fusion
  7.0 0.6 broadcast_in_dim.9
  7.6 6.8 %all-to-all-start = ((s32[8,1,16]{2,1,0:T(1,128)}), s32[8,1,16]{2,1,0:T(1,128)S(1)}, u32[]{:S(2)}, u32[]{:S(2)}) async-start(s32[8,1,16]{2,1,0:T(1,128)} %broadcast_in_dim.9), calls=%async_computation | async-start | bytes 8192 | tf_op jit(solution)/shard_map/all_to_all | solution.py:247
  14.5 5.1 %compress.1 = bf16[16,1024,128]{2,1,0:T(8,128)(2,1)} custom-call(s32[8,32]{1,0:T(8,128)} %mask_ref.1, bf16[1024,4096]{1,0:T(8,128)(2,1)} %amp_ref.1), custom_call_target="tpu_custom_call" | custom-call | tf_op jit(solution)/shard_map/compress/pallas_call | solution.py:89
  19.5 0.0 copy-start.1
  19.5 4.8 %all-to-all-start.1 = ((bf16[16,1024,128]{2,1,0:T(8,128)(2,1)}), bf16[16,1024,128]{2,1,0:T(8,128)(2,1)}, u32[]{:S(2)}, u32[]{:S(2)}) async-start(bf16[16,1024,128]{2,1,0:T(8,128)(2,1)} %compress.1), calls=%async_computation.1 | async-start | bytes 8388608 | tf_op jit(solution)/shard_map/all_to_all | solution.py:257
  24.4 1.9 %collective-permute-start.2 = (s32[8,16]{1,0:T(8,128)S(1)}, s32[8,16]{1,0:T(8,128)S(1)}, u32[]{:S(2)}, u32[]{:S(2)}) collective-permute-start(s32[8,16]{1,0:T(8,128)S(1)} %bitcast.14), channel_id=1, source_target_pairs={{0,1},{1,2},{2,3},{3,0},{4,5},{5,6},{6,7},{7,4},{8,9},{9,10},{10,1... | collective-permute-start | bytes 1544 | tf_op jit(solution)/shard_map/ppermute | solution.py:248
  26.3 1.0 collective-permute-start.1
  27.3 1.3 collective-permute-done.2
  28.6 0.5 collective-permute-start
  29.1 0.1 stack.19.info_ref
  29.1 1.6 %collective-permute-done.1 = s32[8,16]{1,0:T(8,128)S(1)} collective-permute-done((s32[8,16]{1,0:T(8,128)S(1)}, s32[8,16]{1,0:T(8,128)S(1)}, u32[]{:S(2)}, u32[]{:S(2)}) %collective-permute-start.1) | collective-permute-done | bytes 544 | tf_op jit(solution)/shard_map/ppermute | solution.py:248
  30.8 0.7 collective-permute-done
  31.5 0.1 pad_add_fusion.needs_ref
  31.6 2.7 %collective-permute-done.5.refs_3_.refs_13_ = bf16[2,2,128,1280]{3,2,1,0:T(8,128)(2,1)S(1)} collective-permute-done((bf16[2,2,128,1280]{3,2,1,0:T(8,128)(2,1)S(1)}, bf16[2,2,128,1280]{3,2,1,0:T(8,128)(2,1)S(1)}, u32[]{:S(2)}, u32[]{:S(2)}) %collective-permute-start.5) | collective-permute-done | bytes 1310752 | tf_op jit(solution)/shard_map/ppermute | solution.py:254
  34.3 3.8 %collective-permute-done.3.refs_1_.refs_11_ = bf16[2,2,128,1280]{3,2,1,0:T(8,128)(2,1)} collective-permute-done((bf16[2,2,128,1280]{3,2,1,0:T(8,128)(2,1)S(1)}, bf16[2,2,128,1280]{3,2,1,0:T(8,128)(2,1)}, u32[]{:S(2)}, u32[]{:S(2)}) %collective-permute-start.3) | collective-permute-done | bytes 1310752 | tf_op jit(solution)/shard_map/ppermute | solution.py:254
  38.1 5.0 %pick.1 = (bf16[2,4,128,1280]{3,2,1,0:T(8,128)(2,1)}, bf16[2,4,128,1280]{3,2,1,0:T(8,128)(2,1)}, bf16[2,4,128,1280]{3,2,1,0:T(8,128)(2,1)}) custom-call(s32[8,64]{1,0:T(8,128)S(1)} %pad_add_fusion.needs_ref, s32[6]{0:T(128)S(1)} %stack.19.info_ref, bf16[2,2,128,1280]{3,2,1,0:T(8,128)(2,1)S(1)} %broadcast_multiply_fusion.refs_0_.refs_10_, ...), custom_call_target="tpu_custom_call" | custom-call | flops 27599998976 | bytes 8388608 | tf_op jit(solution)/shard_map/pick/pallas_call | solution.py:150
  43.1 3.6 %collective-permute-start.16 = (bf16[2,4,128,1280]{3,2,1,0:T(8,128)(2,1)}, bf16[2,4,128,1280]{3,2,1,0:T(8,128)(2,1)}, u32[]{:S(2)}, u32[]{:S(2)}) collective-permute-start(bf16[2,4,128,1280]{3,2,1,0:T(8,128)(2,1)} %get-tuple-element.9), channel_id=1, source_target_pairs={{0,2},{1,3},{2,0},{3,1},{4,6},{5,7},{6,4},{7,5},{8,10},{9,11},{10,... | collective-permute-start | bytes 7864328 | tf_op jit(solution)/shard_map/ppermute | solution.py:263
  46.7 0.6 collective-permute-start.17
  47.2 0.9 collective-permute-start.15
  48.1 25.2 %all-to-all-done.1.pieces_ref = bf16[16,1024,128]{2,1,0:T(8,128)(2,1)} async-done(((bf16[16,1024,128]{2,1,0:T(8,128)(2,1)}), bf16[16,1024,128]{2,1,0:T(8,128)(2,1)}, u32[]{:S(2)}, u32[]{:S(2)}) %all-to-all-start.1) | async-done | bytes 4194336 | tf_op jit(solution)/shard_map/all_to_all | solution.py:257
  73.3 1.8 %choose.1.refs_0_ = bf16[2,2,1024,128]{3,2,1,0:T(8,128)(2,1)S(1)} custom-call(s32[6]{0:T(128)S(1)} %stack.19.info_ref, bf16[2,4,128,1280]{3,2,1,0:T(8,128)(2,1)} %get-tuple-element.8.after_ref, bf16[16,1024,128]{2,1,0:T(8,128)(2,1)} %all-to-all-done.1.pieces_ref), custom_call_target="tpu_custom_call" | custom-call | flops 13799999488 | bytes 2097152 | tf_op jit(solution)/shard_map/choose/pallas_call | solution.py:118
  75.1 1.0 collective-permute-start.7
  76.1 0.6 collective-permute-start.6
  76.6 22.4 %collective-permute-done.7.refs_2_ = bf16[2,2,1024,128]{3,2,1,0:T(8,128)(2,1)S(1)} collective-permute-done((bf16[2,2,1024,128]{3,2,1,0:T(8,128)(2,1)S(1)}, bf16[2,2,1024,128]{3,2,1,0:T(8,128)(2,1)S(1)}, u32[]{:S(2)}, u32[]{:S(2)}) %collective-permute-start.7) | collective-permute-done | bytes 1048608 | tf_op jit(solution)/shard_map/ppermute | solution.py:259
  99.1 1.7 %collective-permute-start.10 = (bf16[2,2,1024,128]{3,2,1,0:T(8,128)(2,1)S(1)}, bf16[2,2,1024,128]{3,2,1,0:T(8,128)(2,1)S(1)}, u32[]{:S(2)}, u32[]{:S(2)}) collective-permute-start(bf16[2,2,1024,128]{3,2,1,0:T(8,128)(2,1)S(1)} %choose.1.refs_0_), channel_id=1, source_target_pairs={{0,16},{16,0},{1,17},{17,1},{2,18},{18,2},{3,19},{19,3},{4,20},{20... | collective-permute-start | bytes 3145736 | tf_op jit(solution)/shard_map/ppermute | solution.py:261
  100.8 0.1 collective-permute-done.6.refs_1_
  100.9 2.1 %collective-permute-start.9 = (bf16[2,1024,128]{2,1,0:T(8,128)(2,1)S(1)}, bf16[2,1024,128]{2,1,0:T(8,128)(2,1)S(1)}, u32[]{:S(2)}, u32[]{:S(2)}) collective-permute-start(bf16[2,1024,128]{2,1,0:T(8,128)(2,1)S(1)} %slice_bitcast_fusion), channel_id=1, source_target_pairs={{0,96},{32,0},{64,32},{96,64},{1,97},{33,1},{65,33},{97,65},{2,98}... | collective-permute-start | bytes 1572872 | tf_op jit(solution)/shard_map/ppermute | solution.py:260
  103.0 0.0 collective-permute-done.16
  103.0 0.1 collective-permute-start.8
  103.1 1.9 %collective-permute-done.17 = bf16[2,4,128,1280]{3,2,1,0:T(8,128)(2,1)} collective-permute-done((bf16[2,4,128,1280]{3,2,1,0:T(8,128)(2,1)}, bf16[2,4,128,1280]{3,2,1,0:T(8,128)(2,1)}, u32[]{:S(2)}, u32[]{:S(2)}) %collective-permute-start.17) | collective-permute-done | bytes 2621472 | tf_op jit(solution)/shard_map/ppermute | solution.py:263
  105.0 2.7 %collective-permute-start.12 = (bf16[2,2,1024,128]{3,2,1,0:T(8,128)(2,1)S(1)}, bf16[2,2,1024,128]{3,2,1,0:T(8,128)(2,1)S(1)}, u32[]{:S(2)}, u32[]{:S(2)}) collective-permute-start(bf16[2,2,1024,128]{3,2,1,0:T(8,128)(2,1)S(1)} %collective-permute-done.7.refs_2_), channel_id=1, source_target_pairs={{0,16},{16,0},{1,17},{17,1},{2,18},{18,2},{3,19},{19,3},{4,20},{20... | collective-permute-start | bytes 3145736 | tf_op jit(solution)/shard_map/ppermute | solution.py:261
  107.7 0.0 collective-permute-done.15
  107.7 0.0 collective-permute-start.11
  107.7 6.7 %collective-permute-done.9.refs_4_ = bf16[2,1024,128]{2,1,0:T(8,128)(2,1)S(1)} collective-permute-done((bf16[2,1024,128]{2,1,0:T(8,128)(2,1)S(1)}, bf16[2,1024,128]{2,1,0:T(8,128)(2,1)S(1)}, u32[]{:S(2)}, u32[]{:S(2)}) %collective-permute-start.9) | collective-permute-done | bytes 524320 | tf_op jit(solution)/shard_map/ppermute | solution.py:260
  114.3 0.9 collective-permute-start.14
  115.2 2.3 %collective-permute-done.8.refs_3_ = bf16[2,1024,128]{2,1,0:T(8,128)(2,1)S(1)} collective-permute-done((bf16[2,1024,128]{2,1,0:T(8,128)(2,1)S(1)}, bf16[2,1024,128]{2,1,0:T(8,128)(2,1)S(1)}, u32[]{:S(2)}, u32[]{:S(2)}) %collective-permute-start.8) | collective-permute-done | bytes 524320 | tf_op jit(solution)/shard_map/ppermute | solution.py:260
  117.5 1.1 collective-permute-start.13
  118.6 0.0 collective-permute-done.10.refs_5_
  118.6 1.5 %collective-permute-done.13.refs_8_ = bf16[2,1024,128]{2,1,0:T(8,128)(2,1)S(1)} collective-permute-done((bf16[2,1024,128]{2,1,0:T(8,128)(2,1)S(1)}, bf16[2,1024,128]{2,1,0:T(8,128)(2,1)S(1)}, u32[]{:S(2)}, u32[]{:S(2)}) %collective-permute-start.13) | collective-permute-done | bytes 524320 | tf_op jit(solution)/shard_map/ppermute | solution.py:261
  120.2 18.3 %ladder.1 = f32[1024,1280]{1,0:T(8,128)} custom-call(s32[8,64]{1,0:T(8,128)S(1)} %pad_add_fusion.needs_ref, s32[6]{0:T(128)S(1)} %stack.19.info_ref, bf16[2,2,1024,128]{3,2,1,0:T(8,128)(2,1)S(1)} %choose.1.refs_0_, bf16[2,2,1024,128]{3,2,1,0:T(8,128)(2,1)S(1)} %collective-permute-done.6.refs_1_, ...), custom_call_target="tpu_custom_call" | custom-call | flops 10737418240 | bytes 25165824 | tf_op jit(solution)/shard_map/ladder/pallas_call | solution.py:222
  (12 shorter events, 0.1 us)
Async XLA Ops:
  0.0 6.7 %copy-start = (s32[8,32]{1,0:T(8,128)S(1)}, s32[8,32]{1,0:T(8,128)}, u32[]{:S(2)}) copy-start(s32[8,32]{1,0:T(8,128)} %mask_ref.1) | copy-start | bytes 3076
  2.2 32.1 %collective-permute-start.5 = (bf16[2,2,128,1280]{3,2,1,0:T(8,128)(2,1)S(1)}, bf16[2,2,128,1280]{3,2,1,0:T(8,128)(2,1)S(1)}, u32[]{:S(2)}, u32[]{:S(2)}) collective-permute-start(bf16[2,2,128,1280]{3,2,1,0:T(8,128)(2,1)S(1)} %broadcast_multiply_fusion.refs_0_.refs_10_), channel_id=1, source_target_pairs={{0,12},{1,13},{2,14},{3,15},{4,0},{5,1},{6,2},{7,3},{8,4},{9,5},{1... | collective-permute-start | bytes 3932168 | tf_op jit(solution)/shard_map/ppermute | solution.py:254
  5.6 28.7 %collective-permute-start.4 = (bf16[2,2,128,1280]{3,2,1,0:T(8,128)(2,1)S(1)}, bf16[2,2,128,1280]{3,2,1,0:T(8,128)(2,1)}, u32[]{:S(2)}, u32[]{:S(2)}) collective-permute-start(bf16[2,2,128,1280]{3,2,1,0:T(8,128)(2,1)S(1)} %broadcast_multiply_fusion.refs_0_.refs_10_), channel_id=1, source_target_pairs={{0,8},{1,9},{2,10},{3,11},{4,12},{5,13},{6,14},{7,15},{8,0},{9,1},... | collective-permute-start | bytes 3932168 | tf_op jit(solution)/shard_map/ppermute | solution.py:254
  6.1 32.0 %collective-permute-start.3 = (bf16[2,2,128,1280]{3,2,1,0:T(8,128)(2,1)S(1)}, bf16[2,2,128,1280]{3,2,1,0:T(8,128)(2,1)}, u32[]{:S(2)}, u32[]{:S(2)}) collective-permute-start(bf16[2,2,128,1280]{3,2,1,0:T(8,128)(2,1)S(1)} %broadcast_multiply_fusion.refs_0_.refs_10_), channel_id=1, source_target_pairs={{0,4},{1,5},{2,6},{3,7},{4,8},{5,9},{6,10},{7,11},{8,12},{9,13},{1... | collective-permute-start | bytes 3932168 | tf_op jit(solution)/shard_map/ppermute | solution.py:254
  7.6 11.9 %all-to-all-start = ((s32[8,1,16]{2,1,0:T(1,128)}), s32[8,1,16]{2,1,0:T(1,128)S(1)}, u32[]{:S(2)}, u32[]{:S(2)}) async-start(s32[8,1,16]{2,1,0:T(1,128)} %broadcast_in_dim.9), calls=%async_computation | async-start | bytes 8192 | tf_op jit(solution)/shard_map/all_to_all | solution.py:247
  19.5 9.5 %copy-start.1 = (s32[2]{0:T(128)S(1)}, s32[2]{0:T(128)}, u32[]{:S(2)}) copy-start(s32[2]{0:T(128)} %param.9) | copy-start | bytes 28
  19.5 53.7 %all-to-all-start.1 = ((bf16[16,1024,128]{2,1,0:T(8,128)(2,1)}), bf16[16,1024,128]{2,1,0:T(8,128)(2,1)}, u32[]{:S(2)}, u32[]{:S(2)}) async-start(bf16[16,1024,128]{2,1,0:T(8,128)(2,1)} %compress.1), calls=%async_computation.1 | async-start | bytes 8388608 | tf_op jit(solution)/shard_map/all_to_all | solution.py:257
  24.4 4.2 %collective-permute-start.2 = (s32[8,16]{1,0:T(8,128)S(1)}, s32[8,16]{1,0:T(8,128)S(1)}, u32[]{:S(2)}, u32[]{:S(2)}) collective-permute-start(s32[8,16]{1,0:T(8,128)S(1)} %bitcast.14), channel_id=1, source_target_pairs={{0,1},{1,2},{2,3},{3,0},{4,5},{5,6},{6,7},{7,4},{8,9},{9,10},{10,1... | collective-permute-start | bytes 1544 | tf_op jit(solution)/shard_map/ppermute | solution.py:248
  26.3 4.5 %collective-permute-start.1 = (s32[8,16]{1,0:T(8,128)S(1)}, s32[8,16]{1,0:T(8,128)S(1)}, u32[]{:S(2)}, u32[]{:S(2)}) collective-permute-start(s32[8,16]{1,0:T(8,128)S(1)} %bitcast.15), channel_id=1, source_target_pairs={{0,2},{1,3},{2,0},{3,1},{4,6},{5,7},{6,4},{7,5},{8,10},{9,11},{10,... | collective-permute-start | bytes 1544 | tf_op jit(solution)/shard_map/ppermute | solution.py:248
  28.6 3.0 %collective-permute-start = (s32[8,16]{1,0:T(8,128)S(1)}, s32[8,16]{1,0:T(8,128)S(1)}, u32[]{:S(2)}, u32[]{:S(2)}) collective-permute-start(s32[8,16]{1,0:T(8,128)S(1)} %bitcast.16), channel_id=1, source_target_pairs={{0,3},{1,0},{2,1},{3,2},{4,7},{5,4},{6,5},{7,6},{8,11},{9,8},{10,9... | collective-permute-start | bytes 1544 | tf_op jit(solution)/shard_map/ppermute | solution.py:248
  43.1 59.9 %collective-permute-start.16 = (bf16[2,4,128,1280]{3,2,1,0:T(8,128)(2,1)}, bf16[2,4,128,1280]{3,2,1,0:T(8,128)(2,1)}, u32[]{:S(2)}, u32[]{:S(2)}) collective-permute-start(bf16[2,4,128,1280]{3,2,1,0:T(8,128)(2,1)} %get-tuple-element.9), channel_id=1, source_target_pairs={{0,2},{1,3},{2,0},{3,1},{4,6},{5,7},{6,4},{7,5},{8,10},{9,11},{10,... | collective-permute-start | bytes 7864328 | tf_op jit(solution)/shard_map/ppermute | solution.py:263
  46.7 58.3 %collective-permute-start.17 = (bf16[2,4,128,1280]{3,2,1,0:T(8,128)(2,1)}, bf16[2,4,128,1280]{3,2,1,0:T(8,128)(2,1)}, u32[]{:S(2)}, u32[]{:S(2)}) collective-permute-start(bf16[2,4,128,1280]{3,2,1,0:T(8,128)(2,1)} %get-tuple-element.10), channel_id=1, source_target_pairs={{0,3},{1,0},{2,1},{3,2},{4,7},{5,4},{6,5},{7,6},{8,11},{9,8},{10,9... | collective-permute-start | bytes 7864328 | tf_op jit(solution)/shard_map/ppermute | solution.py:263
  47.2 60.5 %collective-permute-start.15 = (bf16[2,4,128,1280]{3,2,1,0:T(8,128)(2,1)}, bf16[2,4,128,1280]{3,2,1,0:T(8,128)(2,1)}, u32[]{:S(2)}, u32[]{:S(2)}) collective-permute-start(bf16[2,4,128,1280]{3,2,1,0:T(8,128)(2,1)} %get-tuple-element.8.after_ref), channel_id=1, source_target_pairs={{0,1},{1,2},{2,3},{3,0},{4,5},{5,6},{6,7},{7,4},{8,9},{9,10},{10,1... | collective-permute-start | bytes 7864328 | tf_op jit(solution)/shard_map/ppermute | solution.py:263
  75.1 24.0 %collective-permute-start.7 = (bf16[2,2,1024,128]{3,2,1,0:T(8,128)(2,1)S(1)}, bf16[2,2,1024,128]{3,2,1,0:T(8,128)(2,1)S(1)}, u32[]{:S(2)}, u32[]{:S(2)}) collective-permute-start(bf16[2,2,1024,128]{3,2,1,0:T(8,128)(2,1)S(1)} %choose.1.refs_0_), channel_id=1, source_target_pairs={{0,96},{32,0},{64,32},{96,64},{1,97},{33,1},{65,33},{97,65},{2,98}... | collective-permute-start | bytes 3145736 | tf_op jit(solution)/shard_map/ppermute | solution.py:259
  76.1 24.8 %collective-permute-start.6 = (bf16[2,2,1024,128]{3,2,1,0:T(8,128)(2,1)S(1)}, bf16[2,2,1024,128]{3,2,1,0:T(8,128)(2,1)S(1)}, u32[]{:S(2)}, u32[]{:S(2)}) collective-permute-start(bf16[2,2,1024,128]{3,2,1,0:T(8,128)(2,1)S(1)} %choose.1.refs_0_), channel_id=1, source_target_pairs={{0,32},{32,64},{64,96},{96,0},{1,33},{33,65},{65,97},{97,1},{2,34}... | collective-permute-start | bytes 3145736 | tf_op jit(solution)/shard_map/ppermute | solution.py:259
  99.1 19.6 %collective-permute-start.10 = (bf16[2,2,1024,128]{3,2,1,0:T(8,128)(2,1)S(1)}, bf16[2,2,1024,128]{3,2,1,0:T(8,128)(2,1)S(1)}, u32[]{:S(2)}, u32[]{:S(2)}) collective-permute-start(bf16[2,2,1024,128]{3,2,1,0:T(8,128)(2,1)S(1)} %choose.1.refs_0_), channel_id=1, source_target_pairs={{0,16},{16,0},{1,17},{17,1},{2,18},{18,2},{3,19},{19,3},{4,20},{20... | collective-permute-start | bytes 3145736 | tf_op jit(solution)/shard_map/ppermute | solution.py:261
  100.9 13.4 %collective-permute-start.9 = (bf16[2,1024,128]{2,1,0:T(8,128)(2,1)S(1)}, bf16[2,1024,128]{2,1,0:T(8,128)(2,1)S(1)}, u32[]{:S(2)}, u32[]{:S(2)}) collective-permute-start(bf16[2,1024,128]{2,1,0:T(8,128)(2,1)S(1)} %slice_bitcast_fusion), channel_id=1, source_target_pairs={{0,96},{32,0},{64,32},{96,64},{1,97},{33,1},{65,33},{97,65},{2,98}... | collective-permute-start | bytes 1572872 | tf_op jit(solution)/shard_map/ppermute | solution.py:260
  103.0 14.5 %collective-permute-start.8 = (bf16[2,1024,128]{2,1,0:T(8,128)(2,1)S(1)}, bf16[2,1024,128]{2,1,0:T(8,128)(2,1)S(1)}, u32[]{:S(2)}, u32[]{:S(2)}) collective-permute-start(bf16[2,1024,128]{2,1,0:T(8,128)(2,1)S(1)} %slice_bitcast_fusion.1), channel_id=1, source_target_pairs={{0,32},{32,64},{64,96},{96,0},{1,33},{33,65},{65,97},{97,1},{2,34}... | collective-permute-start | bytes 1572872 | tf_op jit(solution)/shard_map/ppermute | solution.py:260
  105.0 15.2 %collective-permute-start.12 = (bf16[2,2,1024,128]{3,2,1,0:T(8,128)(2,1)S(1)}, bf16[2,2,1024,128]{3,2,1,0:T(8,128)(2,1)S(1)}, u32[]{:S(2)}, u32[]{:S(2)}) collective-permute-start(bf16[2,2,1024,128]{3,2,1,0:T(8,128)(2,1)S(1)} %collective-permute-done.7.refs_2_), channel_id=1, source_target_pairs={{0,16},{16,0},{1,17},{17,1},{2,18},{18,2},{3,19},{19,3},{4,20},{20... | collective-permute-start | bytes 3145736 | tf_op jit(solution)/shard_map/ppermute | solution.py:261
  107.7 12.5 %collective-permute-start.11 = (bf16[2,2,1024,128]{3,2,1,0:T(8,128)(2,1)S(1)}, bf16[2,2,1024,128]{3,2,1,0:T(8,128)(2,1)S(1)}, u32[]{:S(2)}, u32[]{:S(2)}) collective-permute-start(bf16[2,2,1024,128]{3,2,1,0:T(8,128)(2,1)S(1)} %collective-permute-done.6.refs_1_), channel_id=1, source_target_pairs={{0,16},{16,0},{1,17},{17,1},{2,18},{18,2},{3,19},{19,3},{4,20},{20... | collective-permute-start | bytes 3145736 | tf_op jit(solution)/shard_map/ppermute | solution.py:261
  114.3 4.3 %collective-permute-start.14 = (bf16[2,1024,128]{2,1,0:T(8,128)(2,1)S(1)}, bf16[2,1024,128]{2,1,0:T(8,128)(2,1)S(1)}, u32[]{:S(2)}, u32[]{:S(2)}) collective-permute-start(bf16[2,1024,128]{2,1,0:T(8,128)(2,1)S(1)} %collective-permute-done.9.refs_4_), channel_id=1, source_target_pairs={{0,16},{16,0},{1,17},{17,1},{2,18},{18,2},{3,19},{19,3},{4,20},{20... | collective-permute-start | bytes 1572872 | tf_op jit(solution)/shard_map/ppermute | solution.py:261
  117.5 2.6 %collective-permute-start.13 = (bf16[2,1024,128]{2,1,0:T(8,128)(2,1)S(1)}, bf16[2,1024,128]{2,1,0:T(8,128)(2,1)S(1)}, u32[]{:S(2)}, u32[]{:S(2)}) collective-permute-start(bf16[2,1024,128]{2,1,0:T(8,128)(2,1)S(1)} %collective-permute-done.8.refs_3_), channel_id=1, source_target_pairs={{0,16},{16,0},{1,17},{17,1},{2,18},{18,2},{3,19},{19,3},{4,20},{20... | collective-permute-start | bytes 1572872 | tf_op jit(solution)/shard_map/ppermute | solution.py:261

commit v6 on v5

--- a/solution.py
+++ b/solution.py
@@ -96,36 +96,6 @@
         compiler_params=pltpu.CompilerParams(vmem_limit_bytes=54 << 20),
         name="compress",
     )(amp_mask, amplitudes)
-
-
-def choose_kernel(info_ref, after_ref, pieces_ref, out_ref, held, in_sems, out_sems):
-    each = held.shape[1]
-    loads = [pltpu.make_async_copy(pieces_ref.at[pl.ds(info_ref[step] * each, each)], held.at[step], in_sems.at[step])
-             for step in range(STEPS)]
-    stores = [pltpu.make_async_copy(held.at[step], out_ref.at[step], out_sems.at[step]) for step in range(STEPS)]
-    for load in loads:
-        load.start()
-    for load, store in zip(loads, stores):
-        load.wait()
-        store.start()
-    for store in stores:
-        store.wait()
-
-
-def choose(info, after, pieces):
-    groups, rows, _ = pieces.shape
-    shape = (STEPS, groups // ROWS, rows, TW)
-    return pl.pallas_call(
-        choose_kernel,
-        in_specs=[pl.BlockSpec(memory_space=pltpu.SMEM)] + [pl.BlockSpec(memory_space=pl.ANY)] * 2,
-        out_specs=pl.BlockSpec(memory_space=pl.ANY),
-        out_shape=jax.ShapeDtypeStruct(shape, pieces.dtype),
-        scratch_shapes=[pltpu.VMEM(shape, pieces.dtype),
-                        pltpu.SemaphoreType.DMA((STEPS,)), pltpu.SemaphoreType.DMA((STEPS,))],
-        compiler_params=pltpu.CompilerParams(vmem_limit_bytes=4 << 20),
-        cost_estimate=pl.CostEstimate(flops=13800000000, bytes_accessed=2 << 20, transcendentals=0),
-        name="choose",
-    )(info, after, pieces)
 
 
 def pick_kernel(needs_ref, info_ref, *refs):
@@ -255,7 +225,8 @@
 
     sent = pick(needs, info, held)
     pieces = lax.all_to_all(compress(amplitudes, amp_mask), ROW, 0, 0, tiled=True)
-    halves = [choose(info, sent[0], pieces)]
+    each = pieces.shape[0] // ROWS
+    halves = [jnp.stack([lax.dynamic_slice_in_dim(pieces, steps[step] * each, each, 0) for step in range(STEPS)])]
     halves += [lax.ppermute(halves[0], "y", round_y(shift)) for shift in (1, 3)]
     halves += [lax.ppermute(halves[1][0], "y", round_y(1)), lax.ppermute(halves[2][1], "y", round_y(3))]
     halves += [lax.ppermute(half, "core", [(0, 1), (1, 0)]) for half in halves]

time: 139 us -> 139 us (level)
  waiting for transfers between devices: 70.2 us -> 67.9 us
  Pallas kernels: 30.2 us -> 28.3 us
  local copies, waits for them, and re-layouts: 1.13 us -> 3 us
    all_to_all x1, waiting for transfers between devices: 25.2 us -> 22.8 us  [local(): lax.all_to_all(compress(amplitudes, amp_mask), ROW, 0, 0, tiled=True)]
    pallas_call x1 -> x0, Pallas kernels: 1.82 us -> none  [choose(): pl.pallas_call(choose_kernel, in_specs=[pl.BlockSpec(memory_space=pltpu.S...]
  transfers between devices with their start and end apart: 20 -> 20, of which waited for: 12 -> 12; matrix products, arithmetic and copies ran while one was open for 1% -> 2% of each run, Pallas kernels for 9% -> 7%
where the time goes in v6:
time: 139 us; the launch traced here: 138 us
  waiting for transfers between devices  67.9 us (49%)
  starting transfers between devices  35.1 us (25%)
  Pallas kernels  28.3 us (20%)
  local copies, waits for them, and re-layouts  3 us (2%)
  other arithmetic  2.3 us (2%)
  between operations  1.47 us (1%)
    all_to_all x1, waiting for transfers between devices, local(): lax.all_to_all(compress(amplitudes, amp_mask), ROW, 0, 0, tiled=True)  22.8 us
    ppermute x2, waiting for transfers between devices, local(): halves += [lax.ppermute(halves[0], 'y', round_y(shift)) for shift in (1, 3)]  22.5 us
    pallas_call x1, Pallas kernels, multiply(): pl.pallas_call(ladder_kernel, in_specs=[pl.BlockSpec(memory_space=pltpu.S...  18.3 us
    all_to_all x1, starting transfers between devices, local(): lax.all_to_all(jnp.broadcast_to(own, (ROWS, own.shape[1])), ROW, 0, 0, ti...  6.83 us
    ppermute x3, waiting for transfers between devices, local(): lax.ppermute(block, GRID, plane_perm(True, shift))  6.52 us
    ppermute x5, starting transfers between devices, local(): halves += [lax.ppermute(half, 'core', [(0, 1), (1, 0)]) for half in halves]  6.34 us
    ppermute x1, waiting for transfers between devices, local(): lax.ppermute(halves[2][1], 'y', round_y(3))  5.64 us
    ppermute x3, starting transfers between devices, local(): lax.ppermute(sent[shift - 1], GRID, plane_perm(False, shift))  5.58 us
  transfers between devices with their start and end apart: 20, of which 12 were waited for; matrix products, arithmetic and copies ran while one was open for 2% of the time, Pallas kernels for 7%

profile of v6, /device:TPU:1, one launch (start us, length us, event | category | flops | bytes accessed | tf_op | source)
XLA Modules:
  0.0 138.2 jit_solution(13464890677233925631)
XLA Ops:
  0.0 0.7 convert_element_type.3
  0.7 0.1 mul.33
  0.8 1.4 %broadcast_multiply_fusion.refs_0_.refs_10_ = bf16[2,2,128,1280]{3,2,1,0:T(8,128)(2,1)S(1)} fusion(bf16[2,2,128,1280]{3,2,1,0:T(8,128)(2,1)} %bitcast.19, bf16[2,2,1280]{2,1,0:T(2,128)(2,1)S(1)} %mul.34), kind=kLoop, calls=%fused_computation.1 | loop fusion | flops 655360 | bytes 2631680 | tf_op jit(solution)/shard_map/mul | solution.py:222
  2.2 3.4 %collective-permute-start.14 = (bf16[2,2,128,1280]{3,2,1,0:T(8,128)(2,1)S(1)}, bf16[2,2,128,1280]{3,2,1,0:T(8,128)(2,1)S(1)}, u32[]{:S(2)}, u32[]{:S(2)}) collective-permute-start(bf16[2,2,128,1280]{3,2,1,0:T(8,128)(2,1)S(1)} %broadcast_multiply_fusion.refs_0_.refs_10_), channel_id=1, source_target_pairs={{0,12},{1,13},{2,14},{3,15},{4,0},{5,1},{6,2},{7,3},{8,4},{9,5},{1... | collective-permute-start | bytes 3932168 | tf_op jit(solution)/shard_map/ppermute | solution.py:224
  5.6 0.5 collective-permute-start.13
  6.1 0.6 collective-permute-start.12
  6.7 0.1 reshape.31
  6.8 0.2 slice_reduce_fusion
  7.0 0.6 broadcast_in_dim.9
  7.6 6.8 %all-to-all-start = ((s32[8,1,16]{2,1,0:T(1,128)}), s32[8,1,16]{2,1,0:T(1,128)S(1)}, u32[]{:S(2)}, u32[]{:S(2)}) async-start(s32[8,1,16]{2,1,0:T(1,128)} %broadcast_in_dim.9), calls=%async_computation | async-start | bytes 8192 | tf_op jit(solution)/shard_map/all_to_all | solution.py:217
  14.4 5.0 %compress.1 = bf16[16,1024,128]{2,1,0:T(8,128)(2,1)} custom-call(s32[8,32]{1,0:T(8,128)} %mask_ref.1, bf16[1024,4096]{1,0:T(8,128)(2,1)} %amp_ref.1), custom_call_target="tpu_custom_call" | custom-call | tf_op jit(solution)/shard_map/compress/pallas_call | solution.py:89
  19.5 0.0 copy-start.1
  19.5 0.0 all-to-all-done
  19.5 4.8 %all-to-all-start.1 = ((bf16[16,1024,128]{2,1,0:T(8,128)(2,1)}), bf16[16,1024,128]{2,1,0:T(8,128)(2,1)}, u32[]{:S(2)}, u32[]{:S(2)}) async-start(bf16[16,1024,128]{2,1,0:T(8,128)(2,1)} %compress.1), calls=%async_computation.1 | async-start | bytes 8388608 | tf_op jit(solution)/shard_map/all_to_all | solution.py:227
  24.4 1.9 %collective-permute-start.2 = (s32[8,16]{1,0:T(8,128)S(1)}, s32[8,16]{1,0:T(8,128)S(1)}, u32[]{:S(2)}, u32[]{:S(2)}) collective-permute-start(s32[8,16]{1,0:T(8,128)S(1)} %bitcast.20), channel_id=1, source_target_pairs={{0,1},{1,2},{2,3},{3,0},{4,5},{5,6},{6,7},{7,4},{8,9},{9,10},{10,1... | collective-permute-start | bytes 1544 | tf_op jit(solution)/shard_map/ppermute | solution.py:218
  26.3 0.9 collective-permute-start.1
  27.2 1.3 collective-permute-done.2
  28.5 0.5 collective-permute-start
  29.0 0.1 stack.28.info_ref
  29.1 1.7 %collective-permute-done.1 = s32[8,16]{1,0:T(8,128)S(1)} collective-permute-done((s32[8,16]{1,0:T(8,128)S(1)}, s32[8,16]{1,0:T(8,128)S(1)}, u32[]{:S(2)}, u32[]{:S(2)}) %collective-permute-start.1) | collective-permute-done | bytes 544 | tf_op jit(solution)/shard_map/ppermute | solution.py:218
  30.8 0.7 collective-permute-done
  31.5 0.1 pad_add_fusion.needs_ref
  31.6 2.7 %collective-permute-done.14.refs_3_.refs_13_ = bf16[2,2,128,1280]{3,2,1,0:T(8,128)(2,1)S(1)} collective-permute-done((bf16[2,2,128,1280]{3,2,1,0:T(8,128)(2,1)S(1)}, bf16[2,2,128,1280]{3,2,1,0:T(8,128)(2,1)S(1)}, u32[]{:S(2)}, u32[]{:S(2)}) %collective-permute-start.14) | collective-permute-done | bytes 1310752 | tf_op jit(solution)/shard_map/ppermute | solution.py:224
  34.3 3.8 %collective-permute-done.12.refs_1_.refs_11_ = bf16[2,2,128,1280]{3,2,1,0:T(8,128)(2,1)} collective-permute-done((bf16[2,2,128,1280]{3,2,1,0:T(8,128)(2,1)S(1)}, bf16[2,2,128,1280]{3,2,1,0:T(8,128)(2,1)}, u32[]{:S(2)}, u32[]{:S(2)}) %collective-permute-start.12) | collective-permute-done | bytes 1310752 | tf_op jit(solution)/shard_map/ppermute | solution.py:224
  38.1 5.0 %pick.1 = (bf16[2,4,128,1280]{3,2,1,0:T(8,128)(2,1)}, bf16[2,4,128,1280]{3,2,1,0:T(8,128)(2,1)}, bf16[2,4,128,1280]{3,2,1,0:T(8,128)(2,1)}) custom-call(s32[8,64]{1,0:T(8,128)S(1)} %pad_add_fusion.needs_ref, s32[6]{0:T(128)S(1)} %stack.28.info_ref, bf16[2,2,128,1280]{3,2,1,0:T(8,128)(2,1)S(1)} %broadcast_multiply_fusion.refs_0_.refs_10_, ...), custom_call_target="tpu_custom_call" | custom-call | flops 27599998976 | bytes 8388608 | tf_op jit(solution)/shard_map/pick/pallas_call | solution.py:120
  43.1 1.7 %collective-permute-start.15 = (bf16[2,4,128,1280]{3,2,1,0:T(8,128)(2,1)}, bf16[2,4,128,1280]{3,2,1,0:T(8,128)(2,1)}, u32[]{:S(2)}, u32[]{:S(2)}) collective-permute-start(bf16[2,4,128,1280]{3,2,1,0:T(8,128)(2,1)} %get-tuple-element.8), channel_id=1, source_target_pairs={{0,1},{1,2},{2,3},{3,0},{4,5},{5,6},{6,7},{7,4},{8,9},{9,10},{10,1... | collective-permute-start | bytes 7864328 | tf_op jit(solution)/shard_map/ppermute | solution.py:234
  44.8 3.0 %collective-permute-start.16 = (bf16[2,4,128,1280]{3,2,1,0:T(8,128)(2,1)}, bf16[2,4,128,1280]{3,2,1,0:T(8,128)(2,1)}, u32[]{:S(2)}, u32[]{:S(2)}) collective-permute-start(bf16[2,4,128,1280]{3,2,1,0:T(8,128)(2,1)} %get-tuple-element.9), channel_id=1, source_target_pairs={{0,2},{1,3},{2,0},{3,1},{4,6},{5,7},{6,4},{7,5},{8,10},{9,11},{10,... | collective-permute-start | bytes 7864328 | tf_op jit(solution)/shard_map/ppermute | solution.py:234
  47.8 0.9 collective-permute-start.17
  48.7 0.6 fusion
  50.5 22.8 %all-to-all-done.1 = bf16[16,1024,128]{2,1,0:T(8,128)(2,1)} async-done(((bf16[16,1024,128]{2,1,0:T(8,128)(2,1)}), bf16[16,1024,128]{2,1,0:T(8,128)(2,1)}, u32[]{:S(2)}, u32[]{:S(2)}) %all-to-all-start.1) | async-done | bytes 4194336 | tf_op jit(solution)/shard_map/all_to_all | solution.py:227
  73.3 1.3 dynamic-slice_bitcast_fusion.1
  74.5 0.1 pad_maximum_fusion.refs_0_
  74.7 1.0 collective-permute-start.4
  75.6 0.6 collective-permute-start.3
  76.2 22.4 %collective-permute-done.4.refs_2_ = bf16[2,2,1024,128]{3,2,1,0:T(8,128)(2,1)S(1)} collective-permute-done((bf16[2,2,1024,128]{3,2,1,0:T(8,128)(2,1)S(1)}, bf16[2,2,1024,128]{3,2,1,0:T(8,128)(2,1)S(1)}, u32[]{:S(2)}, u32[]{:S(2)}) %collective-permute-start.4) | collective-permute-done | bytes 1048608 | tf_op jit(solution)/shard_map/ppermute | solution.py:230
  98.6 1.7 %collective-permute-start.7 = (bf16[2,2,1024,128]{3,2,1,0:T(8,128)(2,1)S(1)}, bf16[2,2,1024,128]{3,2,1,0:T(8,128)(2,1)S(1)}, u32[]{:S(2)}, u32[]{:S(2)}) collective-permute-start(bf16[2,2,1024,128]{3,2,1,0:T(8,128)(2,1)S(1)} %pad_maximum_fusion.refs_0_), channel_id=1, source_target_pairs={{0,16},{16,0},{1,17},{17,1},{2,18},{18,2},{3,19},{19,3},{4,20},{20... | collective-permute-start | bytes 3145736 | tf_op jit(solution)/shard_map/ppermute | solution.py:232
  100.3 0.1 collective-permute-done.3.refs_1_
  100.4 2.1 %collective-permute-start.6 = (bf16[2,1024,128]{2,1,0:T(8,128)(2,1)S(1)}, bf16[2,1024,128]{2,1,0:T(8,128)(2,1)S(1)}, u32[]{:S(2)}, u32[]{:S(2)}) collective-permute-start(bf16[2,1024,128]{2,1,0:T(8,128)(2,1)S(1)} %slice_bitcast_fusion), channel_id=1, source_target_pairs={{0,96},{32,0},{64,32},{96,64},{1,97},{33,1},{65,33},{97,65},{2,98}... | collective-permute-start | bytes 1572872 | tf_op jit(solution)/shard_map/ppermute | solution.py:231
  102.6 0.1 collective-permute-start.5
  102.6 2.9 %collective-permute-done.16 = bf16[2,4,128,1280]{3,2,1,0:T(8,128)(2,1)} collective-permute-done((bf16[2,4,128,1280]{3,2,1,0:T(8,128)(2,1)}, bf16[2,4,128,1280]{3,2,1,0:T(8,128)(2,1)}, u32[]{:S(2)}, u32[]{:S(2)}) %collective-permute-start.16) | collective-permute-done | bytes 2621472 | tf_op jit(solution)/shard_map/ppermute | solution.py:234
  105.6 2.7 %collective-permute-start.9 = (bf16[2,2,1024,128]{3,2,1,0:T(8,128)(2,1)S(1)}, bf16[2,2,1024,128]{3,2,1,0:T(8,128)(2,1)S(1)}, u32[]{:S(2)}, u32[]{:S(2)}) collective-permute-start(bf16[2,2,1024,128]{3,2,1,0:T(8,128)(2,1)S(1)} %collective-permute-done.4.refs_2_), channel_id=1, source_target_pairs={{0,16},{16,0},{1,17},{17,1},{2,18},{18,2},{3,19},{19,3},{4,20},{20... | collective-permute-start | bytes 3145736 | tf_op jit(solution)/shard_map/ppermute | solution.py:232
  108.2 0.0 collective-permute-start.8
  108.2 5.6 %collective-permute-done.6.refs_4_ = bf16[2,1024,128]{2,1,0:T(8,128)(2,1)S(1)} collective-permute-done((bf16[2,1024,128]{2,1,0:T(8,128)(2,1)S(1)}, bf16[2,1024,128]{2,1,0:T(8,128)(2,1)S(1)}, u32[]{:S(2)}, u32[]{:S(2)}) %collective-permute-start.6) | collective-permute-done | bytes 524320 | tf_op jit(solution)/shard_map/ppermute | solution.py:231
  113.9 0.9 collective-permute-start.11
  114.8 2.3 %collective-permute-done.5.refs_3_ = bf16[2,1024,128]{2,1,0:T(8,128)(2,1)S(1)} collective-permute-done((bf16[2,1024,128]{2,1,0:T(8,128)(2,1)S(1)}, bf16[2,1024,128]{2,1,0:T(8,128)(2,1)S(1)}, u32[]{:S(2)}, u32[]{:S(2)}) %collective-permute-start.5) | collective-permute-done | bytes 524320 | tf_op jit(solution)/shard_map/ppermute | solution.py:231
  117.1 1.1 collective-permute-start.10
  118.2 1.5 %collective-permute-done.10.refs_8_ = bf16[2,1024,128]{2,1,0:T(8,128)(2,1)S(1)} collective-permute-done((bf16[2,1024,128]{2,1,0:T(8,128)(2,1)S(1)}, bf16[2,1024,128]{2,1,0:T(8,128)(2,1)S(1)}, u32[]{:S(2)}, u32[]{:S(2)}) %collective-permute-start.10) | collective-permute-done | bytes 524320 | tf_op jit(solution)/shard_map/ppermute | solution.py:232
  119.7 18.3 %ladder.1 = f32[1024,1280]{1,0:T(8,128)} custom-call(s32[8,64]{1,0:T(8,128)S(1)} %pad_add_fusion.needs_ref, s32[6]{0:T(128)S(1)} %stack.28.info_ref, bf16[2,2,1024,128]{3,2,1,0:T(8,128)(2,1)S(1)} %pad_maximum_fusion.refs_0_, bf16[2,2,1024,128]{3,2,1,0:T(8,128)(2,1)S(1)} %collective-permute-done.3.refs_1_, ...), custom_call_target="tpu_custom_call" | custom-call | flops 10737418240 | bytes 25165824 | tf_op jit(solution)/shard_map/ladder/pallas_call | solution.py:192
  (14 shorter events, 0.1 us)
Async XLA Ops:
  0.0 6.7 %copy-start = (s32[8,32]{1,0:T(8,128)S(1)}, s32[8,32]{1,0:T(8,128)}, u32[]{:S(2)}) copy-start(s32[8,32]{1,0:T(8,128)} %mask_ref.1) | copy-start | bytes 3076
  2.2 32.1 %collective-permute-start.14 = (bf16[2,2,128,1280]{3,2,1,0:T(8,128)(2,1)S(1)}, bf16[2,2,128,1280]{3,2,1,0:T(8,128)(2,1)S(1)}, u32[]{:S(2)}, u32[]{:S(2)}) collective-permute-start(bf16[2,2,128,1280]{3,2,1,0:T(8,128)(2,1)S(1)} %broadcast_multiply_fusion.refs_0_.refs_10_), channel_id=1, source_target_pairs={{0,12},{1,13},{2,14},{3,15},{4,0},{5,1},{6,2},{7,3},{8,4},{9,5},{1... | collective-permute-start | bytes 3932168 | tf_op jit(solution)/shard_map/ppermute | solution.py:224
  5.6 28.7 %collective-permute-start.13 = (bf16[2,2,128,1280]{3,2,1,0:T(8,128)(2,1)S(1)}, bf16[2,2,128,1280]{3,2,1,0:T(8,128)(2,1)}, u32[]{:S(2)}, u32[]{:S(2)}) collective-permute-start(bf16[2,2,128,1280]{3,2,1,0:T(8,128)(2,1)S(1)} %broadcast_multiply_fusion.refs_0_.refs_10_), channel_id=1, source_target_pairs={{0,8},{1,9},{2,10},{3,11},{4,12},{5,13},{6,14},{7,15},{8,0},{9,1},... | collective-permute-start | bytes 3932168 | tf_op jit(solution)/shard_map/ppermute | solution.py:224
  6.1 32.0 %collective-permute-start.12 = (bf16[2,2,128,1280]{3,2,1,0:T(8,128)(2,1)S(1)}, bf16[2,2,128,1280]{3,2,1,0:T(8,128)(2,1)}, u32[]{:S(2)}, u32[]{:S(2)}) collective-permute-start(bf16[2,2,128,1280]{3,2,1,0:T(8,128)(2,1)S(1)} %broadcast_multiply_fusion.refs_0_.refs_10_), channel_id=1, source_target_pairs={{0,4},{1,5},{2,6},{3,7},{4,8},{5,9},{6,10},{7,11},{8,12},{9,13},{1... | collective-permute-start | bytes 3932168 | tf_op jit(solution)/shard_map/ppermute | solution.py:224
  7.6 11.9 %all-to-all-start = ((s32[8,1,16]{2,1,0:T(1,128)}), s32[8,1,16]{2,1,0:T(1,128)S(1)}, u32[]{:S(2)}, u32[]{:S(2)}) async-start(s32[8,1,16]{2,1,0:T(1,128)} %broadcast_in_dim.9), calls=%async_computation | async-start | bytes 8192 | tf_op jit(solution)/shard_map/all_to_all | solution.py:217
  19.5 9.5 %copy-start.1 = (s32[2]{0:T(128)S(1)}, s32[2]{0:T(128)}, u32[]{:S(2)}) copy-start(s32[2]{0:T(128)} %param.9) | copy-start | bytes 28
  19.5 53.8 %all-to-all-start.1 = ((bf16[16,1024,128]{2,1,0:T(8,128)(2,1)}), bf16[16,1024,128]{2,1,0:T(8,128)(2,1)}, u32[]{:S(2)}, u32[]{:S(2)}) async-start(bf16[16,1024,128]{2,1,0:T(8,128)(2,1)} %compress.1), calls=%async_computation.1 | async-start | bytes 8388608 | tf_op jit(solution)/shard_map/all_to_all | solution.py:227
  24.4 4.2 %collective-permute-start.2 = (s32[8,16]{1,0:T(8,128)S(1)}, s32[8,16]{1,0:T(8,128)S(1)}, u32[]{:S(2)}, u32[]{:S(2)}) collective-permute-start(s32[8,16]{1,0:T(8,128)S(1)} %bitcast.20), channel_id=1, source_target_pairs={{0,1},{1,2},{2,3},{3,0},{4,5},{5,6},{6,7},{7,4},{8,9},{9,10},{10,1... | collective-permute-start | bytes 1544 | tf_op jit(solution)/shard_map/ppermute | solution.py:218
  26.3 4.5 %collective-permute-start.1 = (s32[8,16]{1,0:T(8,128)S(1)}, s32[8,16]{1,0:T(8,128)S(1)}, u32[]{:S(2)}, u32[]{:S(2)}) collective-permute-start(s32[8,16]{1,0:T(8,128)S(1)} %bitcast.21), channel_id=1, source_target_pairs={{0,2},{1,3},{2,0},{3,1},{4,6},{5,7},{6,4},{7,5},{8,10},{9,11},{10,... | collective-permute-start | bytes 1544 | tf_op jit(solution)/shard_map/ppermute | solution.py:218
  28.5 3.0 %collective-permute-start = (s32[8,16]{1,0:T(8,128)S(1)}, s32[8,16]{1,0:T(8,128)S(1)}, u32[]{:S(2)}, u32[]{:S(2)}) collective-permute-start(s32[8,16]{1,0:T(8,128)S(1)} %bitcast.22), channel_id=1, source_target_pairs={{0,3},{1,0},{2,1},{3,2},{4,7},{5,4},{6,5},{7,6},{8,11},{9,8},{10,9... | collective-permute-start | bytes 1544 | tf_op jit(solution)/shard_map/ppermute | solution.py:218
  43.1 59.4 %collective-permute-start.15 = (bf16[2,4,128,1280]{3,2,1,0:T(8,128)(2,1)}, bf16[2,4,128,1280]{3,2,1,0:T(8,128)(2,1)}, u32[]{:S(2)}, u32[]{:S(2)}) collective-permute-start(bf16[2,4,128,1280]{3,2,1,0:T(8,128)(2,1)} %get-tuple-element.8), channel_id=1, source_target_pairs={{0,1},{1,2},{2,3},{3,0},{4,5},{5,6},{6,7},{7,4},{8,9},{9,10},{10,1... | collective-permute-start | bytes 7864328 | tf_op jit(solution)/shard_map/ppermute | solution.py:234
  44.8 60.7 %collective-permute-start.16 = (bf16[2,4,128,1280]{3,2,1,0:T(8,128)(2,1)}, bf16[2,4,128,1280]{3,2,1,0:T(8,128)(2,1)}, u32[]{:S(2)}, u32[]{:S(2)}) collective-permute-start(bf16[2,4,128,1280]{3,2,1,0:T(8,128)(2,1)} %get-tuple-element.9), channel_id=1, source_target_pairs={{0,2},{1,3},{2,0},{3,1},{4,6},{5,7},{6,4},{7,5},{8,10},{9,11},{10,... | collective-permute-start | bytes 7864328 | tf_op jit(solution)/shard_map/ppermute | solution.py:234
  47.8 60.4 %collective-permute-start.17 = (bf16[2,4,128,1280]{3,2,1,0:T(8,128)(2,1)}, bf16[2,4,128,1280]{3,2,1,0:T(8,128)(2,1)}, u32[]{:S(2)}, u32[]{:S(2)}) collective-permute-start(bf16[2,4,128,1280]{3,2,1,0:T(8,128)(2,1)} %get-tuple-element.10), channel_id=1, source_target_pairs={{0,3},{1,0},{2,1},{3,2},{4,7},{5,4},{6,5},{7,6},{8,11},{9,8},{10,9... | collective-permute-start | bytes 7864328 | tf_op jit(solution)/shard_map/ppermute | solution.py:234
  74.7 24.0 %collective-permute-start.4 = (bf16[2,2,1024,128]{3,2,1,0:T(8,128)(2,1)S(1)}, bf16[2,2,1024,128]{3,2,1,0:T(8,128)(2,1)S(1)}, u32[]{:S(2)}, u32[]{:S(2)}) collective-permute-start(bf16[2,2,1024,128]{3,2,1,0:T(8,128)(2,1)S(1)} %pad_maximum_fusion.refs_0_), channel_id=1, source_target_pairs={{0,96},{32,0},{64,32},{96,64},{1,97},{33,1},{65,33},{97,65},{2,98}... | collective-permute-start | bytes 3145736 | tf_op jit(solution)/shard_map/ppermute | solution.py:230
  75.6 24.8 %collective-permute-start.3 = (bf16[2,2,1024,128]{3,2,1,0:T(8,128)(2,1)S(1)}, bf16[2,2,1024,128]{3,2,1,0:T(8,128)(2,1)S(1)}, u32[]{:S(2)}, u32[]{:S(2)}) collective-permute-start(bf16[2,2,1024,128]{3,2,1,0:T(8,128)(2,1)S(1)} %pad_maximum_fusion.refs_0_), channel_id=1, source_target_pairs={{0,32},{32,64},{64,96},{96,0},{1,33},{33,65},{65,97},{97,1},{2,34}... | collective-permute-start | bytes 3145736 | tf_op jit(solution)/shard_map/ppermute | solution.py:230
  98.6 19.6 %collective-permute-start.7 = (bf16[2,2,1024,128]{3,2,1,0:T(8,128)(2,1)S(1)}, bf16[2,2,1024,128]{3,2,1,0:T(8,128)(2,1)S(1)}, u32[]{:S(2)}, u32[]{:S(2)}) collective-permute-start(bf16[2,2,1024,128]{3,2,1,0:T(8,128)(2,1)S(1)} %pad_maximum_fusion.refs_0_), channel_id=1, source_target_pairs={{0,16},{16,0},{1,17},{17,1},{2,18},{18,2},{3,19},{19,3},{4,20},{20... | collective-permute-start | bytes 3145736 | tf_op jit(solution)/shard_map/ppermute | solution.py:232
  100.4 13.4 %collective-permute-start.6 = (bf16[2,1024,128]{2,1,0:T(8,128)(2,1)S(1)}, bf16[2,1024,128]{2,1,0:T(8,128)(2,1)S(1)}, u32[]{:S(2)}, u32[]{:S(2)}) collective-permute-start(bf16[2,1024,128]{2,1,0:T(8,128)(2,1)S(1)} %slice_bitcast_fusion), channel_id=1, source_target_pairs={{0,96},{32,0},{64,32},{96,64},{1,97},{33,1},{65,33},{97,65},{2,98}... | collective-permute-start | bytes 1572872 | tf_op jit(solution)/shard_map/ppermute | solution.py:231
  102.6 14.5 %collective-permute-start.5 = (bf16[2,1024,128]{2,1,0:T(8,128)(2,1)S(1)}, bf16[2,1024,128]{2,1,0:T(8,128)(2,1)S(1)}, u32[]{:S(2)}, u32[]{:S(2)}) collective-permute-start(bf16[2,1024,128]{2,1,0:T(8,128)(2,1)S(1)} %slice_bitcast_fusion.1), channel_id=1, source_target_pairs={{0,32},{32,64},{64,96},{96,0},{1,33},{33,65},{65,97},{97,1},{2,34}... | collective-permute-start | bytes 1572872 | tf_op jit(solution)/shard_map/ppermute | solution.py:231
  105.6 14.2 %collective-permute-start.9 = (bf16[2,2,1024,128]{3,2,1,0:T(8,128)(2,1)S(1)}, bf16[2,2,1024,128]{3,2,1,0:T(8,128)(2,1)S(1)}, u32[]{:S(2)}, u32[]{:S(2)}) collective-permute-start(bf16[2,2,1024,128]{3,2,1,0:T(8,128)(2,1)S(1)} %collective-permute-done.4.refs_2_), channel_id=1, source_target_pairs={{0,16},{16,0},{1,17},{17,1},{2,18},{18,2},{3,19},{19,3},{4,20},{20... | collective-permute-start | bytes 3145736 | tf_op jit(solution)/shard_map/ppermute | solution.py:232
  108.2 11.5 %collective-permute-start.8 = (bf16[2,2,1024,128]{3,2,1,0:T(8,128)(2,1)S(1)}, bf16[2,2,1024,128]{3,2,1,0:T(8,128)(2,1)S(1)}, u32[]{:S(2)}, u32[]{:S(2)}) collective-permute-start(bf16[2,2,1024,128]{3,2,1,0:T(8,128)(2,1)S(1)} %collective-permute-done.3.refs_1_), channel_id=1, source_target_pairs={{0,16},{16,0},{1,17},{17,1},{2,18},{18,2},{3,19},{19,3},{4,20},{20... | collective-permute-start | bytes 3145736 | tf_op jit(solution)/shard_map/ppermute | solution.py:232
  113.9 4.3 %collective-permute-start.11 = (bf16[2,1024,128]{2,1,0:T(8,128)(2,1)S(1)}, bf16[2,1024,128]{2,1,0:T(8,128)(2,1)S(1)}, u32[]{:S(2)}, u32[]{:S(2)}) collective-permute-start(bf16[2,1024,128]{2,1,0:T(8,128)(2,1)S(1)} %collective-permute-done.6.refs_4_), channel_id=1, source_target_pairs={{0,16},{16,0},{1,17},{17,1},{2,18},{18,2},{3,19},{19,3},{4,20},{20... | collective-permute-start | bytes 1572872 | tf_op jit(solution)/shard_map/ppermute | solution.py:232
  117.1 2.6 %collective-permute-start.10 = (bf16[2,1024,128]{2,1,0:T(8,128)(2,1)S(1)}, bf16[2,1024,128]{2,1,0:T(8,128)(2,1)S(1)}, u32[]{:S(2)}, u32[]{:S(2)}) collective-permute-start(bf16[2,1024,128]{2,1,0:T(8,128)(2,1)S(1)} %collective-permute-done.5.refs_3_), channel_id=1, source_target_pairs={{0,16},{16,0},{1,17},{17,1},{2,18},{18,2},{3,19},{19,3},{4,20},{20... | collective-permute-start | bytes 1572872 | tf_op jit(solution)/shard_map/ppermute | solution.py:232

commit v7 on v6

--- a/solution.py
+++ b/solution.py
@@ -96,6 +96,48 @@
         compiler_params=pltpu.CompilerParams(vmem_limit_bytes=54 << 20),
         name="compress",
     )(amp_mask, amplitudes)
+
+
+def gate_kernel(mask_ref, gate_ref, int_ref, block_ref, own_ref, held, in_sems, out_sems):
+    steps, tiles, rows, width = held.shape
+    loads, stores = [], []
+    for step in range(steps):
+        for tile in range(tiles):
+            loads.append(pltpu.make_async_copy(
+                int_ref.at[step, tile], held.at[step, tile], in_sems.at[step, tile]))
+            loads[-1].start()
+    lane = lax.broadcasted_iota(jnp.int32, own_ref.shape, 1)
+    own = jnp.zeros(own_ref.shape, jnp.int32)
+    for group in range(own_ref.shape[1]):
+        own = jnp.where(lane == group, needed_tile(mask_ref, group), own)
+    own_ref[...] = own
+    for step in range(steps):
+        for tile in range(tiles):
+            loads[step * tiles + tile].wait()
+            for place in range(width // TW):
+                @pl.when(gate_ref[step, tile, place] == 0)
+                def _():
+                    held[step, tile, :, place * TW:(place + 1) * TW] = jnp.zeros((rows, TW), held.dtype)
+            stores.append(pltpu.make_async_copy(
+                held.at[step, tile], block_ref.at[step, tile], out_sems.at[step, tile]))
+            stores[-1].start()
+    for store in stores:
+        store.wait()
+
+
+def gate(amp_mask, integrals, int_mask):
+    groups = amp_mask.shape[1] // 2
+    return pl.pallas_call(
+        gate_kernel,
+        in_specs=[pl.BlockSpec(memory_space=pltpu.SMEM)] * 2 + [pl.BlockSpec(memory_space=pl.ANY)],
+        out_specs=[pl.BlockSpec(memory_space=pl.ANY), pl.BlockSpec(memory_space=pltpu.VMEM)],
+        out_shape=[jax.ShapeDtypeStruct(integrals.shape, integrals.dtype),
+                   jax.ShapeDtypeStruct((ROWS, groups), jnp.int32)],
+        scratch_shapes=[pltpu.VMEM(integrals.shape, integrals.dtype),
+                        pltpu.SemaphoreType.DMA(int_mask.shape[:2]), pltpu.SemaphoreType.DMA(int_mask.shape[:2])],
+        compiler_params=pltpu.CompilerParams(vmem_limit_bytes=60 << 20),
+        name="gate",
+    )(amp_mask, int_mask, integrals)
 
 
 def pick_kernel(needs_ref, info_ref, *refs):
@@ -213,14 +255,12 @@
     core, z, x = (lax.axis_index(axis) for axis in GRID)
     info = jnp.stack([steps[0], steps[1], row, core, z, x]).astype(jnp.int32)
 
-    own = jnp.max(amp_mask, axis=0).reshape(1, -1, 2)[:, :, 1]
-    by_row = lax.all_to_all(jnp.broadcast_to(own, (ROWS, own.shape[1])), ROW, 0, 0, tiled=True)
+    block, own = gate(amp_mask, integrals.reshape(STEPS, tiles, TW, ab_width), int_mask)
+
+    by_row = lax.all_to_all(own, ROW, 0, 0, tiled=True)
     readers = [by_row] + [lax.ppermute(by_row, GRID, plane_perm(False, RING - ahead)) for ahead in (1, 2, 3)]
     needs = jnp.concatenate(readers, axis=1)
 
-    gate = int_mask.astype(integrals.dtype)[:, :, None, :, None]
-    block = integrals.reshape(STEPS, tiles, TW, ab_width // TW, TW) * gate
-    block = block.reshape(STEPS, tiles, TW, ab_width)
     held = [block] + [lax.ppermute(block, GRID, plane_perm(True, shift)) for shift in (1, 2, 3)]
 
     sent = pick(needs, info, held)

time: 139 us -> 139 us (level)
  Pallas kernels: 28.3 us -> 31.5 us
  other arithmetic: 2.3 us -> 0.17 us
    pallas_call x0 -> x1, Pallas kernels: none -> 3.49 us  [gate(): pl.pallas_call(gate_kernel, in_specs=[pl.BlockSpec(memory_space=pltpu.SME...]
    mul x1 -> x0, other arithmetic: 1.41 us -> none  [local(): block = integrals.reshape(STEPS, tiles, TW, ab_width // TW, TW) * gate]
where the time goes in v7:
time: 139 us; the launch traced here: 138 us
  waiting for transfers between devices  68.1 us (49%)
  starting transfers between devices  35 us (25%)
  Pallas kernels  31.5 us (23%)
  local copies, waits for them, and re-layouts  2.03 us (1%)
  between operations  1.52 us (1%)
    ppermute x2, waiting for transfers between devices, local(): halves += [lax.ppermute(halves[0], 'y', round_y(shift)) for shift in (1, 3)]  22.5 us
    all_to_all x1, waiting for transfers between devices, local(): lax.all_to_all(compress(amplitudes, amp_mask), ROW, 0, 0, tiled=True)  21.8 us
    pallas_call x1, Pallas kernels, multiply(): pl.pallas_call(ladder_kernel, in_specs=[pl.BlockSpec(memory_space=pltpu.S...  17.9 us
    ppermute x3, waiting for transfers between devices, local(): lax.ppermute(block, GRID, plane_perm(True, shift))  7.5 us
    all_to_all x1, starting transfers between devices, local(): by_row = lax.all_to_all(own, ROW, 0, 0, tiled=True)  6.81 us
    ppermute x5, starting transfers between devices, local(): halves += [lax.ppermute(half, 'core', [(0, 1), (1, 0)]) for half in halves]  6.34 us
    ppermute x3, starting transfers between devices, local(): lax.ppermute(sent[shift - 1], GRID, plane_perm(False, shift))  5.45 us
    pallas_call x1, Pallas kernels, pick(): pl.pallas_call(pick_kernel, in_specs=[pl.BlockSpec(memory_space=pltpu.SME...  5.1 us
  transfers between devices with their start and end apart: 20, of which 12 were waited for; matrix products, arithmetic and copies ran while one was open for 2% of the time, Pallas kernels for 7%

profile of v7, /device:TPU:1, one launch (start us, length us, event | category | flops | bytes accessed | tf_op | source)
XLA Modules:
  0.0 138.4 jit_solution(3455244280173902001)
XLA Ops:
  0.0 3.5 %gate.1 = (bf16[2,2,128,1280]{3,2,1,0:T(8,128)(2,1)}, s32[8,16]{1,0:T(8,128)}) custom-call(s32[8,32]{1,0:T(8,128)} %mask_ref.3, s32[2,2,10]{2,1,0:T(2,128)} %gate_ref.1, bf16[2,2,128,1280]{3,2,1,0:T(8,128)(2,1)} %bitcast.23), custom_call_target="tpu_custom_call" | custom-call | tf_op jit(solution)/shard_map/gate/pallas_call | solution.py:130
  3.5 3.4 %collective-permute-start.14 = (bf16[2,2,128,1280]{3,2,1,0:T(8,128)(2,1)}, bf16[2,2,128,1280]{3,2,1,0:T(8,128)(2,1)S(1)}, u32[]{:S(2)}, u32[]{:S(2)}) collective-permute-start(bf16[2,2,128,1280]{3,2,1,0:T(8,128)(2,1)} %get-tuple-element.11.refs_0_.refs_10_), channel_id=1, source_target_pairs={{0,12},{1,13},{2,14},{3,15},{4,0},{5,1},{6,2},{7,3},{8,4},{9,5},{1... | collective-permute-start | bytes 3932168 | tf_op jit(solution)/shard_map/ppermute | solution.py:264
  6.9 0.5 collective-permute-start.13
  7.4 0.6 collective-permute-start.12
  8.0 6.8 %all-to-all-start = ((s32[8,1,16]{2,1,0:T(1,128)}), s32[8,1,16]{2,1,0:T(1,128)S(1)}, u32[]{:S(2)}, u32[]{:S(2)}) async-start(s32[8,1,16]{2,1,0:T(1,128)} %bitcast.28), calls=%async_computation | async-start | bytes 8192 | tf_op jit(solution)/shard_map/all_to_all | solution.py:260
  14.8 5.0 %compress.1 = bf16[16,1024,128]{2,1,0:T(8,128)(2,1)} custom-call(s32[8,32]{1,0:T(8,128)} %mask_ref.3, bf16[1024,4096]{1,0:T(8,128)(2,1)} %amp_ref.1), custom_call_target="tpu_custom_call" | custom-call | tf_op jit(solution)/shard_map/compress/pallas_call | solution.py:89
  19.8 0.0 copy-start.4
  19.8 0.0 all-to-all-done
  19.9 5.0 %all-to-all-start.1 = ((bf16[16,1024,128]{2,1,0:T(8,128)(2,1)}), bf16[16,1024,128]{2,1,0:T(8,128)(2,1)}, u32[]{:S(2)}, u32[]{:S(2)}) async-start(bf16[16,1024,128]{2,1,0:T(8,128)(2,1)} %compress.1), calls=%async_computation.1 | async-start | bytes 8388608 | tf_op jit(solution)/shard_map/all_to_all | solution.py:267
  24.9 2.0 %collective-permute-start.2 = (s32[8,16]{1,0:T(8,128)S(1)}, s32[8,16]{1,0:T(8,128)S(1)}, u32[]{:S(2)}, u32[]{:S(2)}) collective-permute-start(s32[8,16]{1,0:T(8,128)S(1)} %bitcast.24), channel_id=1, source_target_pairs={{0,1},{1,2},{2,3},{3,0},{4,5},{5,6},{6,7},{7,4},{8,9},{9,10},{10,1... | collective-permute-start | bytes 1544 | tf_op jit(solution)/shard_map/ppermute | solution.py:261
  26.8 0.8 collective-permute-start.1
  27.7 1.4 collective-permute-done.2
  29.0 0.4 collective-permute-start
  29.5 0.1 stack.28.info_ref
  29.5 1.8 %collective-permute-done.1 = s32[8,16]{1,0:T(8,128)S(1)} collective-permute-done((s32[8,16]{1,0:T(8,128)S(1)}, s32[8,16]{1,0:T(8,128)S(1)}, u32[]{:S(2)}, u32[]{:S(2)}) %collective-permute-start.1) | collective-permute-done | bytes 544 | tf_op jit(solution)/shard_map/ppermute | solution.py:261
  31.3 0.7 collective-permute-done
  32.0 0.1 pad_add_fusion.needs_ref
  32.1 3.8 %collective-permute-done.14.refs_3_.refs_13_ = bf16[2,2,128,1280]{3,2,1,0:T(8,128)(2,1)S(1)} collective-permute-done((bf16[2,2,128,1280]{3,2,1,0:T(8,128)(2,1)}, bf16[2,2,128,1280]{3,2,1,0:T(8,128)(2,1)S(1)}, u32[]{:S(2)}, u32[]{:S(2)}) %collective-permute-start.14) | collective-permute-done | bytes 1310752 | tf_op jit(solution)/shard_map/ppermute | solution.py:264
  35.9 0.0 collective-permute-done.13.refs_2_.refs_12_
  35.9 3.7 %collective-permute-done.12.refs_1_.refs_11_ = bf16[2,2,128,1280]{3,2,1,0:T(8,128)(2,1)} collective-permute-done((bf16[2,2,128,1280]{3,2,1,0:T(8,128)(2,1)}, bf16[2,2,128,1280]{3,2,1,0:T(8,128)(2,1)}, u32[]{:S(2)}, u32[]{:S(2)}) %collective-permute-start.12) | collective-permute-done | bytes 1310752 | tf_op jit(solution)/shard_map/ppermute | solution.py:264
  39.6 5.1 %pick.1 = (bf16[2,4,128,1280]{3,2,1,0:T(8,128)(2,1)}, bf16[2,4,128,1280]{3,2,1,0:T(8,128)(2,1)}, bf16[2,4,128,1280]{3,2,1,0:T(8,128)(2,1)}) custom-call(s32[8,64]{1,0:T(8,128)S(1)} %pad_add_fusion.needs_ref, s32[6]{0:T(128)S(1)} %stack.28.info_ref, bf16[2,2,128,1280]{3,2,1,0:T(8,128)(2,1)S(1)} %copy-done, ...), custom_call_target="tpu_custom_call" | custom-call | flops 27599998976 | bytes 8388608 | tf_op jit(solution)/shard_map/pick/pallas_call | solution.py:162
  44.7 1.7 %collective-permute-start.15 = (bf16[2,4,128,1280]{3,2,1,0:T(8,128)(2,1)}, bf16[2,4,128,1280]{3,2,1,0:T(8,128)(2,1)S(1)}, u32[]{:S(2)}, u32[]{:S(2)}) collective-permute-start(bf16[2,4,128,1280]{3,2,1,0:T(8,128)(2,1)} %get-tuple-element.12), channel_id=1, source_target_pairs={{0,1},{1,2},{2,3},{3,0},{4,5},{5,6},{6,7},{7,4},{8,9},{9,10},{10,1... | collective-permute-start | bytes 7864328 | tf_op jit(solution)/shard_map/ppermute | solution.py:274
  46.4 3.0 %collective-permute-start.16 = (bf16[2,4,128,1280]{3,2,1,0:T(8,128)(2,1)}, bf16[2,4,128,1280]{3,2,1,0:T(8,128)(2,1)}, u32[]{:S(2)}, u32[]{:S(2)}) collective-permute-start(bf16[2,4,128,1280]{3,2,1,0:T(8,128)(2,1)} %get-tuple-element.13), channel_id=1, source_target_pairs={{0,2},{1,3},{2,0},{3,1},{4,6},{5,7},{6,4},{7,5},{8,10},{9,11},{10,... | collective-permute-start | bytes 7864328 | tf_op jit(solution)/shard_map/ppermute | solution.py:274
  49.4 0.7 collective-permute-start.17
  50.2 0.6 fusion
  52.0 21.8 %all-to-all-done.1 = bf16[16,1024,128]{2,1,0:T(8,128)(2,1)} async-done(((bf16[16,1024,128]{2,1,0:T(8,128)(2,1)}), bf16[16,1024,128]{2,1,0:T(8,128)(2,1)}, u32[]{:S(2)}, u32[]{:S(2)}) %all-to-all-start.1) | async-done | bytes 4194336 | tf_op jit(solution)/shard_map/all_to_all | solution.py:267
  73.8 1.3 dynamic-slice_bitcast_fusion.1
  75.1 0.1 pad_maximum_fusion.refs_0_
  75.2 1.0 collective-permute-start.4
  76.1 0.6 collective-permute-start.3
  76.7 22.4 %collective-permute-done.4.refs_2_ = bf16[2,2,1024,128]{3,2,1,0:T(8,128)(2,1)S(1)} collective-permute-done((bf16[2,2,1024,128]{3,2,1,0:T(8,128)(2,1)S(1)}, bf16[2,2,1024,128]{3,2,1,0:T(8,128)(2,1)S(1)}, u32[]{:S(2)}, u32[]{:S(2)}) %collective-permute-start.4) | collective-permute-done | bytes 1048608 | tf_op jit(solution)/shard_map/ppermute | solution.py:270
  99.2 1.7 %collective-permute-start.7 = (bf16[2,2,1024,128]{3,2,1,0:T(8,128)(2,1)S(1)}, bf16[2,2,1024,128]{3,2,1,0:T(8,128)(2,1)S(1)}, u32[]{:S(2)}, u32[]{:S(2)}) collective-permute-start(bf16[2,2,1024,128]{3,2,1,0:T(8,128)(2,1)S(1)} %pad_maximum_fusion.refs_0_), channel_id=1, source_target_pairs={{0,16},{16,0},{1,17},{17,1},{2,18},{18,2},{3,19},{19,3},{4,20},{20... | collective-permute-start | bytes 3145736 | tf_op jit(solution)/shard_map/ppermute | solution.py:272
  100.9 0.1 collective-permute-done.3.refs_1_
  101.0 2.1 %collective-permute-start.6 = (bf16[2,1024,128]{2,1,0:T(8,128)(2,1)S(1)}, bf16[2,1024,128]{2,1,0:T(8,128)(2,1)S(1)}, u32[]{:S(2)}, u32[]{:S(2)}) collective-permute-start(bf16[2,1024,128]{2,1,0:T(8,128)(2,1)S(1)} %slice_bitcast_fusion), channel_id=1, source_target_pairs={{0,96},{32,0},{64,32},{96,64},{1,97},{33,1},{65,33},{97,65},{2,98}... | collective-permute-start | bytes 1572872 | tf_op jit(solution)/shard_map/ppermute | solution.py:271
  103.1 0.1 collective-permute-start.5
  103.2 4.0 %collective-permute-done.16 = bf16[2,4,128,1280]{3,2,1,0:T(8,128)(2,1)} collective-permute-done((bf16[2,4,128,1280]{3,2,1,0:T(8,128)(2,1)}, bf16[2,4,128,1280]{3,2,1,0:T(8,128)(2,1)}, u32[]{:S(2)}, u32[]{:S(2)}) %collective-permute-start.16) | collective-permute-done | bytes 2621472 | tf_op jit(solution)/shard_map/ppermute | solution.py:274
  107.2 2.7 %collective-permute-start.9 = (bf16[2,2,1024,128]{3,2,1,0:T(8,128)(2,1)S(1)}, bf16[2,2,1024,128]{3,2,1,0:T(8,128)(2,1)S(1)}, u32[]{:S(2)}, u32[]{:S(2)}) collective-permute-start(bf16[2,2,1024,128]{3,2,1,0:T(8,128)(2,1)S(1)} %collective-permute-done.4.refs_2_), channel_id=1, source_target_pairs={{0,16},{16,0},{1,17},{17,1},{2,18},{18,2},{3,19},{19,3},{4,20},{20... | collective-permute-start | bytes 3145736 | tf_op jit(solution)/shard_map/ppermute | solution.py:272
  109.8 0.0 collective-permute-done.17
  109.9 0.0 collective-permute-start.8
  109.9 4.5 %collective-permute-done.6.refs_4_ = bf16[2,1024,128]{2,1,0:T(8,128)(2,1)S(1)} collective-permute-done((bf16[2,1024,128]{2,1,0:T(8,128)(2,1)S(1)}, bf16[2,1024,128]{2,1,0:T(8,128)(2,1)S(1)}, u32[]{:S(2)}, u32[]{:S(2)}) %collective-permute-start.6) | collective-permute-done | bytes 524320 | tf_op jit(solution)/shard_map/ppermute | solution.py:271
  114.4 0.9 collective-permute-start.11
  115.3 2.3 %collective-permute-done.5.refs_3_ = bf16[2,1024,128]{2,1,0:T(8,128)(2,1)S(1)} collective-permute-done((bf16[2,1024,128]{2,1,0:T(8,128)(2,1)S(1)}, bf16[2,1024,128]{2,1,0:T(8,128)(2,1)S(1)}, u32[]{:S(2)}, u32[]{:S(2)}) %collective-permute-start.5) | collective-permute-done | bytes 524320 | tf_op jit(solution)/shard_map/ppermute | solution.py:271
  117.6 1.1 collective-permute-start.10
  118.7 0.0 collective-permute-done.7.refs_5_
  118.7 0.0 collective-permute-done.11.refs_9_
  118.7 1.5 %collective-permute-done.10.refs_8_ = bf16[2,1024,128]{2,1,0:T(8,128)(2,1)S(1)} collective-permute-done((bf16[2,1024,128]{2,1,0:T(8,128)(2,1)S(1)}, bf16[2,1024,128]{2,1,0:T(8,128)(2,1)S(1)}, u32[]{:S(2)}, u32[]{:S(2)}) %collective-permute-start.10) | collective-permute-done | bytes 524320 | tf_op jit(solution)/shard_map/ppermute | solution.py:272
  120.3 0.0 collective-permute-done.9.refs_7_
  120.3 17.9 %ladder.1 = f32[1024,1280]{1,0:T(8,128)} custom-call(s32[8,64]{1,0:T(8,128)S(1)} %pad_add_fusion.needs_ref, s32[6]{0:T(128)S(1)} %stack.28.info_ref, bf16[2,2,1024,128]{3,2,1,0:T(8,128)(2,1)S(1)} %pad_maximum_fusion.refs_0_, bf16[2,2,1024,128]{3,2,1,0:T(8,128)(2,1)S(1)} %collective-permute-done.3.refs_1_, ...), custom_call_target="tpu_custom_call" | custom-call | flops 10737418240 | bytes 25165824 | tf_op jit(solution)/shard_map/ladder/pallas_call | solution.py:234
  (13 shorter events, 0.1 us)
Async XLA Ops:
  3.5 32.4 %collective-permute-start.14 = (bf16[2,2,128,1280]{3,2,1,0:T(8,128)(2,1)}, bf16[2,2,128,1280]{3,2,1,0:T(8,128)(2,1)S(1)}, u32[]{:S(2)}, u32[]{:S(2)}) collective-permute-start(bf16[2,2,128,1280]{3,2,1,0:T(8,128)(2,1)} %get-tuple-element.11.refs_0_.refs_10_), channel_id=1, source_target_pairs={{0,12},{1,13},{2,14},{3,15},{4,0},{5,1},{6,2},{7,3},{8,4},{9,5},{1... | collective-permute-start | bytes 3932168 | tf_op jit(solution)/shard_map/ppermute | solution.py:264
  6.9 29.0 %collective-permute-start.13 = (bf16[2,2,128,1280]{3,2,1,0:T(8,128)(2,1)}, bf16[2,2,128,1280]{3,2,1,0:T(8,128)(2,1)}, u32[]{:S(2)}, u32[]{:S(2)}) collective-permute-start(bf16[2,2,128,1280]{3,2,1,0:T(8,128)(2,1)} %get-tuple-element.11.refs_0_.refs_10_), channel_id=1, source_target_pairs={{0,8},{1,9},{2,10},{3,11},{4,12},{5,13},{6,14},{7,15},{8,0},{9,1},... | collective-permute-start | bytes 3932168 | tf_op jit(solution)/shard_map/ppermute | solution.py:264
  7.4 32.2 %collective-permute-start.12 = (bf16[2,2,128,1280]{3,2,1,0:T(8,128)(2,1)}, bf16[2,2,128,1280]{3,2,1,0:T(8,128)(2,1)}, u32[]{:S(2)}, u32[]{:S(2)}) collective-permute-start(bf16[2,2,128,1280]{3,2,1,0:T(8,128)(2,1)} %get-tuple-element.11.refs_0_.refs_10_), channel_id=1, source_target_pairs={{0,4},{1,5},{2,6},{3,7},{4,8},{5,9},{6,10},{7,11},{8,12},{9,13},{1... | collective-permute-start | bytes 3932168 | tf_op jit(solution)/shard_map/ppermute | solution.py:264
  8.0 11.8 %all-to-all-start = ((s32[8,1,16]{2,1,0:T(1,128)}), s32[8,1,16]{2,1,0:T(1,128)S(1)}, u32[]{:S(2)}, u32[]{:S(2)}) async-start(s32[8,1,16]{2,1,0:T(1,128)} %bitcast.28), calls=%async_computation | async-start | bytes 8192 | tf_op jit(solution)/shard_map/all_to_all | solution.py:260
  19.8 9.6 %copy-start.4 = (s32[2]{0:T(128)S(1)}, s32[2]{0:T(128)}, u32[]{:S(2)}) copy-start(s32[2]{0:T(128)} %param.9) | copy-start | bytes 28
  19.8 19.8 %copy-start = (bf16[2,2,128,1280]{3,2,1,0:T(8,128)(2,1)S(1)}, bf16[2,2,128,1280]{3,2,1,0:T(8,128)(2,1)}, u32[]{:S(2)}) copy-start(bf16[2,2,128,1280]{3,2,1,0:T(8,128)(2,1)} %get-tuple-element.11.refs_0_.refs_10_) | copy-start | bytes 3932164
  19.9 53.9 %all-to-all-start.1 = ((bf16[16,1024,128]{2,1,0:T(8,128)(2,1)}), bf16[16,1024,128]{2,1,0:T(8,128)(2,1)}, u32[]{:S(2)}, u32[]{:S(2)}) async-start(bf16[16,1024,128]{2,1,0:T(8,128)(2,1)} %compress.1), calls=%async_computation.1 | async-start | bytes 8388608 | tf_op jit(solution)/shard_map/all_to_all | solution.py:267
  24.9 4.2 %collective-permute-start.2 = (s32[8,16]{1,0:T(8,128)S(1)}, s32[8,16]{1,0:T(8,128)S(1)}, u32[]{:S(2)}, u32[]{:S(2)}) collective-permute-start(s32[8,16]{1,0:T(8,128)S(1)} %bitcast.24), channel_id=1, source_target_pairs={{0,1},{1,2},{2,3},{3,0},{4,5},{5,6},{6,7},{7,4},{8,9},{9,10},{10,1... | collective-permute-start | bytes 1544 | tf_op jit(solution)/shard_map/ppermute | solution.py:261
  26.8 4.5 %collective-permute-start.1 = (s32[8,16]{1,0:T(8,128)S(1)}, s32[8,16]{1,0:T(8,128)S(1)}, u32[]{:S(2)}, u32[]{:S(2)}) collective-permute-start(s32[8,16]{1,0:T(8,128)S(1)} %bitcast.25), channel_id=1, source_target_pairs={{0,2},{1,3},{2,0},{3,1},{4,6},{5,7},{6,4},{7,5},{8,10},{9,11},{10,... | collective-permute-start | bytes 1544 | tf_op jit(solution)/shard_map/ppermute | solution.py:261
  29.0 3.0 %collective-permute-start = (s32[8,16]{1,0:T(8,128)S(1)}, s32[8,16]{1,0:T(8,128)S(1)}, u32[]{:S(2)}, u32[]{:S(2)}) collective-permute-start(s32[8,16]{1,0:T(8,128)S(1)} %bitcast.26), channel_id=1, source_target_pairs={{0,3},{1,0},{2,1},{3,2},{4,7},{5,4},{6,5},{7,6},{8,11},{9,8},{10,9... | collective-permute-start | bytes 1544 | tf_op jit(solution)/shard_map/ppermute | solution.py:261
  35.9 8.8 %copy-start.2 = (bf16[2,2,128,1280]{3,2,1,0:T(8,128)(2,1)}, bf16[2,2,128,1280]{3,2,1,0:T(8,128)(2,1)S(1)}, u32[]{:S(2)}) copy-start(bf16[2,2,128,1280]{3,2,1,0:T(8,128)(2,1)S(1)} %collective-permute-done.14.refs_3_.refs_13_) | copy-start | bytes 3932164
  44.7 58.4 %collective-permute-start.15 = (bf16[2,4,128,1280]{3,2,1,0:T(8,128)(2,1)}, bf16[2,4,128,1280]{3,2,1,0:T(8,128)(2,1)S(1)}, u32[]{:S(2)}, u32[]{:S(2)}) collective-permute-start(bf16[2,4,128,1280]{3,2,1,0:T(8,128)(2,1)} %get-tuple-element.12), channel_id=1, source_target_pairs={{0,1},{1,2},{2,3},{3,0},{4,5},{5,6},{6,7},{7,4},{8,9},{9,10},{10,1... | collective-permute-start | bytes 7864328 | tf_op jit(solution)/shard_map/ppermute | solution.py:274
  46.4 60.8 %collective-permute-start.16 = (bf16[2,4,128,1280]{3,2,1,0:T(8,128)(2,1)}, bf16[2,4,128,1280]{3,2,1,0:T(8,128)(2,1)}, u32[]{:S(2)}, u32[]{:S(2)}) collective-permute-start(bf16[2,4,128,1280]{3,2,1,0:T(8,128)(2,1)} %get-tuple-element.13), channel_id=1, source_target_pairs={{0,2},{1,3},{2,0},{3,1},{4,6},{5,7},{6,4},{7,5},{8,10},{9,11},{10,... | collective-permute-start | bytes 7864328 | tf_op jit(solution)/shard_map/ppermute | solution.py:274
  49.4 60.4 %collective-permute-start.17 = (bf16[2,4,128,1280]{3,2,1,0:T(8,128)(2,1)}, bf16[2,4,128,1280]{3,2,1,0:T(8,128)(2,1)}, u32[]{:S(2)}, u32[]{:S(2)}) collective-permute-start(bf16[2,4,128,1280]{3,2,1,0:T(8,128)(2,1)} %get-tuple-element.14), channel_id=1, source_target_pairs={{0,3},{1,0},{2,1},{3,2},{4,7},{5,4},{6,5},{7,6},{8,11},{9,8},{10,9... | collective-permute-start | bytes 7864328 | tf_op jit(solution)/shard_map/ppermute | solution.py:274
  75.1 45.2 %copy-start.1 = (bf16[2,2,128,1280]{3,2,1,0:T(8,128)(2,1)S(1)}, bf16[2,2,128,1280]{3,2,1,0:T(8,128)(2,1)}, u32[]{:S(2)}) copy-start(bf16[2,2,128,1280]{3,2,1,0:T(8,128)(2,1)} %get-tuple-element.11.refs_0_.refs_10_) | copy-start | bytes 3932164
  75.1 45.2 %copy-start.3 = (bf16[2,2,128,1280]{3,2,1,0:T(8,128)(2,1)S(1)}, bf16[2,2,128,1280]{3,2,1,0:T(8,128)(2,1)}, u32[]{:S(2)}) copy-start(bf16[2,2,128,1280]{3,2,1,0:T(8,128)(2,1)} %copy-done.2) | copy-start | bytes 3932164
  75.2 24.0 %collective-permute-start.4 = (bf16[2,2,1024,128]{3,2,1,0:T(8,128)(2,1)S(1)}, bf16[2,2,1024,128]{3,2,1,0:T(8,128)(2,1)S(1)}, u32[]{:S(2)}, u32[]{:S(2)}) collective-permute-start(bf16[2,2,1024,128]{3,2,1,0:T(8,128)(2,1)S(1)} %pad_maximum_fusion.refs_0_), channel_id=1, source_target_pairs={{0,96},{32,0},{64,32},{96,64},{1,97},{33,1},{65,33},{97,65},{2,98}... | collective-permute-start | bytes 3145736 | tf_op jit(solution)/shard_map/ppermute | solution.py:270
  76.1 24.8 %collective-permute-start.3 = (bf16[2,2,1024,128]{3,2,1,0:T(8,128)(2,1)S(1)}, bf16[2,2,1024,128]{3,2,1,0:T(8,128)(2,1)S(1)}, u32[]{:S(2)}, u32[]{:S(2)}) collective-permute-start(bf16[2,2,1024,128]{3,2,1,0:T(8,128)(2,1)S(1)} %pad_maximum_fusion.refs_0_), channel_id=1, source_target_pairs={{0,32},{32,64},{64,96},{96,0},{1,33},{33,65},{65,97},{97,1},{2,34}... | collective-permute-start | bytes 3145736 | tf_op jit(solution)/shard_map/ppermute | solution.py:270
  99.2 19.6 %collective-permute-start.7 = (bf16[2,2,1024,128]{3,2,1,0:T(8,128)(2,1)S(1)}, bf16[2,2,1024,128]{3,2,1,0:T(8,128)(2,1)S(1)}, u32[]{:S(2)}, u32[]{:S(2)}) collective-permute-start(bf16[2,2,1024,128]{3,2,1,0:T(8,128)(2,1)S(1)} %pad_maximum_fusion.refs_0_), channel_id=1, source_target_pairs={{0,16},{16,0},{1,17},{17,1},{2,18},{18,2},{3,19},{19,3},{4,20},{20... | collective-permute-start | bytes 3145736 | tf_op jit(solution)/shard_map/ppermute | solution.py:272
  101.0 13.4 %collective-permute-start.6 = (bf16[2,1024,128]{2,1,0:T(8,128)(2,1)S(1)}, bf16[2,1024,128]{2,1,0:T(8,128)(2,1)S(1)}, u32[]{:S(2)}, u32[]{:S(2)}) collective-permute-start(bf16[2,1024,128]{2,1,0:T(8,128)(2,1)S(1)} %slice_bitcast_fusion), channel_id=1, source_target_pairs={{0,96},{32,0},{64,32},{96,64},{1,97},{33,1},{65,33},{97,65},{2,98}... | collective-permute-start | bytes 1572872 | tf_op jit(solution)/shard_map/ppermute | solution.py:271
  103.1 14.5 %collective-permute-start.5 = (bf16[2,1024,128]{2,1,0:T(8,128)(2,1)S(1)}, bf16[2,1024,128]{2,1,0:T(8,128)(2,1)S(1)}, u32[]{:S(2)}, u32[]{:S(2)}) collective-permute-start(bf16[2,1024,128]{2,1,0:T(8,128)(2,1)S(1)} %slice_bitcast_fusion.1), channel_id=1, source_target_pairs={{0,32},{32,64},{64,96},{96,0},{1,33},{33,65},{65,97},{97,1},{2,34}... | collective-permute-start | bytes 1572872 | tf_op jit(solution)/shard_map/ppermute | solution.py:271
  107.2 13.1 %collective-permute-start.9 = (bf16[2,2,1024,128]{3,2,1,0:T(8,128)(2,1)S(1)}, bf16[2,2,1024,128]{3,2,1,0:T(8,128)(2,1)S(1)}, u32[]{:S(2)}, u32[]{:S(2)}) collective-permute-start(bf16[2,2,1024,128]{3,2,1,0:T(8,128)(2,1)S(1)} %collective-permute-done.4.refs_2_), channel_id=1, source_target_pairs={{0,16},{16,0},{1,17},{17,1},{2,18},{18,2},{3,19},{19,3},{4,20},{20... | collective-permute-start | bytes 3145736 | tf_op jit(solution)/shard_map/ppermute | solution.py:272
  109.9 10.4 %collective-permute-start.8 = (bf16[2,2,1024,128]{3,2,1,0:T(8,128)(2,1)S(1)}, bf16[2,2,1024,128]{3,2,1,0:T(8,128)(2,1)S(1)}, u32[]{:S(2)}, u32[]{:S(2)}) collective-permute-start(bf16[2,2,1024,128]{3,2,1,0:T(8,128)(2,1)S(1)} %collective-permute-done.3.refs_1_), channel_id=1, source_target_pairs={{0,16},{16,0},{1,17},{17,1},{2,18},{18,2},{3,19},{19,3},{4,20},{20... | collective-permute-start | bytes 3145736 | tf_op jit(solution)/shard_map/ppermute | solution.py:272
  114.4 4.3 %collective-permute-start.11 = (bf16[2,1024,128]{2,1,0:T(8,128)(2,1)S(1)}, bf16[2,1024,128]{2,1,0:T(8,128)(2,1)S(1)}, u32[]{:S(2)}, u32[]{:S(2)}) collective-permute-start(bf16[2,1024,128]{2,1,0:T(8,128)(2,1)S(1)} %collective-permute-done.6.refs_4_), channel_id=1, source_target_pairs={{0,16},{16,0},{1,17},{17,1},{2,18},{18,2},{3,19},{19,3},{4,20},{20... | collective-permute-start | bytes 1572872 | tf_op jit(solution)/shard_map/ppermute | solution.py:272
  117.6 2.6 %collective-permute-start.10 = (bf16[2,1024,128]{2,1,0:T(8,128)(2,1)S(1)}, bf16[2,1024,128]{2,1,0:T(8,128)(2,1)S(1)}, u32[]{:S(2)}, u32[]{:S(2)}) collective-permute-start(bf16[2,1024,128]{2,1,0:T(8,128)(2,1)S(1)} %collective-permute-done.5.refs_3_), channel_id=1, source_target_pairs={{0,16},{16,0},{1,17},{17,1},{2,18},{18,2},{3,19},{19,3},{4,20},{20... | collective-permute-start | bytes 1572872 | tf_op jit(solution)/shard_map/ppermute | solution.py:272

commit v8 on v7

--- a/solution.py
+++ b/solution.py
@@ -98,13 +98,13 @@
     )(amp_mask, amplitudes)
 
 
-def gate_kernel(mask_ref, gate_ref, int_ref, block_ref, own_ref, held, in_sems, out_sems):
-    steps, tiles, rows, width = held.shape
-    loads, stores = [], []
+def gate_kernel(mask_ref, gate_ref, int_ref, block_ref, own_ref, in_sems):
+    steps, tiles, rows, width = block_ref.shape
+    loads = []
     for step in range(steps):
         for tile in range(tiles):
             loads.append(pltpu.make_async_copy(
-                int_ref.at[step, tile], held.at[step, tile], in_sems.at[step, tile]))
+                int_ref.at[step, tile], block_ref.at[step, tile], in_sems.at[step, tile]))
             loads[-1].start()
     lane = lax.broadcasted_iota(jnp.int32, own_ref.shape, 1)
     own = jnp.zeros(own_ref.shape, jnp.int32)
@@ -117,12 +117,7 @@
             for place in range(width // TW):
                 @pl.when(gate_ref[step, tile, place] == 0)
                 def _():
-                    held[step, tile, :, place * TW:(place + 1) * TW] = jnp.zeros((rows, TW), held.dtype)
-            stores.append(pltpu.make_async_copy(
-                held.at[step, tile], block_ref.at[step, tile], out_sems.at[step, tile]))
-            stores[-1].start()
-    for store in stores:
-        store.wait()
+                    block_ref[step, tile, :, place * TW:(place + 1) * TW] = jnp.zeros((rows, TW), block_ref.dtype)
 
 
 def gate(amp_mask, integrals, int_mask):
@@ -130,11 +125,10 @@
     return pl.pallas_call(
         gate_kernel,
         in_specs=[pl.BlockSpec(memory_space=pltpu.SMEM)] * 2 + [pl.BlockSpec(memory_space=pl.ANY)],
-        out_specs=[pl.BlockSpec(memory_space=pl.ANY), pl.BlockSpec(memory_space=pltpu.VMEM)],
+        out_specs=[pl.BlockSpec(memory_space=pltpu.VMEM)] * 2,
         out_shape=[jax.ShapeDtypeStruct(integrals.shape, integrals.dtype),
                    jax.ShapeDtypeStruct((ROWS, groups), jnp.int32)],
-        scratch_shapes=[pltpu.VMEM(integrals.shape, integrals.dtype),
-                        pltpu.SemaphoreType.DMA(int_mask.shape[:2]), pltpu.SemaphoreType.DMA(int_mask.shape[:2])],
+        scratch_shapes=[pltpu.SemaphoreType.DMA(int_mask.shape[:2])],
         compiler_params=pltpu.CompilerParams(vmem_limit_bytes=60 << 20),
         name="gate",
     )(amp_mask, int_mask, integrals)

time: 139 us -> 138 us (level)
  no operation moved by 1% of the time
where the time goes in v8:
time: 138 us
  waiting for transfers between devices  67.9 us (49%)
  starting transfers between devices  35.1 us (25%)
  Pallas kernels  31.3 us (23%)
  local copies, waits for them, and re-layouts  2.03 us (1%)
  between operations  1.52 us (1%)
    ppermute x2, waiting for transfers between devices, local(): halves += [lax.ppermute(halves[0], 'y', round_y(shift)) for shift in (1, 3)]  22.5 us
    all_to_all x1, waiting for transfers between devices, local(): lax.all_to_all(compress(amplitudes, amp_mask), ROW, 0, 0, tiled=True)  21.8 us
    pallas_call x1, Pallas kernels, multiply(): pl.pallas_call(ladder_kernel, in_specs=[pl.BlockSpec(memory_space=pltpu.S...  17.9 us
    ppermute x3, waiting for transfers between devices, local(): lax.ppermute(block, GRID, plane_perm(True, shift))  7.5 us
    all_to_all x1, starting transfers between devices, local(): by_row = lax.all_to_all(own, ROW, 0, 0, tiled=True)  6.82 us
    ppermute x5, starting transfers between devices, local(): halves += [lax.ppermute(half, 'core', [(0, 1), (1, 0)]) for half in halves]  6.35 us
    ppermute x3, starting transfers between devices, local(): lax.ppermute(sent[shift - 1], GRID, plane_perm(False, shift))  5.44 us
    pallas_call x1, Pallas kernels, pick(): pl.pallas_call(pick_kernel, in_specs=[pl.BlockSpec(memory_space=pltpu.SME...  5.1 us
  transfers between devices with their start and end apart: 20, of which 12 were waited for; matrix products, arithmetic and copies ran while one was open for 2% of the time, Pallas kernels for 7%

profile of v8, /device:TPU:1, one launch (start us, length us, event | category | flops | bytes accessed | tf_op | source)
XLA Modules:
  0.0 138.0 jit_solution(3020857776601192170)
XLA Ops:
  0.0 3.2 %gate.1 = (bf16[2,2,128,1280]{3,2,1,0:T(8,128)(2,1)}, s32[8,16]{1,0:T(8,128)}) custom-call(s32[8,32]{1,0:T(8,128)} %mask_ref.3, s32[2,2,10]{2,1,0:T(2,128)} %gate_ref.1, bf16[2,2,128,1280]{3,2,1,0:T(8,128)(2,1)} %bitcast.23), custom_call_target="tpu_custom_call" | custom-call | tf_op jit(solution)/shard_map/gate/pallas_call | solution.py:125
  3.2 3.4 %collective-permute-start.14 = (bf16[2,2,128,1280]{3,2,1,0:T(8,128)(2,1)}, bf16[2,2,128,1280]{3,2,1,0:T(8,128)(2,1)S(1)}, u32[]{:S(2)}, u32[]{:S(2)}) collective-permute-start(bf16[2,2,128,1280]{3,2,1,0:T(8,128)(2,1)} %get-tuple-element.11.refs_0_.refs_10_), channel_id=1, source_target_pairs={{0,12},{1,13},{2,14},{3,15},{4,0},{5,1},{6,2},{7,3},{8,4},{9,5},{1... | collective-permute-start | bytes 3932168 | tf_op jit(solution)/shard_map/ppermute | solution.py:258
  6.6 0.5 collective-permute-start.13
  7.1 0.6 collective-permute-start.12
  7.7 6.8 %all-to-all-start = ((s32[8,1,16]{2,1,0:T(1,128)}), s32[8,1,16]{2,1,0:T(1,128)S(1)}, u32[]{:S(2)}, u32[]{:S(2)}) async-start(s32[8,1,16]{2,1,0:T(1,128)} %bitcast.28), calls=%async_computation | async-start | bytes 8192 | tf_op jit(solution)/shard_map/all_to_all | solution.py:254
  14.5 5.1 %compress.1 = bf16[16,1024,128]{2,1,0:T(8,128)(2,1)} custom-call(s32[8,32]{1,0:T(8,128)} %mask_ref.3, bf16[1024,4096]{1,0:T(8,128)(2,1)} %amp_ref.1), custom_call_target="tpu_custom_call" | custom-call | tf_op jit(solution)/shard_map/compress/pallas_call | solution.py:89
  19.6 0.0 copy-start.4
  19.7 0.0 all-to-all-done
  19.7 4.9 %all-to-all-start.1 = ((bf16[16,1024,128]{2,1,0:T(8,128)(2,1)}), bf16[16,1024,128]{2,1,0:T(8,128)(2,1)}, u32[]{:S(2)}, u32[]{:S(2)}) async-start(bf16[16,1024,128]{2,1,0:T(8,128)(2,1)} %compress.1), calls=%async_computation.1 | async-start | bytes 8388608 | tf_op jit(solution)/shard_map/all_to_all | solution.py:261
  24.6 1.9 %collective-permute-start.2 = (s32[8,16]{1,0:T(8,128)S(1)}, s32[8,16]{1,0:T(8,128)S(1)}, u32[]{:S(2)}, u32[]{:S(2)}) collective-permute-start(s32[8,16]{1,0:T(8,128)S(1)} %bitcast.24), channel_id=1, source_target_pairs={{0,1},{1,2},{2,3},{3,0},{4,5},{5,6},{6,7},{7,4},{8,9},{9,10},{10,1... | collective-permute-start | bytes 1544 | tf_op jit(solution)/shard_map/ppermute | solution.py:255
  26.5 0.9 collective-permute-start.1
  27.5 1.3 collective-permute-done.2
  28.8 0.5 collective-permute-start
  29.2 0.1 stack.28.info_ref
  29.3 1.7 %collective-permute-done.1 = s32[8,16]{1,0:T(8,128)S(1)} collective-permute-done((s32[8,16]{1,0:T(8,128)S(1)}, s32[8,16]{1,0:T(8,128)S(1)}, u32[]{:S(2)}, u32[]{:S(2)}) %collective-permute-start.1) | collective-permute-done | bytes 544 | tf_op jit(solution)/shard_map/ppermute | solution.py:255
  31.0 0.7 collective-permute-done
  31.7 0.1 pad_add_fusion.needs_ref
  31.8 3.8 %collective-permute-done.14.refs_3_.refs_13_ = bf16[2,2,128,1280]{3,2,1,0:T(8,128)(2,1)S(1)} collective-permute-done((bf16[2,2,128,1280]{3,2,1,0:T(8,128)(2,1)}, bf16[2,2,128,1280]{3,2,1,0:T(8,128)(2,1)S(1)}, u32[]{:S(2)}, u32[]{:S(2)}) %collective-permute-start.14) | collective-permute-done | bytes 1310752 | tf_op jit(solution)/shard_map/ppermute | solution.py:258
  35.6 0.0 collective-permute-done.13.refs_2_.refs_12_
  35.6 3.7 %collective-permute-done.12.refs_1_.refs_11_ = bf16[2,2,128,1280]{3,2,1,0:T(8,128)(2,1)} collective-permute-done((bf16[2,2,128,1280]{3,2,1,0:T(8,128)(2,1)}, bf16[2,2,128,1280]{3,2,1,0:T(8,128)(2,1)}, u32[]{:S(2)}, u32[]{:S(2)}) %collective-permute-start.12) | collective-permute-done | bytes 1310752 | tf_op jit(solution)/shard_map/ppermute | solution.py:258
  39.3 5.1 %pick.1 = (bf16[2,4,128,1280]{3,2,1,0:T(8,128)(2,1)}, bf16[2,4,128,1280]{3,2,1,0:T(8,128)(2,1)}, bf16[2,4,128,1280]{3,2,1,0:T(8,128)(2,1)}) custom-call(s32[8,64]{1,0:T(8,128)S(1)} %pad_add_fusion.needs_ref, s32[6]{0:T(128)S(1)} %stack.28.info_ref, bf16[2,2,128,1280]{3,2,1,0:T(8,128)(2,1)S(1)} %copy-done, ...), custom_call_target="tpu_custom_call" | custom-call | flops 27599998976 | bytes 8388608 | tf_op jit(solution)/shard_map/pick/pallas_call | solution.py:156
  44.4 1.7 %collective-permute-start.15 = (bf16[2,4,128,1280]{3,2,1,0:T(8,128)(2,1)}, bf16[2,4,128,1280]{3,2,1,0:T(8,128)(2,1)S(1)}, u32[]{:S(2)}, u32[]{:S(2)}) collective-permute-start(bf16[2,4,128,1280]{3,2,1,0:T(8,128)(2,1)} %get-tuple-element.12), channel_id=1, source_target_pairs={{0,1},{1,2},{2,3},{3,0},{4,5},{5,6},{6,7},{7,4},{8,9},{9,10},{10,1... | collective-permute-start | bytes 7864328 | tf_op jit(solution)/shard_map/ppermute | solution.py:268
  46.1 3.0 %collective-permute-start.16 = (bf16[2,4,128,1280]{3,2,1,0:T(8,128)(2,1)}, bf16[2,4,128,1280]{3,2,1,0:T(8,128)(2,1)}, u32[]{:S(2)}, u32[]{:S(2)}) collective-permute-start(bf16[2,4,128,1280]{3,2,1,0:T(8,128)(2,1)} %get-tuple-element.13), channel_id=1, source_target_pairs={{0,2},{1,3},{2,0},{3,1},{4,6},{5,7},{6,4},{7,5},{8,10},{9,11},{10,... | collective-permute-start | bytes 7864328 | tf_op jit(solution)/shard_map/ppermute | solution.py:268
  49.1 0.8 collective-permute-start.17
  49.9 0.6 fusion
  51.7 21.8 %all-to-all-done.1 = bf16[16,1024,128]{2,1,0:T(8,128)(2,1)} async-done(((bf16[16,1024,128]{2,1,0:T(8,128)(2,1)}), bf16[16,1024,128]{2,1,0:T(8,128)(2,1)}, u32[]{:S(2)}, u32[]{:S(2)}) %all-to-all-start.1) | async-done | bytes 4194336 | tf_op jit(solution)/shard_map/all_to_all | solution.py:261
  73.5 1.3 dynamic-slice_bitcast_fusion.1
  74.8 0.1 pad_maximum_fusion.refs_0_
  74.9 1.0 collective-permute-start.4
  75.9 0.6 collective-permute-start.3
  76.4 22.4 %collective-permute-done.4.refs_2_ = bf16[2,2,1024,128]{3,2,1,0:T(8,128)(2,1)S(1)} collective-permute-done((bf16[2,2,1024,128]{3,2,1,0:T(8,128)(2,1)S(1)}, bf16[2,2,1024,128]{3,2,1,0:T(8,128)(2,1)S(1)}, u32[]{:S(2)}, u32[]{:S(2)}) %collective-permute-start.4) | collective-permute-done | bytes 1048608 | tf_op jit(solution)/shard_map/ppermute | solution.py:264
  98.9 1.7 %collective-permute-start.7 = (bf16[2,2,1024,128]{3,2,1,0:T(8,128)(2,1)S(1)}, bf16[2,2,1024,128]{3,2,1,0:T(8,128)(2,1)S(1)}, u32[]{:S(2)}, u32[]{:S(2)}) collective-permute-start(bf16[2,2,1024,128]{3,2,1,0:T(8,128)(2,1)S(1)} %pad_maximum_fusion.refs_0_), channel_id=1, source_target_pairs={{0,16},{16,0},{1,17},{17,1},{2,18},{18,2},{3,19},{19,3},{4,20},{20... | collective-permute-start | bytes 3145736 | tf_op jit(solution)/shard_map/ppermute | solution.py:266
  100.6 0.1 collective-permute-done.3.refs_1_
  100.7 2.1 %collective-permute-start.6 = (bf16[2,1024,128]{2,1,0:T(8,128)(2,1)S(1)}, bf16[2,1024,128]{2,1,0:T(8,128)(2,1)S(1)}, u32[]{:S(2)}, u32[]{:S(2)}) collective-permute-start(bf16[2,1024,128]{2,1,0:T(8,128)(2,1)S(1)} %slice_bitcast_fusion), channel_id=1, source_target_pairs={{0,96},{32,0},{64,32},{96,64},{1,97},{33,1},{65,33},{97,65},{2,98}... | collective-permute-start | bytes 1572872 | tf_op jit(solution)/shard_map/ppermute | solution.py:265
  102.8 0.1 collective-permute-start.5
  102.9 4.0 %collective-permute-done.16 = bf16[2,4,128,1280]{3,2,1,0:T(8,128)(2,1)} collective-permute-done((bf16[2,4,128,1280]{3,2,1,0:T(8,128)(2,1)}, bf16[2,4,128,1280]{3,2,1,0:T(8,128)(2,1)}, u32[]{:S(2)}, u32[]{:S(2)}) %collective-permute-start.16) | collective-permute-done | bytes 2621472 | tf_op jit(solution)/shard_map/ppermute | solution.py:268
  106.8 2.7 %collective-permute-start.9 = (bf16[2,2,1024,128]{3,2,1,0:T(8,128)(2,1)S(1)}, bf16[2,2,1024,128]{3,2,1,0:T(8,128)(2,1)S(1)}, u32[]{:S(2)}, u32[]{:S(2)}) collective-permute-start(bf16[2,2,1024,128]{3,2,1,0:T(8,128)(2,1)S(1)} %collective-permute-done.4.refs_2_), channel_id=1, source_target_pairs={{0,16},{16,0},{1,17},{17,1},{2,18},{18,2},{3,19},{19,3},{4,20},{20... | collective-permute-start | bytes 3145736 | tf_op jit(solution)/shard_map/ppermute | solution.py:266
  109.5 0.0 collective-permute-done.17
  109.5 0.0 collective-permute-start.8
  109.5 4.6 %collective-permute-done.6.refs_4_ = bf16[2,1024,128]{2,1,0:T(8,128)(2,1)S(1)} collective-permute-done((bf16[2,1024,128]{2,1,0:T(8,128)(2,1)S(1)}, bf16[2,1024,128]{2,1,0:T(8,128)(2,1)S(1)}, u32[]{:S(2)}, u32[]{:S(2)}) %collective-permute-start.6) | collective-permute-done | bytes 524320 | tf_op jit(solution)/shard_map/ppermute | solution.py:265
  114.1 0.9 collective-permute-start.11
  115.0 2.3 %collective-permute-done.5.refs_3_ = bf16[2,1024,128]{2,1,0:T(8,128)(2,1)S(1)} collective-permute-done((bf16[2,1024,128]{2,1,0:T(8,128)(2,1)S(1)}, bf16[2,1024,128]{2,1,0:T(8,128)(2,1)S(1)}, u32[]{:S(2)}, u32[]{:S(2)}) %collective-permute-start.5) | collective-permute-done | bytes 524320 | tf_op jit(solution)/shard_map/ppermute | solution.py:265
  117.3 1.1 collective-permute-start.10
  118.4 0.0 collective-permute-done.7.refs_5_
  118.4 1.5 %collective-permute-done.10.refs_8_ = bf16[2,1024,128]{2,1,0:T(8,128)(2,1)S(1)} collective-permute-done((bf16[2,1024,128]{2,1,0:T(8,128)(2,1)S(1)}, bf16[2,1024,128]{2,1,0:T(8,128)(2,1)S(1)}, u32[]{:S(2)}, u32[]{:S(2)}) %collective-permute-start.10) | collective-permute-done | bytes 524320 | tf_op jit(solution)/shard_map/ppermute | solution.py:266
  120.0 0.0 collective-permute-done.9.refs_7_
  120.0 0.0 collective-permute-done.8.refs_6_
  120.0 17.9 %ladder.1 = f32[1024,1280]{1,0:T(8,128)} custom-call(s32[8,64]{1,0:T(8,128)S(1)} %pad_add_fusion.needs_ref, s32[6]{0:T(128)S(1)} %stack.28.info_ref, bf16[2,2,1024,128]{3,2,1,0:T(8,128)(2,1)S(1)} %pad_maximum_fusion.refs_0_, bf16[2,2,1024,128]{3,2,1,0:T(8,128)(2,1)S(1)} %collective-permute-done.3.refs_1_, ...), custom_call_target="tpu_custom_call" | custom-call | flops 10737418240 | bytes 25165824 | tf_op jit(solution)/shard_map/ladder/pallas_call | solution.py:228
  (13 shorter events, 0.1 us)
Async XLA Ops:
  3.2 32.4 %collective-permute-start.14 = (bf16[2,2,128,1280]{3,2,1,0:T(8,128)(2,1)}, bf16[2,2,128,1280]{3,2,1,0:T(8,128)(2,1)S(1)}, u32[]{:S(2)}, u32[]{:S(2)}) collective-permute-start(bf16[2,2,128,1280]{3,2,1,0:T(8,128)(2,1)} %get-tuple-element.11.refs_0_.refs_10_), channel_id=1, source_target_pairs={{0,12},{1,13},{2,14},{3,15},{4,0},{5,1},{6,2},{7,3},{8,4},{9,5},{1... | collective-permute-start | bytes 3932168 | tf_op jit(solution)/shard_map/ppermute | solution.py:258
  6.6 29.0 %collective-permute-start.13 = (bf16[2,2,128,1280]{3,2,1,0:T(8,128)(2,1)}, bf16[2,2,128,1280]{3,2,1,0:T(8,128)(2,1)}, u32[]{:S(2)}, u32[]{:S(2)}) collective-permute-start(bf16[2,2,128,1280]{3,2,1,0:T(8,128)(2,1)} %get-tuple-element.11.refs_0_.refs_10_), channel_id=1, source_target_pairs={{0,8},{1,9},{2,10},{3,11},{4,12},{5,13},{6,14},{7,15},{8,0},{9,1},... | collective-permute-start | bytes 3932168 | tf_op jit(solution)/shard_map/ppermute | solution.py:258
  7.1 32.2 %collective-permute-start.12 = (bf16[2,2,128,1280]{3,2,1,0:T(8,128)(2,1)}, bf16[2,2,128,1280]{3,2,1,0:T(8,128)(2,1)}, u32[]{:S(2)}, u32[]{:S(2)}) collective-permute-start(bf16[2,2,128,1280]{3,2,1,0:T(8,128)(2,1)} %get-tuple-element.11.refs_0_.refs_10_), channel_id=1, source_target_pairs={{0,4},{1,5},{2,6},{3,7},{4,8},{5,9},{6,10},{7,11},{8,12},{9,13},{1... | collective-permute-start | bytes 3932168 | tf_op jit(solution)/shard_map/ppermute | solution.py:258
  7.7 11.9 %all-to-all-start = ((s32[8,1,16]{2,1,0:T(1,128)}), s32[8,1,16]{2,1,0:T(1,128)S(1)}, u32[]{:S(2)}, u32[]{:S(2)}) async-start(s32[8,1,16]{2,1,0:T(1,128)} %bitcast.28), calls=%async_computation | async-start | bytes 8192 | tf_op jit(solution)/shard_map/all_to_all | solution.py:254
  19.6 9.6 %copy-start.4 = (s32[2]{0:T(128)S(1)}, s32[2]{0:T(128)}, u32[]{:S(2)}) copy-start(s32[2]{0:T(128)} %param.9) | copy-start | bytes 28
  19.7 19.6 %copy-start = (bf16[2,2,128,1280]{3,2,1,0:T(8,128)(2,1)S(1)}, bf16[2,2,128,1280]{3,2,1,0:T(8,128)(2,1)}, u32[]{:S(2)}) copy-start(bf16[2,2,128,1280]{3,2,1,0:T(8,128)(2,1)} %get-tuple-element.11.refs_0_.refs_10_) | copy-start | bytes 3932164
  19.7 53.8 %all-to-all-start.1 = ((bf16[16,1024,128]{2,1,0:T(8,128)(2,1)}), bf16[16,1024,128]{2,1,0:T(8,128)(2,1)}, u32[]{:S(2)}, u32[]{:S(2)}) async-start(bf16[16,1024,128]{2,1,0:T(8,128)(2,1)} %compress.1), calls=%async_computation.1 | async-start | bytes 8388608 | tf_op jit(solution)/shard_map/all_to_all | solution.py:261
  24.6 4.2 %collective-permute-start.2 = (s32[8,16]{1,0:T(8,128)S(1)}, s32[8,16]{1,0:T(8,128)S(1)}, u32[]{:S(2)}, u32[]{:S(2)}) collective-permute-start(s32[8,16]{1,0:T(8,128)S(1)} %bitcast.24), channel_id=1, source_target_pairs={{0,1},{1,2},{2,3},{3,0},{4,5},{5,6},{6,7},{7,4},{8,9},{9,10},{10,1... | collective-permute-start | bytes 1544 | tf_op jit(solution)/shard_map/ppermute | solution.py:255
  26.5 4.5 %collective-permute-start.1 = (s32[8,16]{1,0:T(8,128)S(1)}, s32[8,16]{1,0:T(8,128)S(1)}, u32[]{:S(2)}, u32[]{:S(2)}) collective-permute-start(s32[8,16]{1,0:T(8,128)S(1)} %bitcast.25), channel_id=1, source_target_pairs={{0,2},{1,3},{2,0},{3,1},{4,6},{5,7},{6,4},{7,5},{8,10},{9,11},{10,... | collective-permute-start | bytes 1544 | tf_op jit(solution)/shard_map/ppermute | solution.py:255
  28.8 3.0 %collective-permute-start = (s32[8,16]{1,0:T(8,128)S(1)}, s32[8,16]{1,0:T(8,128)S(1)}, u32[]{:S(2)}, u32[]{:S(2)}) collective-permute-start(s32[8,16]{1,0:T(8,128)S(1)} %bitcast.26), channel_id=1, source_target_pairs={{0,3},{1,0},{2,1},{3,2},{4,7},{5,4},{6,5},{7,6},{8,11},{9,8},{10,9... | collective-permute-start | bytes 1544 | tf_op jit(solution)/shard_map/ppermute | solution.py:255
  35.6 8.8 %copy-start.2 = (bf16[2,2,128,1280]{3,2,1,0:T(8,128)(2,1)}, bf16[2,2,128,1280]{3,2,1,0:T(8,128)(2,1)S(1)}, u32[]{:S(2)}) copy-start(bf16[2,2,128,1280]{3,2,1,0:T(8,128)(2,1)S(1)} %collective-permute-done.14.refs_3_.refs_13_) | copy-start | bytes 3932164
  44.4 58.4 %collective-permute-start.15 = (bf16[2,4,128,1280]{3,2,1,0:T(8,128)(2,1)}, bf16[2,4,128,1280]{3,2,1,0:T(8,128)(2,1)S(1)}, u32[]{:S(2)}, u32[]{:S(2)}) collective-permute-start(bf16[2,4,128,1280]{3,2,1,0:T(8,128)(2,1)} %get-tuple-element.12), channel_id=1, source_target_pairs={{0,1},{1,2},{2,3},{3,0},{4,5},{5,6},{6,7},{7,4},{8,9},{9,10},{10,1... | collective-permute-start | bytes 7864328 | tf_op jit(solution)/shard_map/ppermute | solution.py:268
  46.1 60.7 %collective-permute-start.16 = (bf16[2,4,128,1280]{3,2,1,0:T(8,128)(2,1)}, bf16[2,4,128,1280]{3,2,1,0:T(8,128)(2,1)}, u32[]{:S(2)}, u32[]{:S(2)}) collective-permute-start(bf16[2,4,128,1280]{3,2,1,0:T(8,128)(2,1)} %get-tuple-element.13), channel_id=1, source_target_pairs={{0,2},{1,3},{2,0},{3,1},{4,6},{5,7},{6,4},{7,5},{8,10},{9,11},{10,... | collective-permute-start | bytes 7864328 | tf_op jit(solution)/shard_map/ppermute | solution.py:268
  49.1 60.4 %collective-permute-start.17 = (bf16[2,4,128,1280]{3,2,1,0:T(8,128)(2,1)}, bf16[2,4,128,1280]{3,2,1,0:T(8,128)(2,1)}, u32[]{:S(2)}, u32[]{:S(2)}) collective-permute-start(bf16[2,4,128,1280]{3,2,1,0:T(8,128)(2,1)} %get-tuple-element.14), channel_id=1, source_target_pairs={{0,3},{1,0},{2,1},{3,2},{4,7},{5,4},{6,5},{7,6},{8,11},{9,8},{10,9... | collective-permute-start | bytes 7864328 | tf_op jit(solution)/shard_map/ppermute | solution.py:268
  74.8 45.2 %copy-start.1 = (bf16[2,2,128,1280]{3,2,1,0:T(8,128)(2,1)S(1)}, bf16[2,2,128,1280]{3,2,1,0:T(8,128)(2,1)}, u32[]{:S(2)}) copy-start(bf16[2,2,128,1280]{3,2,1,0:T(8,128)(2,1)} %get-tuple-element.11.refs_0_.refs_10_) | copy-start | bytes 3932164
  74.8 45.2 %copy-start.3 = (bf16[2,2,128,1280]{3,2,1,0:T(8,128)(2,1)S(1)}, bf16[2,2,128,1280]{3,2,1,0:T(8,128)(2,1)}, u32[]{:S(2)}) copy-start(bf16[2,2,128,1280]{3,2,1,0:T(8,128)(2,1)} %copy-done.2) | copy-start | bytes 3932164
  74.9 24.0 %collective-permute-start.4 = (bf16[2,2,1024,128]{3,2,1,0:T(8,128)(2,1)S(1)}, bf16[2,2,1024,128]{3,2,1,0:T(8,128)(2,1)S(1)}, u32[]{:S(2)}, u32[]{:S(2)}) collective-permute-start(bf16[2,2,1024,128]{3,2,1,0:T(8,128)(2,1)S(1)} %pad_maximum_fusion.refs_0_), channel_id=1, source_target_pairs={{0,96},{32,0},{64,32},{96,64},{1,97},{33,1},{65,33},{97,65},{2,98}... | collective-permute-start | bytes 3145736 | tf_op jit(solution)/shard_map/ppermute | solution.py:264
  75.9 24.8 %collective-permute-start.3 = (bf16[2,2,1024,128]{3,2,1,0:T(8,128)(2,1)S(1)}, bf16[2,2,1024,128]{3,2,1,0:T(8,128)(2,1)S(1)}, u32[]{:S(2)}, u32[]{:S(2)}) collective-permute-start(bf16[2,2,1024,128]{3,2,1,0:T(8,128)(2,1)S(1)} %pad_maximum_fusion.refs_0_), channel_id=1, source_target_pairs={{0,32},{32,64},{64,96},{96,0},{1,33},{33,65},{65,97},{97,1},{2,34}... | collective-permute-start | bytes 3145736 | tf_op jit(solution)/shard_map/ppermute | solution.py:264
  98.9 19.6 %collective-permute-start.7 = (bf16[2,2,1024,128]{3,2,1,0:T(8,128)(2,1)S(1)}, bf16[2,2,1024,128]{3,2,1,0:T(8,128)(2,1)S(1)}, u32[]{:S(2)}, u32[]{:S(2)}) collective-permute-start(bf16[2,2,1024,128]{3,2,1,0:T(8,128)(2,1)S(1)} %pad_maximum_fusion.refs_0_), channel_id=1, source_target_pairs={{0,16},{16,0},{1,17},{17,1},{2,18},{18,2},{3,19},{19,3},{4,20},{20... | collective-permute-start | bytes 3145736 | tf_op jit(solution)/shard_map/ppermute | solution.py:266
  100.7 13.4 %collective-permute-start.6 = (bf16[2,1024,128]{2,1,0:T(8,128)(2,1)S(1)}, bf16[2,1024,128]{2,1,0:T(8,128)(2,1)S(1)}, u32[]{:S(2)}, u32[]{:S(2)}) collective-permute-start(bf16[2,1024,128]{2,1,0:T(8,128)(2,1)S(1)} %slice_bitcast_fusion), channel_id=1, source_target_pairs={{0,96},{32,0},{64,32},{96,64},{1,97},{33,1},{65,33},{97,65},{2,98}... | collective-permute-start | bytes 1572872 | tf_op jit(solution)/shard_map/ppermute | solution.py:265
  102.8 14.5 %collective-permute-start.5 = (bf16[2,1024,128]{2,1,0:T(8,128)(2,1)S(1)}, bf16[2,1024,128]{2,1,0:T(8,128)(2,1)S(1)}, u32[]{:S(2)}, u32[]{:S(2)}) collective-permute-start(bf16[2,1024,128]{2,1,0:T(8,128)(2,1)S(1)} %slice_bitcast_fusion.1), channel_id=1, source_target_pairs={{0,32},{32,64},{64,96},{96,0},{1,33},{33,65},{65,97},{97,1},{2,34}... | collective-permute-start | bytes 1572872 | tf_op jit(solution)/shard_map/ppermute | solution.py:265
  106.8 13.1 %collective-permute-start.9 = (bf16[2,2,1024,128]{3,2,1,0:T(8,128)(2,1)S(1)}, bf16[2,2,1024,128]{3,2,1,0:T(8,128)(2,1)S(1)}, u32[]{:S(2)}, u32[]{:S(2)}) collective-permute-start(bf16[2,2,1024,128]{3,2,1,0:T(8,128)(2,1)S(1)} %collective-permute-done.4.refs_2_), channel_id=1, source_target_pairs={{0,16},{16,0},{1,17},{17,1},{2,18},{18,2},{3,19},{19,3},{4,20},{20... | collective-permute-start | bytes 3145736 | tf_op jit(solution)/shard_map/ppermute | solution.py:266
  109.5 10.4 %collective-permute-start.8 = (bf16[2,2,1024,128]{3,2,1,0:T(8,128)(2,1)S(1)}, bf16[2,2,1024,128]{3,2,1,0:T(8,128)(2,1)S(1)}, u32[]{:S(2)}, u32[]{:S(2)}) collective-permute-start(bf16[2,2,1024,128]{3,2,1,0:T(8,128)(2,1)S(1)} %collective-permute-done.3.refs_1_), channel_id=1, source_target_pairs={{0,16},{16,0},{1,17},{17,1},{2,18},{18,2},{3,19},{19,3},{4,20},{20... | collective-permute-start | bytes 3145736 | tf_op jit(solution)/shard_map/ppermute | solution.py:266
  114.1 4.3 %collective-permute-start.11 = (bf16[2,1024,128]{2,1,0:T(8,128)(2,1)S(1)}, bf16[2,1024,128]{2,1,0:T(8,128)(2,1)S(1)}, u32[]{:S(2)}, u32[]{:S(2)}) collective-permute-start(bf16[2,1024,128]{2,1,0:T(8,128)(2,1)S(1)} %collective-permute-done.6.refs_4_), channel_id=1, source_target_pairs={{0,16},{16,0},{1,17},{17,1},{2,18},{18,2},{3,19},{19,3},{4,20},{20... | collective-permute-start | bytes 1572872 | tf_op jit(solution)/shard_map/ppermute | solution.py:266
  117.3 2.6 %collective-permute-start.10 = (bf16[2,1024,128]{2,1,0:T(8,128)(2,1)S(1)}, bf16[2,1024,128]{2,1,0:T(8,128)(2,1)S(1)}, u32[]{:S(2)}, u32[]{:S(2)}) collective-permute-start(bf16[2,1024,128]{2,1,0:T(8,128)(2,1)S(1)} %collective-permute-done.5.refs_3_), channel_id=1, source_target_pairs={{0,16},{16,0},{1,17},{17,1},{2,18},{18,2},{3,19},{19,3},{4,20},{20... | collective-permute-start | bytes 1572872 | tf_op jit(solution)/shard_map/ppermute | solution.py:266
